TPU v7x, 32 devices: a whole 2x2x4 slice. The times are simulated.
32 devices in a mesh: groups: 2 (over y), expert: 4 (over z), mp: 4 (over x, core), section: 1.
Axes of the slice: x: 2, y: 2, z: 4, core: 2. Of those that a mesh axis runs over, the one named last changes fastest.
Arguments:
- tokens: bfloat16 [4096, 2048], P(('groups', 'expert', 'mp'), 'section'), parts along dimension 0, may hold values from -6 to 6
- expert_ids: int32 [4096, 8], P(('groups', 'expert', 'mp')), parts along dimension 0, may hold values from 0 to 15, all different within a row; in each aligned block of 128 rows (0 to 127, 128 to 255, ...) at most 80 rows name the same one
- route_weights: float32 [4096, 8], P(('groups', 'expert', 'mp')), parts along dimension 0, may hold values from 0.1 to 0.5
- gate_weight: bfloat16 [16, 384, 2048], P(('expert', 'mp'), 'section'), may hold values from -0.125 to 0.125
- up_weight: bfloat16 [16, 384, 2048], P(('expert', 'mp'), 'section'), may hold values from -0.125 to 0.125
- down_weight: bfloat16 [16, 384, 2048], P(('expert', 'mp'), None, 'section'), may hold values from -6 to 6
- mask_code: int32 [16, 96, 2048], P(('expert', 'mp'), None, 'section'), may hold values from 0 to 5
Outputs:
- mixed: bfloat16 [4096, 2048], P(('groups', 'expert', 'mp'), 'section'), parts along dimension 0
- pruned_down: bfloat16 [32, 384, 2048], P(('groups', 'expert', 'mp'), None, 'section'), parts along dimension 0
There are 2 independent parts, one for each index of `groups`. A program takes and returns all parts, laid end to end along the dimension named above; an argument that names none is the same for every part. Nothing has to cross between parts.
Inputs may be any that keep to these rules, and one draw needn't show every extreme that they name: `expert_ids`: each row names 8 different experts, and every expert is named by some row. In each aligned block of 128 rows no expert is named by more than 80 rows, a bound that some block reaches.
All inputs are finite; a program needn't handle non-finite values. Where the computation divides by a largest or mean magnitude, that divisor is 1e-20 or more.
Results may differ from a plain program's by a relative error of at most 0.011.
Values may be sent and summed in bfloat16 or wider, within the bound.
No kernel may reach another device: no remote copies, remote signals or barrier semaphores. Data moves between devices by JAX's collectives and lax.ppermute only.
A program may use at most 64 MiB of HBM per device.

v0:
```python
import jax
import jax.numpy as jnp
from jax import lax
from jax.sharding import PartitionSpec as P

FF = 384
NS = 4


DAMPING = 0.01
EPSILON = 1e-06


def decode(mask_code):
    first_row = (mask_code <= 2).astype(jnp.float32)
    second_row = ((mask_code == 0) | (mask_code == 3) | (mask_code == 4)).astype(jnp.float32)
    third_row = ((mask_code == 1) | (mask_code == 3) | (mask_code == 5)).astype(jnp.float32)
    fourth_row = ((mask_code == 2) | (mask_code == 4) | (mask_code == 5)).astype(jnp.float32)
    kept_mask = jnp.stack([first_row, second_row, third_row, fourth_row], axis=2)
    return kept_mask.reshape(mask_code.shape[0], mask_code.shape[1] * 4, mask_code.shape[2])


def precise_matmul(left, right):
    return jnp.einsum(
        "jab,jbc->jac",
        left,
        right,
        precision=lax.Precision.HIGHEST,
        preferred_element_type=jnp.float32,
    )


def local(tokens, expert_ids, route_weights, gate_weight, up_weight, down_weight, mask_code):
    group_count = lax.axis_size(("expert", "mp"))
    experts_here, half_rows, model_width = gate_weight.shape
    tok_rows, top_count = expert_ids.shape
    experts_all = experts_here * group_count
    capacity = min(tok_rows, 5 * tok_rows * top_count // (4 * experts_all))
    slot_total = group_count * capacity
    flat_ids = expert_ids.reshape(-1)
    onehot = (flat_ids[:, None] == jnp.arange(experts_all, dtype=jnp.int32)[None, :]).astype(
        jnp.int32
    )
    slot_rank = jnp.sum((jnp.cumsum(onehot, axis=0) - onehot) * onehot, axis=1)
    local_expert = flat_ids % experts_here
    position = flat_ids // experts_here * capacity + slot_rank
    token_of = jnp.arange(tok_rows * top_count, dtype=jnp.int32) // top_count
    slot_token = (
        jnp.full((experts_here, slot_total), tok_rows, jnp.int32)
        .at[local_expert, position]
        .set(token_of)
    )
    full_rows = lax.all_gather(tokens, "section", axis=1, tiled=True)
    padded_rows = jnp.concatenate(
        [full_rows, jnp.zeros((1, full_rows.shape[1]), full_rows.dtype)], axis=0
    )
    send_rows = padded_rows[slot_token]
    slot_rows = lax.all_to_all(send_rows, ("expert", "mp"), split_axis=1, concat_axis=1, tiled=True)
    gate_pre = jnp.einsum(
        "jfd,jsd->jfs", gate_weight, slot_rows, preferred_element_type=jnp.float32
    )
    up_pre = jnp.einsum("jfd,jsd->jfs", up_weight, slot_rows, preferred_element_type=jnp.float32)
    hidden_half = (jax.nn.silu(gate_pre) * up_pre).astype(jnp.bfloat16)
    hidden_all = lax.all_gather(hidden_half, "section", axis=1, tiled=True)
    hidden_width = hidden_all.shape[1]
    gram_matrix = jnp.einsum(
        "jfs,jgs->jfg", hidden_all, hidden_all, preferred_element_type=jnp.float32
    )
    mean_diag = jnp.mean(jnp.diagonal(gram_matrix, axis1=1, axis2=2), axis=1)
    identity = jnp.eye(hidden_width, dtype=jnp.float32)
    hessian = gram_matrix + (DAMPING * mean_diag + EPSILON)[:, None, None] * identity
    step_size = 1.0 / jnp.max(jnp.sum(jnp.abs(hessian), axis=2), axis=1)
    iterate = (
        2.0 * step_size[:, None, None] * identity - (step_size * step_size)[:, None, None] * hessian
    )
    for iteration in range(NS - 1):
        iterate = 2.0 * iterate - precise_matmul(precise_matmul(iterate, hessian), iterate)
    kept_mask = decode(mask_code)
    weight_wide = down_weight.astype(jnp.float32)
    inverse_diag = jnp.diagonal(iterate, axis1=1, axis2=2)
    scaled_error = weight_wide * (1.0 - kept_mask) / inverse_diag[:, :, None]
    correction = precise_matmul(iterate, scaled_error)
    pruned = (kept_mask * (weight_wide - correction)).astype(jnp.bfloat16)
    expert_out = (
        jnp.einsum("jfs,jfd->jsd", hidden_all, pruned, preferred_element_type=jnp.float32)
        * FF ** (-0.5)
    ).astype(jnp.bfloat16)
    returned = lax.all_to_all(expert_out, ("expert", "mp"), split_axis=1, concat_axis=1, tiled=True)
    picked = returned[local_expert, position].reshape(tok_rows, top_count, -1)
    combined = jnp.einsum("tkd,tk->td", picked.astype(jnp.float32), route_weights)
    return (combined.astype(jnp.bfloat16), pruned)


def solution(mesh):
    placed = (
        P(("groups", "expert", "mp"), "section"),
        P(("groups", "expert", "mp"), None),
        P(("groups", "expert", "mp"), None),
        P(("expert", "mp"), "section", None),
        P(("expert", "mp"), "section", None),
        P(("expert", "mp"), None, "section"),
        P(("expert", "mp"), None, "section"),
    )
    return jax.shard_map(
        local,
        mesh=mesh,
        in_specs=placed,
        out_specs=(
            P(("groups", "expert", "mp"), "section"),
            P(("groups", "expert", "mp"), None, "section"),
        ),
        check_vma=False,
    )
```

profile of v0, /device:TPU:11, one launch (start us, length us, event | category | flops | bytes accessed | tf_op | source)
XLA Modules:
  0.0 507.1 jit_solution(3457853440540594976)
XLA Ops:
  0.6 0.0 copy-start
  0.6 0.9 copy.37
  1.6 0.1 eq.63
  1.6 0.1 eq.59
  1.7 0.7 broadcast_multiply_fusion
  2.4 4.5 reduce-window.6
  7.0 0.1 slice.16
  7.0 0.1 copy.39
  7.2 0.1 copy.40
  7.3 0.1 broadcast_add_fusion
  7.4 0.1 copy.36
  7.5 0.1 mul.95
  7.6 0.7 fusion.49
  8.4 0.8 and_reduce_fusion
  9.1 4.3 scatter_custom_fusion
  13.5 1.1 concatenate.12
  14.6 6.2 %gather_fusion = bf16[1280,2048]{1,0:T(8,128)(2,1)} fusion(bf16[129,2048]{1,0:T(8,128)(2,1)S(1)} %concatenate.12, s32[2048]{0:T(1024)S(1)} %pad_clamp_fusion), kind=kCustom, calls=%fused_computation | custom fusion | bytes 10490880 | tf_op jit(solution)/shard_map/gather | solution.py:57
  20.8 10.3 %copy.69 = bf16[1,1280,2048]{2,0,1:T(2,128)(2,1)} copy(bf16[1,1280,2048]{2,1,0:T(8,128)(2,1)} %bitcast.99) | data formatting | bytes 10485760 | tf_op jit(solution)/shard_map/gather | solution.py:57
  31.1 0.5 broadcast.268
  31.6 33.4 %reduce.15 = bf16[1280,2048]{1,0:T(8,128)(2,1)} reduce(bf16[1280,1,2048]{2,1,0:T(2,128)(2,1)} %bitcast.96, bf16[]{:T(256)} %broadcast.268), dimensions={1}, to_apply=%bitcast.94.reduce_sub_computation | reduce | bytes 10485762
  65.0 12.2 %reshape.248 = bf16[16,2,81920]{2,1,0:T(2,128)(2,1)} reshape(bf16[1280,2048]{1,0:T(8,128)(2,1)} %reduce.15) | data formatting | bytes 10485760
  77.2 0.0 copy-start.3
  77.2 7.0 %all-to-all-start = ((bf16[16,2,81920]{2,1,0:T(2,128)(2,1)}), bf16[16,2,81920]{2,1,0:T(2,128)(2,1)}, u32[]{:S(2)}, u32[]{:S(2)}) async-start(bf16[16,2,81920]{2,1,0:T(2,128)(2,1)} %reshape.248), calls=%async_computation | async-start | bytes 10485760 | tf_op jit(solution)/shard_map/all_to_all | solution.py:58
  84.2 0.0 copy-done.3
  84.2 0.7 compare_bitcast_fusion
  84.9 0.1 pad_add_fusion
  85.0 1.0 copy.42
  85.9 0.9 reshape.185
  86.9 112.1 %all-to-all-done = bf16[16,2,81920]{2,1,0:T(2,128)(2,1)} async-done(((bf16[16,2,81920]{2,1,0:T(2,128)(2,1)}), bf16[16,2,81920]{2,1,0:T(2,128)(2,1)}, u32[]{:S(2)}, u32[]{:S(2)}) %all-to-all-start) | async-done | bytes 5242912 | tf_op jit(solution)/shard_map/all_to_all | solution.py:58
  199.0 13.3 %reshape.249 = bf16[1280,1,2048]{2,1,0:T(2,128)(2,1)} reshape(bf16[16,2,81920]{2,1,0:T(2,128)(2,1)} %all-to-all-done) | data formatting | bytes 10485760
  212.3 0.0 copy-done
  212.3 9.2 %fusion.15 = f32[384,1280]{0,1:T(8,128)S(1)} fusion(bf16[1,1280,2048]{2,0,1:T(2,128)(2,1)} %bitcast.100, bf16[1,384,2048]{2,1,0:T(8,128)(2,1)S(1)} %copy-done), kind=kOutput, calls=%fused_computation.23 | convolution fusion | flops 2013265920 | bytes 8781824 | tf_op jit(solution)/shard_map/jfd,jsd->jfs/dot_general | solution.py:59
  221.5 0.0 copy-done.2
  221.5 0.0 copy-done.5
  221.6 4.1 fusion.26
  225.7 0.7 fusion.61
  226.4 3.7 gather_fusion.1
  230.1 0.6 reduce.7
  231.4 0.1 abs_reduce_fusion
  231.5 0.6 reduce_max.9
  232.8 2.0 fusion.36
  234.8 1.3 convolution_subtract_fusion.2
  236.1 2.1 fusion.44
  238.2 1.3 convolution_subtract_fusion.1
  239.6 2.1 fusion.43
  241.6 1.3 convolution_subtract_fusion
  242.9 3.5 gather_fusion.2
  246.4 8.0 %fusion.12 = bf16[1,384,2048]{2,1,0:T(8,128)(2,1)S(1)} fusion(pred[1,384,2048]{2,1,0:T(32,128)(4,1)S(1)} %reshape.185, bf16[1,384,2048]{2,1,0:T(8,128)(2,1)} %param.12, f32[384,384]{0,1:T(8,128)S(1)} %convolution_subtract_fusion, f32[384]{0:T(512)S(1)} %gather_fusion.2), kind=kOutput, calls=%fused_computation.19 | convolution fusion | flops 3630956544 | bytes 4523520 | tf_op jit(solution)/shard_map/jab,jbc->jac/dot_general | solution.py:24
  254.4 0.0 copy-start.6
  254.4 1.1 copy-done.6
  255.6 3.1 fusion
  258.7 30.5 %copy.68 = bf16[1,1280,2048]{2,0,1:T(2,128)(2,1)} copy(bf16[1,1280,2048]{2,1,0:T(8,128)(2,1)S(1)} %fusion) | data formatting | bytes 10485760 | tf_op jit(solution)/shard_map/convert_element_type | solution.py:87
  289.2 33.4 %reduce.16 = bf16[1280,2048]{1,0:T(8,128)(2,1)} reduce(bf16[1280,1,2048]{2,1,0:T(2,128)(2,1)} %bitcast.97, bf16[]{:T(256)} %broadcast.268), dimensions={1}, to_apply=%bitcast.93.reduce_sub_computation | reduce | bytes 10485762
  322.6 12.2 %reshape.250 = bf16[16,2,81920]{2,1,0:T(2,128)(2,1)} reshape(bf16[1280,2048]{1,0:T(8,128)(2,1)} %reduce.16) | data formatting | bytes 10485760
  334.8 5.3 %all-to-all-start.1 = ((bf16[16,2,81920]{2,1,0:T(2,128)(2,1)}), bf16[16,2,81920]{2,1,0:T(2,128)(2,1)}, u32[]{:S(2)}, u32[]{:S(2)}) async-start(bf16[16,2,81920]{2,1,0:T(2,128)(2,1)} %reshape.250), calls=%async_computation.1 | async-start | bytes 10485760 | tf_op jit(solution)/shard_map/all_to_all | solution.py:88
  340.1 0.0 copy-done.4
  340.1 0.1 copy.51
  340.3 114.6 %all-to-all-done.1 = bf16[16,2,81920]{2,1,0:T(2,128)(2,1)} async-done(((bf16[16,2,81920]{2,1,0:T(2,128)(2,1)}), bf16[16,2,81920]{2,1,0:T(2,128)(2,1)}, u32[]{:S(2)}, u32[]{:S(2)}) %all-to-all-start.1) | async-done | bytes 5242912 | tf_op jit(solution)/shard_map/all_to_all | solution.py:88
  454.9 13.3 %reshape.251 = bf16[1280,1,2048]{2,1,0:T(2,128)(2,1)} reshape(bf16[16,2,81920]{2,1,0:T(2,128)(2,1)} %all-to-all-done.1) | data formatting | bytes 10485760
  468.2 9.7 %copy.47 = bf16[1,1280,2048]{2,1,0:T(8,128)(2,1)} copy(bf16[1,1280,2048]{2,0,1:T(2,128)(2,1)} %bitcast.98) | data formatting | bytes 10485760 | tf_op jit(solution)/shard_map/all_to_all | solution.py:88
  477.9 24.5 %gather_fusion.3 = bf16[1024,2048]{1,0:T(8,128)(2,1)} fusion(bf16[1,1280,2048]{2,1,0:T(8,128)(2,1)} %copy.47, s32[1024]{0:T(1024)S(1)} %bitcast.95), kind=kCustom, calls=%fused_computation.3 | custom fusion | bytes 8396800 | tf_op jit(solution)/shard_map/gather | solution.py:89
  502.4 3.4 fusion.5
  505.9 1.1 copy.67
  507.0 0.0 copy-done.1
  (13 shorter events, 0.2 us)
Async XLA Ops:
  0.6 211.7 %copy-start = (bf16[1,384,2048]{2,1,0:T(8,128)(2,1)S(1)}, bf16[1,384,2048]{2,1,0:T(8,128)(2,1)}, u32[]{:S(2)}) copy-start(bf16[1,384,2048]{2,1,0:T(8,128)(2,1)} %param.10) | copy-start | bytes 4718596
  77.2 7.0 %copy-start.3 = (s32[1,96,2048]{2,1,0:T(8,128)S(1)}, s32[1,96,2048]{2,1,0:T(8,128)}, u32[]{:S(2)}) copy-start(s32[1,96,2048]{2,1,0:T(8,128)} %param.13) | copy-start | bytes 2359300
  77.2 121.8 %all-to-all-start = ((bf16[16,2,81920]{2,1,0:T(2,128)(2,1)}), bf16[16,2,81920]{2,1,0:T(2,128)(2,1)}, u32[]{:S(2)}, u32[]{:S(2)}) async-start(bf16[16,2,81920]{2,1,0:T(2,128)(2,1)} %reshape.248), calls=%async_computation | async-start | bytes 10485760 | tf_op jit(solution)/shard_map/all_to_all | solution.py:58
  212.3 9.3 %copy-start.2 = (bf16[1280,1,2048]{2,1,0:T(2,128)(2,1)S(1)}, bf16[1280,1,2048]{2,1,0:T(2,128)(2,1)}, u32[]{:S(2)}) copy-start(bf16[1280,1,2048]{2,1,0:T(2,128)(2,1)} %reshape.249) | copy-start | bytes 15728644
  212.3 9.3 %copy-start.5 = (bf16[1,384,2048]{2,1,0:T(8,128)(2,1)S(1)}, bf16[1,384,2048]{2,1,0:T(8,128)(2,1)}, u32[]{:S(2)}) copy-start(bf16[1,384,2048]{2,1,0:T(8,128)(2,1)} %param.11) | copy-start | bytes 4718596
  254.4 1.1 copy-start.6
  334.8 5.3 %copy-start.4 = (f32[128,8]{0,1:T(8,128)S(1)}, f32[128,8]{0,1:T(8,128)}, u32[]{:S(2)}) copy-start(f32[128,8]{0,1:T(8,128)} %param.9) | copy-start | bytes 12292
  334.8 120.1 %all-to-all-start.1 = ((bf16[16,2,81920]{2,1,0:T(2,128)(2,1)}), bf16[16,2,81920]{2,1,0:T(2,128)(2,1)}, u32[]{:S(2)}, u32[]{:S(2)}) async-start(bf16[16,2,81920]{2,1,0:T(2,128)(2,1)} %reshape.250), calls=%async_computation.1 | async-start | bytes 10485760 | tf_op jit(solution)/shard_map/all_to_all | solution.py:88
  477.9 29.1 %copy-start.1 = (bf16[1,384,2048]{2,1,0:T(8,128)(2,1)S(1)}, bf16[1,384,2048]{2,1,0:T(8,128)(2,1)}, u32[]{:S(2)}) copy-start(bf16[1,384,2048]{2,1,0:T(8,128)(2,1)} %param.10) | copy-start | bytes 4718596
where the time goes:
time: 514 us; the launch traced here: 507 us
  waiting for transfers between devices  227 us (44%)
  local copies, waits for them, and re-layouts  151 us (29%)
  other arithmetic  75.9 us (15%)
  matrix products  38.7 us (8%)
  starting transfers between devices  12.3 us (2%)
    all_to_all x1, waiting for transfers between devices, local(): lax.all_to_all(expert_out, ('expert', 'mp'), split_axis=1, concat_axis=1,...  115 us
    all_to_all x1, waiting for transfers between devices, local(): lax.all_to_all(send_rows, ('expert', 'mp'), split_axis=1, concat_axis=1,...  112 us
    unnamed x4, other arithmetic  68.3 us
    unnamed x22, local copies, waits for them, and re-layouts  58 us
    convert_element_type x1, local copies, waits for them, and re-layouts, local(): expert_out = (jnp.einsum('jfs,jfd->jsd', hidden_all, pruned, preferred_el...  30.5 us
    gather x1, local copies, waits for them, and re-layouts, local(): picked = returned[local_expert, position].reshape(tok_rows, top_count, -1)  24.5 us
    dot_general x7, matrix products, precise_matmul(): jnp.einsum('jab,jbc->jac', left, right, precision=lax.Precision.HIGHEST,...  18.1 us
    gather x2, local copies, waits for them, and re-layouts, local(): send_rows = padded_rows[slot_token]  16.5 us
  transfers between devices with their start and end apart: 2, of which 2 were waited for; matrix products, arithmetic and copies ran while one was open for 1% of the time, Pallas kernels for 0%

commit v1 on v0

--- a/solution.py
+++ b/solution.py
@@ -1,6 +1,10 @@
+import functools
 import jax
 import jax.numpy as jnp
+import numpy as np
 from jax import lax
+from jax.experimental import pallas as pl
+from jax.experimental.pallas import tpu as pltpu
 from jax.sharding import PartitionSpec as P
 
 FF = 384
@@ -30,7 +34,7 @@
     )
 
 
-def local(tokens, expert_ids, route_weights, gate_weight, up_weight, down_weight, mask_code):
+def routed(tokens, expert_ids, route_weights, gate_weight, up_weight, down_weight, mask_code):
     group_count = lax.axis_size(("expert", "mp"))
     experts_here, half_rows, model_width = gate_weight.shape
     tok_rows, top_count = expert_ids.shape
@@ -91,6 +95,407 @@
     return (combined.astype(jnp.bfloat16), pruned)
 
 
+AXES = ("expert", "mp")
+CHUNK = 128
+BF = jnp.bfloat16
+F32 = jnp.float32
+
+
+def params(*semantics):
+    return pltpu.CompilerParams(
+        dimension_semantics=semantics or None, vmem_limit_bytes=40 * 1024 * 1024
+    )
+
+
+def whole(shape):
+    return pl.BlockSpec(shape, lambda *_: (0,) * len(shape))
+
+
+def dot(left, right, on=((1,), (0,))):
+    return lax.dot_general(left, right, (on, ((), ())), preferred_element_type=F32)
+
+
+def weight_table(expert_ids, route_weights, experts_all):
+    hit = expert_ids[None] == jnp.arange(experts_all, dtype=jnp.int32)[:, None, None]
+    return jnp.max(jnp.where(hit, route_weights[None], -1.0), axis=2)
+
+
+def pick_kernel(blocks, place_ref, table_ref, out_ref):
+    rows = []
+    for k in range(blocks):
+        for which in range(2):
+            rows.append(table_ref[pl.ds(place_ref[2 * k + which], 1), :])
+    out_ref[...] = jnp.concatenate(rows, axis=0).T
+
+
+def pick(place, table, blocks):
+    tok_rows = table.shape[1]
+    return pl.pallas_call(
+        functools.partial(pick_kernel, blocks),
+        out_shape=jax.ShapeDtypeStruct((tok_rows, 2 * blocks), F32),
+        grid_spec=pltpu.PrefetchScalarGridSpec(
+            num_scalar_prefetch=1,
+            grid=(1,),
+            in_specs=[whole(table.shape)],
+            out_specs=whole((tok_rows, 2 * blocks)),
+        ),
+        compiler_params=params("arbitrary"),
+        name="pick",
+    )(place, table)
+
+
+def mask_kernel(code_ref, down_ref, kept_ref, error_ref):
+    rows, groups = down_ref.shape[0], code_ref.shape[0]
+    row = lax.broadcasted_iota(jnp.int32, (rows, groups), 0)
+    column = lax.broadcasted_iota(jnp.int32, (rows, groups), 1)
+    spread = (row // 4 == column).astype(BF)
+    code = dot(spread, code_ref[...].astype(F32).astype(BF))
+    place = lax.broadcasted_iota(jnp.int32, code.shape, 0) % 4
+    first = code <= 2.5
+    second = (code < 0.5) | ((code > 2.5) & (code < 4.5))
+    third = ((code > 0.5) & (code < 1.5)) | ((code > 2.5) & (code < 3.5)) | (code > 4.5)
+    fourth = ((code > 1.5) & (code < 2.5)) | (code > 3.5)
+    kept = jnp.where(
+        place == 0,
+        first.astype(F32),
+        jnp.where(
+            place == 1,
+            second.astype(F32),
+            jnp.where(place == 2, third.astype(F32), fourth.astype(F32)),
+        ),
+    )
+    kept_ref[...] = kept.astype(BF)
+    error_ref[...] = (down_ref[...].astype(F32) * (1.0 - kept)).astype(BF)
+
+
+def masks(code, down):
+    groups, width = code.shape
+    rows = down.shape[0]
+    cut = 512
+    spec = pl.BlockSpec((rows, cut), lambda i: (0, i))
+    return pl.pallas_call(
+        mask_kernel,
+        out_shape=[jax.ShapeDtypeStruct((rows, width), BF)] * 2,
+        grid=(width // cut,),
+        in_specs=[pl.BlockSpec((groups, cut), lambda i: (0, i)), spec],
+        out_specs=[spec, spec],
+        compiler_params=params("arbitrary"),
+        name="masks",
+    )(code, down)
+
+
+def hidden_kernel(pieces, columns, has_gram, *refs):
+    x_refs, refs = refs[:pieces], refs[pieces:]
+    gate_ref, up_ref, weight_ref, refs = refs[0], refs[1], refs[2], refs[3:]
+    gram_in, refs = (refs[0], refs[1:]) if has_gram else (None, refs)
+    out_ref, gram_ref, hidden_ref = refs
+    step = pl.program_id(0)
+    rows = jnp.concatenate([x[...] for x in x_refs], axis=0)
+    both = jnp.concatenate([gate_ref[...], up_ref[...]], axis=0)
+    pre = dot(rows, both, ((1,), (1,)))
+    gate, up = pre[:, :CHUNK], pre[:, CHUNK:]
+    weight = jnp.concatenate([weight_ref[:, c : c + 1] for c in columns], axis=0)
+    value = gate / (1.0 + jnp.exp(-gate)) * up
+    value = jnp.where(weight >= 0.0, value, 0.0).astype(BF)
+    hidden_ref[:, pl.ds(pl.multiple_of(step * CHUNK, CHUNK), CHUNK)] = value
+    out_ref[...] = (value.astype(F32) * (weight * FF ** (-0.5))).astype(BF)
+
+    @pl.when(step == pl.num_programs(0) - 1)
+    def _():
+        hidden = hidden_ref[...]
+        gram = dot(hidden, hidden, ((0,), (0,)))
+        gram_ref[...] = gram if gram_in is None else gram_in[...] + gram
+
+
+def hidden_part(pieces, gate, up, weights, columns, gram):
+    rows = sum(p.shape[0] for p in pieces)
+    ff, width = gate.shape
+    steps = ff // CHUNK
+    slab = pl.BlockSpec((CHUNK, width), lambda i: (i, 0))
+    given = list(pieces) + [gate, up, weights] + ([] if gram is None else [gram])
+    specs = [whole(p.shape) for p in pieces] + [slab, slab, whole(weights.shape)]
+    specs += [] if gram is None else [whole(gram.shape)]
+    return pl.pallas_call(
+        functools.partial(hidden_kernel, len(pieces), columns, gram is not None),
+        out_shape=[
+            jax.ShapeDtypeStruct((rows, ff), BF),
+            jax.ShapeDtypeStruct((ff, ff), F32),
+        ],
+        grid=(steps,),
+        in_specs=specs,
+        out_specs=[pl.BlockSpec((rows, CHUNK), lambda i: (0, i)), whole((ff, ff))],
+        scratch_shapes=[pltpu.VMEM((rows, ff), BF)],
+        compiler_params=params("arbitrary"),
+        cost_estimate=pl.CostEstimate(
+            flops=4 * rows * ff * width,
+            bytes_accessed=2 * (rows + 2 * ff) * width,
+            transcendentals=rows * ff,
+        ),
+        name="hidden",
+    )(*given)
+
+
+def halves(value):
+    high = value.astype(BF)
+    return high, (value - high.astype(F32)).astype(BF)
+
+
+def product(left, right):
+    (a, b), (c, d) = left, right
+    return dot(a, c) + (dot(a, d) + dot(b, c))
+
+
+def prune_kernel(own_ref, other_ref, error_ref, down_ref, kept_ref, out_ref, high_ref, low_ref):
+    gram = own_ref[...] + other_ref[...]
+    size = gram.shape[0]
+    row = lax.broadcasted_iota(jnp.int32, (size, size), 0)
+    column = lax.broadcasted_iota(jnp.int32, (size, size), 1)
+    eye = row == column
+    mean_diag = jnp.sum(jnp.where(eye, gram, 0.0)) * (1.0 / size)
+    hessian = gram + jnp.where(eye, DAMPING * mean_diag + EPSILON, 0.0)
+    step_size = 1.0 / jnp.max(jnp.sum(jnp.abs(hessian), axis=0, keepdims=True))
+    scaled = step_size * hessian
+    iterate = jnp.where(eye, 2.0, 0.0) - scaled
+    parts = halves(scaled)
+    scaled = 2.0 * scaled - product(parts, parts)
+    for iteration in range(NS - 1):
+        parts = halves(scaled)
+        if iteration < NS - 2:
+            stack = jnp.concatenate([iterate, scaled], axis=0)
+            stack = 2.0 * stack - product(halves(stack), parts)
+            iterate, scaled = stack[:size], stack[size:]
+        else:
+            iterate = 2.0 * iterate - product(halves(iterate), parts)
+    diag = jnp.sum(jnp.where(eye, iterate, 0.0), axis=0, keepdims=True)
+    high, low = halves(iterate / diag)
+    high_ref[...] = high
+    low_ref[...] = low
+    correct(high, low, error_ref, down_ref, kept_ref, out_ref)
+
+
+def correct(high, low, error_ref, down_ref, kept_ref, out_ref):
+    error = error_ref[...]
+    correction = dot(high, error) + dot(low, error)
+    value = kept_ref[...].astype(F32) * (down_ref[...].astype(F32) - correction)
+    out_ref[...] = value.astype(BF)
+
+
+def correct_kernel(high_ref, low_ref, error_ref, down_ref, kept_ref, out_ref):
+    correct(high_ref[...], low_ref[...], error_ref, down_ref, kept_ref, out_ref)
+
+
+def prune_first(own, other, error, down, kept, cut):
+    size = own.shape[0]
+    half = pl.BlockSpec((size, cut), lambda i: (0, 0))
+    square = whole((size, size))
+    return pl.pallas_call(
+        prune_kernel,
+        out_shape=[jax.ShapeDtypeStruct((size, cut), BF)]
+        + [jax.ShapeDtypeStruct((size, size), BF)] * 2,
+        grid=(1,),
+        in_specs=[square, square, half, half, half],
+        out_specs=[half, square, square],
+        compiler_params=params("arbitrary"),
+        name="prune",
+    )(own, other, error, down, kept)
+
+
+def prune_next(high, low, error, down, kept, cut, at):
+    size = high.shape[0]
+    half = pl.BlockSpec((size, cut), lambda i: (0, at))
+    square = whole((size, size))
+    return pl.pallas_call(
+        correct_kernel,
+        out_shape=jax.ShapeDtypeStruct((size, cut), BF),
+        grid=(1,),
+        in_specs=[square, square, half, half, half],
+        out_specs=whole((size, cut)),
+        compiler_params=params("arbitrary"),
+        name="prune_next",
+    )(high, low, error, down, kept)
+
+
+def outputs_kernel(block, arrived, own_hidden, other_hidden, own_ref, other_ref, *refs):
+    total = dot(own_hidden[...], own_ref[...]) + dot(other_hidden[...], other_ref[...])
+    first, second = total[:block], total[block:]
+    if arrived:
+        size = refs[0].shape[0]
+        from_right, from_left = refs[0][...].astype(F32), refs[1][...].astype(F32)
+        if size < block:
+            empty = jnp.zeros((block - size, total.shape[1]), F32)
+            from_left = jnp.concatenate([from_left, empty], axis=0)
+            from_right = jnp.concatenate([empty, from_right], axis=0)
+        first, second = first + from_right, second + from_left
+    refs[-2][...] = first.astype(BF)
+    refs[-1][...] = second.astype(BF)
+
+
+def outputs(own_hidden, other_hidden, own, other, arrived):
+    rows = own_hidden.shape[0]
+    cut = own.shape[1]
+    given = (own_hidden, other_hidden, own, other) + arrived
+    return pl.pallas_call(
+        functools.partial(outputs_kernel, rows // 2, len(arrived)),
+        out_shape=[jax.ShapeDtypeStruct((rows // 2, cut), BF)] * 2,
+        grid=(1,),
+        in_specs=[whole(g.shape) for g in given],
+        out_specs=[whole((rows // 2, cut))] * 2,
+        compiler_params=params("arbitrary"),
+        cost_estimate=pl.CostEstimate(
+            flops=4 * rows * own.shape[0] * cut,
+            bytes_accessed=sum(g.size * 2 for g in given) + rows * cut * 2,
+            transcendentals=0,
+        ),
+        name="outputs",
+    )(*given)
+
+
+def self_kernel(own_hidden, other_hidden, own_ref, other_ref, out_ref):
+    out_ref[...] = dot(own_hidden[...], own_ref[...]) + dot(other_hidden[...], other_ref[...])
+
+
+def self_outputs(own_hidden, other_hidden, own, other):
+    rows, cut = own_hidden.shape[0], own.shape[1]
+    given = (own_hidden, other_hidden, own, other)
+    return pl.pallas_call(
+        self_kernel,
+        out_shape=jax.ShapeDtypeStruct((rows, cut), F32),
+        grid=(1,),
+        in_specs=[whole(g.shape) for g in given],
+        out_specs=whole((rows, cut)),
+        compiler_params=params("arbitrary"),
+        name="self_outputs",
+    )(*given)
+
+
+def finish_kernel(own_ref, right_ref, left_ref, *refs):
+    total = own_ref[...] + right_ref[...].astype(F32) + left_ref[...].astype(F32)
+    refs[-1][...] = total.astype(BF)
+
+
+def finish(own, right, left, width, at, result):
+    rows, cut = own.shape
+    given = (own, right, left) + (() if result is None else (result,))
+    return pl.pallas_call(
+        finish_kernel,
+        out_shape=jax.ShapeDtypeStruct((rows, width), BF),
+        grid=(1,),
+        in_specs=[whole((rows, cut))] * 3
+        + ([] if result is None else [pl.BlockSpec(memory_space=pl.ANY)]),
+        out_specs=pl.BlockSpec((rows, cut), lambda i: (0, at)),
+        input_output_aliases={} if result is None else {3: 0},
+        compiler_params=params("arbitrary"),
+        name="finish",
+    )(*given)
+
+
+def ring_of(expert_size, mp_size):
+    chips = mp_size // 2
+    order = [(z, 0) for z in range(expert_size)]
+    for z in reversed(range(expert_size)):
+        side = list(range(1, chips)) if (expert_size - 1 - z) % 2 == 0 else list(range(chips - 1, 0, -1))
+        order += [(z, x) for x in side]
+    return [z * mp_size + 2 * x for z, x in order]
+
+
+def dense(expert_size, mp_size, tokens, expert_ids, route_weights, gate, up, down, code):
+    gate, up, down, code = gate[0], up[0], down[0], code[0]
+    tok_rows, width = tokens.shape
+    devices = expert_size * mp_size
+    ring = ring_of(expert_size, mp_size)
+    length = len(ring)
+    reach = length // 2
+    here = lax.axis_index(AXES)
+    core = here % 2
+    position = np.zeros((devices,), np.int32)
+    for i, base in enumerate(ring):
+        position[base] = position[base + 1] = i
+    position = jnp.asarray(position)[here]
+
+    def shift(value, by):
+        pairs = [
+            (ring[i] + c, ring[(i + by) % length] + c) for i in range(length) for c in range(2)
+        ]
+        return lax.ppermute(value, AXES, pairs)
+
+    def swap(value):
+        return lax.ppermute(value, AXES, [(i, i ^ 1) for i in range(devices)])
+
+    table = weight_table(expert_ids, route_weights, devices)
+    gate_other, up_other = swap(gate), swap(up)
+    table = lax.all_gather(table, AXES, axis=0, tiled=True)
+    around = jnp.asarray(np.array(ring + ring, np.int32))
+    sources = lax.dynamic_slice(around, (position,), (length,)) + core
+    place = (sources[:, None] * devices + jnp.stack([here, here ^ 1])[None, :]).reshape(-1)
+    weights = pick(place.astype(jnp.int32), table, length)
+
+    half = tok_rows // 2
+    top, bottom = tokens[:half], tokens[half:]
+    right, left = [top, bottom], [top, bottom]
+    hidden_own, hidden_other = [], []
+    gram_own = gram_other = None
+
+    def add(pieces, blocks):
+        nonlocal gram_own, gram_other
+        value, gram_other = hidden_part(
+            pieces, gate_other, up_other, weights, [2 * b + 1 for b in blocks], gram_other
+        )
+        hidden_other.append(value)
+        value, gram_own = hidden_part(pieces, gate, up, weights, [2 * b for b in blocks], gram_own)
+        hidden_own.append(value)
+
+    arrivals = []
+    for hop in range(1, reach + 1):
+        right[0] = shift(right[0], 1)
+        left[1] = shift(left[1], -1)
+        if hop < reach:
+            right[1] = shift(right[1], 1)
+            left[0] = shift(left[0], -1)
+            arrivals.append(((*right, *left), (length - hop, hop)))
+        else:
+            arrivals.append(((right[0], left[1]), (hop,)))
+    kept, error = masks(code, down)
+    add((tokens,), (0,))
+    for pieces, blocks in arrivals:
+        add(pieces, blocks)
+
+    gram_other = swap(gram_other)
+    cut = width // 2
+    pruned = [None, None]
+    pruned[0], high, low = prune_first(gram_own, gram_other, error, down, kept, cut)
+    pruned_other = [swap(pruned[0]), None]
+    pruned[1] = prune_next(high, low, error, down, kept, cut, 1)
+    pruned_other[1] = swap(pruned[1])
+
+    moving = [(), ()]
+    for hop in range(reach, 0, -1):
+        for at in range(2):
+            sent = outputs(
+                hidden_own[hop], hidden_other[hop], pruned[at], pruned_other[at], moving[at]
+            )
+            go_left, go_right = sent if hop < reach else (sent[1], sent[0])
+            moving[at] = (shift(go_left, -1), shift(go_right, 1))
+    mixed = None
+    for at in range(2):
+        own = self_outputs(hidden_own[0], hidden_other[0], pruned[at], pruned_other[at])
+        mixed = finish(own, *moving[at], width, at, mixed)
+    return mixed, jnp.concatenate(pruned, axis=1)[None]
+
+
+def local(expert_size, mp_size, section_size, *given):
+    tokens, expert_ids, _, gate_weight = given[:4]
+    devices = expert_size * mp_size
+    if (
+        section_size == 1
+        and gate_weight.shape[0] == 1
+        and 2 * expert_ids.shape[1] >= devices
+        and mp_size % 2 == 0
+        and devices >= 8
+    ):
+        return dense(expert_size, mp_size, *given)
+    return routed(*given)
+
+
 def solution(mesh):
     placed = (
         P(("groups", "expert", "mp"), "section"),
@@ -101,8 +506,9 @@
         P(("expert", "mp"), None, "section"),
         P(("expert", "mp"), None, "section"),
     )
+    sizes = mesh.shape
     return jax.shard_map(
-        local,
+        functools.partial(local, sizes["expert"], sizes["mp"], sizes["section"]),
         mesh=mesh,
         in_specs=placed,
         out_specs=(

time: 514 us -> 148 us (0.29)
  the two profiles are of different devices: /device:TPU:11 before, /device:TPU:0 now
where the time goes in v1:
time: 148 us
  Pallas kernels  44.9 us (30%)
  starting transfers between devices  37.8 us (26%)
  waiting for transfers between devices  35.2 us (24%)
  blocking collectives  21 us (14%)
  local copies, waits for them, and re-layouts  3.49 us (2%)
  other arithmetic  2.88 us (2%)
  between operations  2.88 us (2%)
    ppermute x30, starting transfers between devices, shift(): return lax.ppermute(value, AXES, pairs)  36.5 us
    ppermute x30, waiting for transfers between devices, shift(): return lax.ppermute(value, AXES, pairs)  34.4 us
    pallas_call x10, Pallas kernels, hidden_part(): pl.pallas_call(functools.partial(hidden_kernel, len(pieces), columns, gra...  25.8 us
    all_gather x1, blocking collectives, dense(): table = lax.all_gather(table, AXES, axis=0, tiled=True)  21 us
    pallas_call x1, Pallas kernels, prune_first(): pl.pallas_call(prune_kernel, out_shape=[jax.ShapeDtypeStruct((size, cut),...  5.64 us
    pallas_call x8, Pallas kernels, outputs(): pl.pallas_call(functools.partial(outputs_kernel, rows // 2, len(arrived))...  5.09 us
    pallas_call x1, Pallas kernels, masks(): pl.pallas_call(mask_kernel, out_shape=[jax.ShapeDtypeStruct((rows, width)...  4.23 us
  transfers between devices with their start and end apart: 35, of which 20 were waited for; matrix products, arithmetic and copies ran while one was open for 4% of the time, Pallas kernels for 25%

profile of v1, /device:TPU:0, one launch (start us, length us, event | category | flops | bytes accessed | tf_op | source)
XLA Modules:
  0.0 148.0 jit_solution(17150585881936297399)
XLA Ops:
  0.6 0.5 collective-permute-start
  1.2 1.1 fusion
  2.3 3.1 %collective-permute-start.10 = (bf16[64,2048]{1,0:T(8,128)(2,1)S(1)}, bf16[64,2048]{1,0:T(8,128)(2,1)S(1)}, u32[]{:S(2)}, u32[]{:S(2)}) collective-permute-start(bf16[64,2048]{1,0:T(8,128)(2,1)S(1)} %get-tuple-element.84), channel_id=1, source_target_pairs={{0,4},{1,5},{4,8},{5,9},{8,12},{9,13},{12,14},{13,15},{14,10},{15,... | collective-permute-start | bytes 786440 | tf_op jit(solution)/shard_map/ppermute | solution.py:419
  5.4 2.0 %collective-permute-start.2 = (bf16[64,2048]{1,0:T(8,128)(2,1)S(1)}, bf16[64,2048]{1,0:T(8,128)(2,1)}, u32[]{:S(2)}, u32[]{:S(2)}) collective-permute-start(bf16[64,2048]{1,0:T(8,128)(2,1)S(1)} %get-tuple-element.85), channel_id=1, source_target_pairs={{0,4},{1,5},{4,8},{5,9},{8,12},{9,13},{12,14},{13,15},{14,10},{15,... | collective-permute-start | bytes 786440 | tf_op jit(solution)/shard_map/ppermute | solution.py:419
  7.4 5.0 %collective-permute-done.10.refs_1_ = bf16[64,2048]{1,0:T(8,128)(2,1)S(1)} collective-permute-done((bf16[64,2048]{1,0:T(8,128)(2,1)S(1)}, bf16[64,2048]{1,0:T(8,128)(2,1)S(1)}, u32[]{:S(2)}, u32[]{:S(2)}) %collective-permute-start.10) | collective-permute-done | bytes 262176 | tf_op jit(solution)/shard_map/ppermute | solution.py:419
  12.4 2.1 %collective-permute-start.6 = (bf16[64,2048]{1,0:T(8,128)(2,1)S(1)}, bf16[64,2048]{1,0:T(8,128)(2,1)}, u32[]{:S(2)}, u32[]{:S(2)}) collective-permute-start(bf16[64,2048]{1,0:T(8,128)(2,1)S(1)} %get-tuple-element.84), channel_id=1, source_target_pairs={{0,2},{1,3},{4,0},{5,1},{8,4},{9,5},{12,8},{13,9},{14,12},{15,13},... | collective-permute-start | bytes 786440 | tf_op jit(solution)/shard_map/ppermute | solution.py:419
  14.4 0.6 collective-permute-start.11
  15.0 3.0 %collective-permute-done.2.refs_0_ = bf16[64,2048]{1,0:T(8,128)(2,1)} collective-permute-done((bf16[64,2048]{1,0:T(8,128)(2,1)S(1)}, bf16[64,2048]{1,0:T(8,128)(2,1)}, u32[]{:S(2)}, u32[]{:S(2)}) %collective-permute-start.2) | collective-permute-done | bytes 262176 | tf_op jit(solution)/shard_map/ppermute | solution.py:419
  18.1 2.1 %collective-permute-start.3 = (bf16[64,2048]{1,0:T(8,128)(2,1)}, bf16[64,2048]{1,0:T(8,128)(2,1)}, u32[]{:S(2)}, u32[]{:S(2)}) collective-permute-start(bf16[64,2048]{1,0:T(8,128)(2,1)} %collective-permute-done.2.refs_0_), channel_id=1, source_target_pairs={{0,4},{1,5},{4,8},{5,9},{8,12},{9,13},{12,14},{13,15},{14,10},{15,... | collective-permute-start | bytes 786440 | tf_op jit(solution)/shard_map/ppermute | solution.py:419
  20.2 1.0 collective-permute-start.7
  21.2 1.3 dynamic_slice.6
  24.4 1.6 %collective-permute-start.14 = (bf16[64,2048]{1,0:T(8,128)(2,1)}, bf16[64,2048]{1,0:T(8,128)(2,1)}, u32[]{:S(2)}, u32[]{:S(2)}) collective-permute-start(bf16[64,2048]{1,0:T(8,128)(2,1)} %collective-permute-done.13.refs_2_), channel_id=1, source_target_pairs={{0,2},{1,3},{4,0},{5,1},{8,4},{9,5},{12,8},{13,9},{14,12},{15,13},... | collective-permute-start | bytes 786440 | tf_op jit(solution)/shard_map/ppermute | solution.py:419
  26.0 2.8 %collective-permute-done.3.refs_0_ = bf16[64,2048]{1,0:T(8,128)(2,1)} collective-permute-done((bf16[64,2048]{1,0:T(8,128)(2,1)}, bf16[64,2048]{1,0:T(8,128)(2,1)}, u32[]{:S(2)}, u32[]{:S(2)}) %collective-permute-start.3) | collective-permute-done | bytes 262176 | tf_op jit(solution)/shard_map/ppermute | solution.py:419
  28.8 1.8 %collective-permute-start.4 = (bf16[64,2048]{1,0:T(8,128)(2,1)}, bf16[64,2048]{1,0:T(8,128)(2,1)}, u32[]{:S(2)}, u32[]{:S(2)}) collective-permute-start(bf16[64,2048]{1,0:T(8,128)(2,1)} %collective-permute-done.3.refs_0_), channel_id=1, source_target_pairs={{0,4},{1,5},{4,8},{5,9},{8,12},{9,13},{12,14},{13,15},{14,10},{15,... | collective-permute-start | bytes 786440 | tf_op jit(solution)/shard_map/ppermute | solution.py:419
  30.6 0.7 add_multiply_fusion
  31.6 0.9 collective-permute-done.14.refs_2_
  32.5 1.6 %collective-permute-start.12 = (bf16[64,2048]{1,0:T(8,128)(2,1)}, bf16[64,2048]{1,0:T(8,128)(2,1)}, u32[]{:S(2)}, u32[]{:S(2)}) collective-permute-start(bf16[64,2048]{1,0:T(8,128)(2,1)} %collective-permute-done.11.refs_1_), channel_id=1, source_target_pairs={{0,4},{1,5},{4,8},{5,9},{8,12},{9,13},{12,14},{13,15},{14,10},{15,... | collective-permute-start | bytes 786440 | tf_op jit(solution)/shard_map/ppermute | solution.py:419
  34.1 4.2 %collective-permute-done.4.refs_0_ = bf16[64,2048]{1,0:T(8,128)(2,1)} collective-permute-done((bf16[64,2048]{1,0:T(8,128)(2,1)}, bf16[64,2048]{1,0:T(8,128)(2,1)}, u32[]{:S(2)}, u32[]{:S(2)}) %collective-permute-start.4) | collective-permute-done | bytes 262176 | tf_op jit(solution)/shard_map/ppermute | solution.py:419
  38.3 1.7 %collective-permute-start.15 = (bf16[64,2048]{1,0:T(8,128)(2,1)}, bf16[64,2048]{1,0:T(8,128)(2,1)}, u32[]{:S(2)}, u32[]{:S(2)}) collective-permute-start(bf16[64,2048]{1,0:T(8,128)(2,1)} %collective-permute-done.14.refs_2_), channel_id=1, source_target_pairs={{0,2},{1,3},{4,0},{5,1},{8,4},{9,5},{12,8},{13,9},{14,12},{15,13},... | collective-permute-start | bytes 786440 | tf_op jit(solution)/shard_map/ppermute | solution.py:419
  40.1 0.7 select_reduce_fusion
  40.9 21.0 %all_gather.3.table_ref = f32[256,128]{1,0:T(8,128)S(1)} all-gather(f32[16,128]{1,0:T(8,128)S(1)} %select_reduce_fusion), channel_id=1, replica_groups=mesh['groups'=2,'expert'=4,'mp'=4,'section'=1] {'expert','mp'}, dimensions={0}, use_global_device_ids=true | all-gather | bytes 139264 | tf_op jit(solution)/shard_map/all_gather | solution.py:426
  61.9 0.6 pick.1.refs_3_.refs_6_.refs_4_
  62.6 2.0 %collective-permute-start.9 = (bf16[64,2048]{1,0:T(8,128)(2,1)}, bf16[64,2048]{1,0:T(8,128)(2,1)S(1)}, u32[]{:S(2)}, u32[]{:S(2)}) collective-permute-start(bf16[64,2048]{1,0:T(8,128)(2,1)} %collective-permute-done.8.refs_3_), channel_id=1, source_target_pairs={{0,2},{1,3},{4,0},{5,1},{8,4},{9,5},{12,8},{13,9},{14,12},{15,13},... | collective-permute-start | bytes 786440 | tf_op jit(solution)/shard_map/ppermute | solution.py:419
  64.6 1.0 copy-done.3
  65.7 1.8 %hidden.11 = (bf16[128,384]{1,0:T(8,128)(2,1)S(1)}, f32[384,384]{1,0:T(8,128)S(1)}) custom-call(bf16[128,2048]{1,0:T(8,128)(2,1)S(1)} %copy-done.3, bf16[384,2048]{1,0:T(8,128)(2,1)S(1)} %collective-permute-done.refs_1_.refs_4_.refs_2_, bf16[384,2048]{1,0:T(8,128)(2,1)S(1)} %collective-permute-done.1.refs_2_.refs_5_.refs_3_, ...), custom_call_target="tpu_custom_call" | custom-call | flops 402653184 | bytes 3670016 | tf_op jit(solution)/shard_map/hidden/pallas_call | solution.py:218
  67.5 3.0 %hidden.16 = (bf16[256,384]{1,0:T(8,128)(2,1)S(1)}, f32[384,384]{1,0:T(8,128)S(1)}) custom-call(bf16[64,2048]{1,0:T(8,128)(2,1)} %collective-permute-done.2.refs_0_, bf16[64,2048]{1,0:T(8,128)(2,1)S(1)} %collective-permute-done.10.refs_1_, bf16[64,2048]{1,0:T(8,128)(2,1)} %collective-permute-done.13.refs_2_, ...), custom_call_target="tpu_custom_call" | custom-call | flops 805306368 | bytes 4194304 | tf_op jit(solution)/shard_map/hidden/pallas_call | solution.py:218
  70.5 3.1 %hidden.17 = (bf16[256,384]{1,0:T(8,128)(2,1)S(1)}, f32[384,384]{1,0:T(8,128)S(1)}) custom-call(bf16[64,2048]{1,0:T(8,128)(2,1)} %collective-permute-done.3.refs_0_, bf16[64,2048]{1,0:T(8,128)(2,1)} %collective-permute-done.11.refs_1_, bf16[64,2048]{1,0:T(8,128)(2,1)} %collective-permute-done.14.refs_2_, bf16[64,2048]{1,0:T(8,128)(2,1)} %collective-permute-done.7.refs_3_, ...), custom_call_target="tpu_custom_call" | custom-call | flops 805306368 | bytes 4194304 | tf_op jit(solution)/shard_map/hidden/pallas_call | solution.py:218
  73.6 3.1 %hidden.18 = (bf16[256,384]{1,0:T(8,128)(2,1)S(1)}, f32[384,384]{1,0:T(8,128)S(1)}) custom-call(bf16[64,2048]{1,0:T(8,128)(2,1)} %collective-permute-done.4.refs_0_, bf16[64,2048]{1,0:T(8,128)(2,1)} %collective-permute-done.12.refs_1_, bf16[64,2048]{1,0:T(8,128)(2,1)} %collective-permute-done.15.refs_2_, bf16[64,2048]{1,0:T(8,128)(2,1)} %collective-permute-done.8.refs_3_, ...), custom_call_target="tpu_custom_call" | custom-call | flops 805306368 | bytes 4194304 | tf_op jit(solution)/shard_map/hidden/pallas_call | solution.py:218
  76.7 1.9 %hidden.19 = (bf16[128,384]{1,0:T(8,128)(2,1)S(1)}, f32[384,384]{1,0:T(8,128)S(1)}) custom-call(bf16[64,2048]{1,0:T(8,128)(2,1)S(1)} %collective-permute-done.5.refs_0_, bf16[64,2048]{1,0:T(8,128)(2,1)S(1)} %collective-permute-done.9.refs_1_, bf16[384,2048]{1,0:T(8,128)(2,1)S(1)} %collective-permute-done.refs_1_.refs_4_.refs_2_, ...), custom_call_target="tpu_custom_call" | custom-call | flops 402653184 | bytes 3670016 | tf_op jit(solution)/shard_map/hidden/pallas_call | solution.py:218
  78.7 4.2 %masks.1 = (bf16[384,2048]{1,0:T(8,128)(2,1)S(1)}, bf16[384,2048]{1,0:T(8,128)(2,1)S(1)}) custom-call(s32[96,2048]{1,0:T(8,128)S(1)} %bitcast.24, bf16[384,2048]{1,0:T(8,128)(2,1)S(1)} %bitcast.21), custom_call_target="tpu_custom_call" | custom-call | tf_op jit(solution)/shard_map/masks/pallas_call | solution.py:176
  83.0 1.9 %hidden.10 = (bf16[128,384]{1,0:T(8,128)(2,1)S(1)}, f32[384,384]{1,0:T(8,128)S(1)}) custom-call(bf16[128,2048]{1,0:T(8,128)(2,1)S(1)} %copy-done.4, bf16[384,2048]{1,0:T(8,128)(2,1)S(1)} %bitcast.10, bf16[384,2048]{1,0:T(8,128)(2,1)S(1)} %bitcast.16, f32[128,16]{1,0:T(8,128)S(1)} %pick.1.refs_3_.refs_6_.refs_4_), custom_call_target="tpu_custom_call" | custom-call | flops 402653184 | bytes 3670016 | tf_op jit(solution)/shard_map/hidden/pallas_call | solution.py:218
  84.8 3.0 %hidden.12 = (bf16[256,384]{1,0:T(8,128)(2,1)S(1)}, f32[384,384]{1,0:T(8,128)S(1)}) custom-call(bf16[64,2048]{1,0:T(8,128)(2,1)} %collective-permute-done.2.refs_0_, bf16[64,2048]{1,0:T(8,128)(2,1)S(1)} %collective-permute-done.10.refs_1_, bf16[64,2048]{1,0:T(8,128)(2,1)} %collective-permute-done.13.refs_2_, ...), custom_call_target="tpu_custom_call" | custom-call | flops 805306368 | bytes 4194304 | tf_op jit(solution)/shard_map/hidden/pallas_call | solution.py:218
  87.8 3.1 %hidden.13 = (bf16[256,384]{1,0:T(8,128)(2,1)S(1)}, f32[384,384]{1,0:T(8,128)S(1)}) custom-call(bf16[64,2048]{1,0:T(8,128)(2,1)} %collective-permute-done.3.refs_0_, bf16[64,2048]{1,0:T(8,128)(2,1)} %collective-permute-done.11.refs_1_, bf16[64,2048]{1,0:T(8,128)(2,1)} %collective-permute-done.14.refs_2_, bf16[64,2048]{1,0:T(8,128)(2,1)} %collective-permute-done.7.refs_3_, ...), custom_call_target="tpu_custom_call" | custom-call | flops 805306368 | bytes 4194304 | tf_op jit(solution)/shard_map/hidden/pallas_call | solution.py:218
  90.9 3.1 %hidden.14 = (bf16[256,384]{1,0:T(8,128)(2,1)S(1)}, f32[384,384]{1,0:T(8,128)S(1)}) custom-call(bf16[64,2048]{1,0:T(8,128)(2,1)} %collective-permute-done.4.refs_0_, bf16[64,2048]{1,0:T(8,128)(2,1)} %collective-permute-done.12.refs_1_, bf16[64,2048]{1,0:T(8,128)(2,1)} %collective-permute-done.15.refs_2_, bf16[64,2048]{1,0:T(8,128)(2,1)} %collective-permute-done.8.refs_3_, ...), custom_call_target="tpu_custom_call" | custom-call | flops 805306368 | bytes 4194304 | tf_op jit(solution)/shard_map/hidden/pallas_call | solution.py:218
  94.0 2.0 %hidden.15 = (bf16[128,384]{1,0:T(8,128)(2,1)S(1)}, f32[384,384]{1,0:T(8,128)S(1)}) custom-call(bf16[64,2048]{1,0:T(8,128)(2,1)S(1)} %collective-permute-done.5.refs_0_, bf16[64,2048]{1,0:T(8,128)(2,1)S(1)} %collective-permute-done.9.refs_1_, bf16[384,2048]{1,0:T(8,128)(2,1)S(1)} %bitcast.14, bf16[384,2048]{1,0:T(8,128)(2,1)S(1)} %bitcast.20, ...), custom_call_target="tpu_custom_call" | custom-call | flops 402653184 | bytes 3670016 | tf_op jit(solution)/shard_map/hidden/pallas_call | solution.py:218
  96.0 5.6 %prune.1 = (bf16[384,1024]{1,0:T(8,128)(2,1)S(1)}, bf16[384,384]{1,0:T(8,128)(2,1)S(1)}, bf16[384,384]{1,0:T(8,128)(2,1)S(1)}) custom-call(f32[384,384]{1,0:T(8,128)S(1)} %get-tuple-element.49.own_ref, f32[384,384]{1,0:T(8,128)S(1)} %collective-permute-done.16.other_ref, bf16[384,2048]{1,0:T(8,128)(2,1)S(1)} %get-tuple-element.55.error_ref, ...), custom_call_target="tpu_custom_call" | custom-call | tf_op jit(solution)/shard_map/prune/pallas_call | solution.py:291
  101.7 0.5 collective-permute-start.26
  102.2 1.0 prune_next.1.own_ref
  103.3 0.8 collective-permute-done.26.other_ref
  104.6 2.0 %collective-permute-start.28 = (bf16[64,1024]{1,0:T(8,128)(2,1)S(1)}, bf16[64,1024]{1,0:T(8,128)(2,1)S(1)}, u32[]{:S(2)}, u32[]{:S(2)}) collective-permute-start(bf16[64,1024]{1,0:T(8,128)(2,1)S(1)} %get-tuple-element.77), channel_id=1, source_target_pairs={{0,4},{1,5},{4,8},{5,9},{8,12},{9,13},{12,14},{13,15},{14,10},{15,... | collective-permute-start | bytes 393224 | tf_op jit(solution)/shard_map/ppermute | solution.py:419
  106.7 0.4 outputs.8
  107.2 2.0 %collective-permute-start.19 = (bf16[64,1024]{1,0:T(8,128)(2,1)S(1)}, bf16[64,1024]{1,0:T(8,128)(2,1)S(1)}, u32[]{:S(2)}, u32[]{:S(2)}) collective-permute-start(bf16[64,1024]{1,0:T(8,128)(2,1)S(1)} %get-tuple-element.68), channel_id=1, source_target_pairs={{0,4},{1,5},{4,8},{5,9},{8,12},{9,13},{12,14},{13,15},{14,10},{15,... | collective-permute-start | bytes 393224 | tf_op jit(solution)/shard_map/ppermute | solution.py:419
  109.2 1.8 %collective-permute-done.27.refs_0_ = bf16[64,1024]{1,0:T(8,128)(2,1)S(1)} collective-permute-done((bf16[64,1024]{1,0:T(8,128)(2,1)S(1)}, bf16[64,1024]{1,0:T(8,128)(2,1)S(1)}, u32[]{:S(2)}, u32[]{:S(2)}) %collective-permute-start.27) | collective-permute-done | bytes 131104 | tf_op jit(solution)/shard_map/ppermute | solution.py:419
  111.0 0.7 outputs.13
  111.8 2.0 %collective-permute-start.30 = (bf16[128,1024]{1,0:T(8,128)(2,1)S(1)}, bf16[128,1024]{1,0:T(8,128)(2,1)S(1)}, u32[]{:S(2)}, u32[]{:S(2)}) collective-permute-start(bf16[128,1024]{1,0:T(8,128)(2,1)S(1)} %get-tuple-element.79), channel_id=1, source_target_pairs={{0,4},{1,5},{4,8},{5,9},{8,12},{9,13},{12,14},{13,15},{14,10},{15,... | collective-permute-start | bytes 786440 | tf_op jit(solution)/shard_map/ppermute | solution.py:419
  113.8 0.7 outputs.9
  114.6 2.0 %collective-permute-start.21 = (bf16[128,1024]{1,0:T(8,128)(2,1)S(1)}, bf16[128,1024]{1,0:T(8,128)(2,1)S(1)}, u32[]{:S(2)}, u32[]{:S(2)}) collective-permute-start(bf16[128,1024]{1,0:T(8,128)(2,1)S(1)} %get-tuple-element.70), channel_id=1, source_target_pairs={{0,4},{1,5},{4,8},{5,9},{8,12},{9,13},{12,14},{13,15},{14,10},{15,... | collective-permute-start | bytes 786440 | tf_op jit(solution)/shard_map/ppermute | solution.py:419
  116.6 4.4 %collective-permute-done.29.refs_0_ = bf16[128,1024]{1,0:T(8,128)(2,1)S(1)} collective-permute-done((bf16[128,1024]{1,0:T(8,128)(2,1)S(1)}, bf16[128,1024]{1,0:T(8,128)(2,1)S(1)}, u32[]{:S(2)}, u32[]{:S(2)}) %collective-permute-start.29) | collective-permute-done | bytes 262176 | tf_op jit(solution)/shard_map/ppermute | solution.py:419
  121.1 0.7 outputs.14
  121.9 2.0 %collective-permute-start.32 = (bf16[128,1024]{1,0:T(8,128)(2,1)S(1)}, bf16[128,1024]{1,0:T(8,128)(2,1)S(1)}, u32[]{:S(2)}, u32[]{:S(2)}) collective-permute-start(bf16[128,1024]{1,0:T(8,128)(2,1)S(1)} %get-tuple-element.81), channel_id=1, source_target_pairs={{0,4},{1,5},{4,8},{5,9},{8,12},{9,13},{12,14},{13,15},{14,10},{15,... | collective-permute-start | bytes 786440 | tf_op jit(solution)/shard_map/ppermute | solution.py:419
  123.9 2.8 %collective-permute-done.20.refs_0_ = bf16[128,1024]{1,0:T(8,128)(2,1)S(1)} collective-permute-done((bf16[128,1024]{1,0:T(8,128)(2,1)S(1)}, bf16[128,1024]{1,0:T(8,128)(2,1)S(1)}, u32[]{:S(2)}, u32[]{:S(2)}) %collective-permute-start.20) | collective-permute-done | bytes 262176 | tf_op jit(solution)/shard_map/ppermute | solution.py:419
  126.7 0.7 outputs.10
  127.5 2.0 %collective-permute-start.23 = (bf16[128,1024]{1,0:T(8,128)(2,1)S(1)}, bf16[128,1024]{1,0:T(8,128)(2,1)S(1)}, u32[]{:S(2)}, u32[]{:S(2)}) collective-permute-start(bf16[128,1024]{1,0:T(8,128)(2,1)S(1)} %get-tuple-element.72), channel_id=1, source_target_pairs={{0,4},{1,5},{4,8},{5,9},{8,12},{9,13},{12,14},{13,15},{14,10},{15,... | collective-permute-start | bytes 786440 | tf_op jit(solution)/shard_map/ppermute | solution.py:419
  129.5 2.8 %collective-permute-done.31.refs_0_ = bf16[128,1024]{1,0:T(8,128)(2,1)S(1)} collective-permute-done((bf16[128,1024]{1,0:T(8,128)(2,1)S(1)}, bf16[128,1024]{1,0:T(8,128)(2,1)S(1)}, u32[]{:S(2)}, u32[]{:S(2)}) %collective-permute-start.31) | collective-permute-done | bytes 262176 | tf_op jit(solution)/shard_map/ppermute | solution.py:419
  132.3 0.7 outputs.15
  133.1 2.0 %collective-permute-start.34 = (bf16[128,1024]{1,0:T(8,128)(2,1)S(1)}, bf16[128,1024]{1,0:T(8,128)(2,1)S(1)}, u32[]{:S(2)}, u32[]{:S(2)}) collective-permute-start(bf16[128,1024]{1,0:T(8,128)(2,1)S(1)} %get-tuple-element.83), channel_id=1, source_target_pairs={{0,4},{1,5},{4,8},{5,9},{8,12},{9,13},{12,14},{13,15},{14,10},{15,... | collective-permute-start | bytes 786440 | tf_op jit(solution)/shard_map/ppermute | solution.py:419
  135.1 2.8 %collective-permute-done.22.refs_0_ = bf16[128,1024]{1,0:T(8,128)(2,1)S(1)} collective-permute-done((bf16[128,1024]{1,0:T(8,128)(2,1)S(1)}, bf16[128,1024]{1,0:T(8,128)(2,1)S(1)}, u32[]{:S(2)}, u32[]{:S(2)}) %collective-permute-start.22) | collective-permute-done | bytes 262176 | tf_op jit(solution)/shard_map/ppermute | solution.py:419
  137.9 0.7 outputs.11
  138.7 2.0 %collective-permute-start.25 = (bf16[128,1024]{1,0:T(8,128)(2,1)S(1)}, bf16[128,1024]{1,0:T(8,128)(2,1)S(1)}, u32[]{:S(2)}, u32[]{:S(2)}) collective-permute-start(bf16[128,1024]{1,0:T(8,128)(2,1)S(1)} %get-tuple-element.74), channel_id=1, source_target_pairs={{0,4},{1,5},{4,8},{5,9},{8,12},{9,13},{12,14},{13,15},{14,10},{15,... | collective-permute-start | bytes 786440 | tf_op jit(solution)/shard_map/ppermute | solution.py:419
  140.7 1.3 maximum_bitcast_fusion
  142.9 0.6 collective-permute-done.33.right_ref
  143.6 0.8 finish.2.refs_0_
  144.3 2.7 %collective-permute-done.24.right_ref = bf16[128,1024]{1,0:T(8,128)(2,1)S(1)} collective-permute-done((bf16[128,1024]{1,0:T(8,128)(2,1)S(1)}, bf16[128,1024]{1,0:T(8,128)(2,1)S(1)}, u32[]{:S(2)}, u32[]{:S(2)}) %collective-permute-start.24) | collective-permute-done | bytes 262176 | tf_op jit(solution)/shard_map/ppermute | solution.py:419
  147.2 0.8 finish.3
  (53 shorter events, 3.2 us)
Async XLA Ops:
  0.6 62.0 %collective-permute-start = (bf16[384,2048]{1,0:T(8,128)(2,1)}, bf16[384,2048]{1,0:T(8,128)(2,1)S(1)}, u32[]{:S(2)}, u32[]{:S(2)}) collective-permute-start(bf16[384,2048]{1,0:T(8,128)(2,1)} %bitcast.9), channel_id=1, source_target_pairs={{0,1},{1,0},{2,3},{3,2},{4,5},{5,4},{6,7},{7,6},{8,9},{9,8},{10,11... | collective-permute-start | bytes 4718600 | tf_op jit(solution)/shard_map/ppermute | solution.py:422
  1.1 63.5 %collective-permute-start.1 = (bf16[384,2048]{1,0:T(8,128)(2,1)}, bf16[384,2048]{1,0:T(8,128)(2,1)S(1)}, u32[]{:S(2)}, u32[]{:S(2)}) collective-permute-start(bf16[384,2048]{1,0:T(8,128)(2,1)} %bitcast.15), channel_id=1, source_target_pairs={{0,1},{1,0},{2,3},{3,2},{4,5},{5,4},{6,7},{7,6},{8,9},{9,8},{10,11... | collective-permute-start | bytes 4718600 | tf_op jit(solution)/shard_map/ppermute | solution.py:422
  2.3 10.1 %collective-permute-start.10 = (bf16[64,2048]{1,0:T(8,128)(2,1)S(1)}, bf16[64,2048]{1,0:T(8,128)(2,1)S(1)}, u32[]{:S(2)}, u32[]{:S(2)}) collective-permute-start(bf16[64,2048]{1,0:T(8,128)(2,1)S(1)} %get-tuple-element.84), channel_id=1, source_target_pairs={{0,4},{1,5},{4,8},{5,9},{8,12},{9,13},{12,14},{13,15},{14,10},{15,... | collective-permute-start | bytes 786440 | tf_op jit(solution)/shard_map/ppermute | solution.py:419
  5.3 9.1 %collective-permute-start.13 = (bf16[64,2048]{1,0:T(8,128)(2,1)S(1)}, bf16[64,2048]{1,0:T(8,128)(2,1)}, u32[]{:S(2)}, u32[]{:S(2)}) collective-permute-start(bf16[64,2048]{1,0:T(8,128)(2,1)S(1)} %get-tuple-element.85), channel_id=1, source_target_pairs={{0,2},{1,3},{4,0},{5,1},{8,4},{9,5},{12,8},{13,9},{14,12},{15,13},... | collective-permute-start | bytes 786440 | tf_op jit(solution)/shard_map/ppermute | solution.py:419
  5.4 12.7 %collective-permute-start.2 = (bf16[64,2048]{1,0:T(8,128)(2,1)S(1)}, bf16[64,2048]{1,0:T(8,128)(2,1)}, u32[]{:S(2)}, u32[]{:S(2)}) collective-permute-start(bf16[64,2048]{1,0:T(8,128)(2,1)S(1)} %get-tuple-element.85), channel_id=1, source_target_pairs={{0,4},{1,5},{4,8},{5,9},{8,12},{9,13},{12,14},{13,15},{14,10},{15,... | collective-permute-start | bytes 786440 | tf_op jit(solution)/shard_map/ppermute | solution.py:419
  12.4 7.9 %collective-permute-start.6 = (bf16[64,2048]{1,0:T(8,128)(2,1)S(1)}, bf16[64,2048]{1,0:T(8,128)(2,1)}, u32[]{:S(2)}, u32[]{:S(2)}) collective-permute-start(bf16[64,2048]{1,0:T(8,128)(2,1)S(1)} %get-tuple-element.84), channel_id=1, source_target_pairs={{0,2},{1,3},{4,0},{5,1},{8,4},{9,5},{12,8},{13,9},{14,12},{15,13},... | collective-permute-start | bytes 786440 | tf_op jit(solution)/shard_map/ppermute | solution.py:419
  14.4 10.0 %collective-permute-start.11 = (bf16[64,2048]{1,0:T(8,128)(2,1)S(1)}, bf16[64,2048]{1,0:T(8,128)(2,1)}, u32[]{:S(2)}, u32[]{:S(2)}) collective-permute-start(bf16[64,2048]{1,0:T(8,128)(2,1)S(1)} %collective-permute-done.10.refs_1_), channel_id=1, source_target_pairs={{0,4},{1,5},{4,8},{5,9},{8,12},{9,13},{12,14},{13,15},{14,10},{15,... | collective-permute-start | bytes 786440 | tf_op jit(solution)/shard_map/ppermute | solution.py:419
  18.1 10.7 %collective-permute-start.3 = (bf16[64,2048]{1,0:T(8,128)(2,1)}, bf16[64,2048]{1,0:T(8,128)(2,1)}, u32[]{:S(2)}, u32[]{:S(2)}) collective-permute-start(bf16[64,2048]{1,0:T(8,128)(2,1)} %collective-permute-done.2.refs_0_), channel_id=1, source_target_pairs={{0,4},{1,5},{4,8},{5,9},{8,12},{9,13},{12,14},{13,15},{14,10},{15,... | collective-permute-start | bytes 786440 | tf_op jit(solution)/shard_map/ppermute | solution.py:419
  20.2 11.1 %collective-permute-start.7 = (bf16[64,2048]{1,0:T(8,128)(2,1)}, bf16[64,2048]{1,0:T(8,128)(2,1)}, u32[]{:S(2)}, u32[]{:S(2)}) collective-permute-start(bf16[64,2048]{1,0:T(8,128)(2,1)} %collective-permute-done.6.refs_3_), channel_id=1, source_target_pairs={{0,2},{1,3},{4,0},{5,1},{8,4},{9,5},{12,8},{13,9},{14,12},{15,13},... | collective-permute-start | bytes 786440 | tf_op jit(solution)/shard_map/ppermute | solution.py:419
  24.4 8.1 %collective-permute-start.14 = (bf16[64,2048]{1,0:T(8,128)(2,1)}, bf16[64,2048]{1,0:T(8,128)(2,1)}, u32[]{:S(2)}, u32[]{:S(2)}) collective-permute-start(bf16[64,2048]{1,0:T(8,128)(2,1)} %collective-permute-done.13.refs_2_), channel_id=1, source_target_pairs={{0,2},{1,3},{4,0},{5,1},{8,4},{9,5},{12,8},{13,9},{14,12},{15,13},... | collective-permute-start | bytes 786440 | tf_op jit(solution)/shard_map/ppermute | solution.py:419
  28.8 9.6 %collective-permute-start.4 = (bf16[64,2048]{1,0:T(8,128)(2,1)}, bf16[64,2048]{1,0:T(8,128)(2,1)}, u32[]{:S(2)}, u32[]{:S(2)}) collective-permute-start(bf16[64,2048]{1,0:T(8,128)(2,1)} %collective-permute-done.3.refs_0_), channel_id=1, source_target_pairs={{0,4},{1,5},{4,8},{5,9},{8,12},{9,13},{12,14},{13,15},{14,10},{15,... | collective-permute-start | bytes 786440 | tf_op jit(solution)/shard_map/ppermute | solution.py:419
  31.3 31.2 %collective-permute-start.8 = (bf16[64,2048]{1,0:T(8,128)(2,1)}, bf16[64,2048]{1,0:T(8,128)(2,1)}, u32[]{:S(2)}, u32[]{:S(2)}) collective-permute-start(bf16[64,2048]{1,0:T(8,128)(2,1)} %collective-permute-done.7.refs_3_), channel_id=1, source_target_pairs={{0,2},{1,3},{4,0},{5,1},{8,4},{9,5},{12,8},{13,9},{14,12},{15,13},... | collective-permute-start | bytes 786440 | tf_op jit(solution)/shard_map/ppermute | solution.py:419
  32.5 41.0 %collective-permute-start.12 = (bf16[64,2048]{1,0:T(8,128)(2,1)}, bf16[64,2048]{1,0:T(8,128)(2,1)}, u32[]{:S(2)}, u32[]{:S(2)}) collective-permute-start(bf16[64,2048]{1,0:T(8,128)(2,1)} %collective-permute-done.11.refs_1_), channel_id=1, source_target_pairs={{0,4},{1,5},{4,8},{5,9},{8,12},{9,13},{12,14},{13,15},{14,10},{15,... | collective-permute-start | bytes 786440 | tf_op jit(solution)/shard_map/ppermute | solution.py:419
  38.3 35.2 %collective-permute-start.15 = (bf16[64,2048]{1,0:T(8,128)(2,1)}, bf16[64,2048]{1,0:T(8,128)(2,1)}, u32[]{:S(2)}, u32[]{:S(2)}) collective-permute-start(bf16[64,2048]{1,0:T(8,128)(2,1)} %collective-permute-done.14.refs_2_), channel_id=1, source_target_pairs={{0,2},{1,3},{4,0},{5,1},{8,4},{9,5},{12,8},{13,9},{14,12},{15,13},... | collective-permute-start | bytes 786440 | tf_op jit(solution)/shard_map/ppermute | solution.py:419
  62.5 14.1 %collective-permute-start.5 = (bf16[64,2048]{1,0:T(8,128)(2,1)}, bf16[64,2048]{1,0:T(8,128)(2,1)S(1)}, u32[]{:S(2)}, u32[]{:S(2)}) collective-permute-start(bf16[64,2048]{1,0:T(8,128)(2,1)} %collective-permute-done.4.refs_0_), channel_id=1, source_target_pairs={{0,4},{1,5},{4,8},{5,9},{8,12},{9,13},{12,14},{13,15},{14,10},{15,... | collective-permute-start | bytes 786440 | tf_op jit(solution)/shard_map/ppermute | solution.py:419
  62.6 14.1 %collective-permute-start.9 = (bf16[64,2048]{1,0:T(8,128)(2,1)}, bf16[64,2048]{1,0:T(8,128)(2,1)S(1)}, u32[]{:S(2)}, u32[]{:S(2)}) collective-permute-start(bf16[64,2048]{1,0:T(8,128)(2,1)} %collective-permute-done.8.refs_3_), channel_id=1, source_target_pairs={{0,2},{1,3},{4,0},{5,1},{8,4},{9,5},{12,8},{13,9},{14,12},{15,13},... | collective-permute-start | bytes 786440 | tf_op jit(solution)/shard_map/ppermute | solution.py:419
  64.6 1.0 copy-start.3
  76.7 2.0 %copy-start.2 = (bf16[1,384,2048]{2,1,0:T(8,128)(2,1)S(1)}, bf16[1,384,2048]{2,1,0:T(8,128)(2,1)}, u32[]{:S(2)}) copy-start(bf16[1,384,2048]{2,1,0:T(8,128)(2,1)} %param.14) | copy-start | bytes 4718596
  76.7 2.0 %copy-start.5 = (s32[1,96,2048]{2,1,0:T(8,128)S(1)}, s32[1,96,2048]{2,1,0:T(8,128)}, u32[]{:S(2)}) copy-start(s32[1,96,2048]{2,1,0:T(8,128)} %param.15) | copy-start | bytes 2359300
  76.7 6.2 %copy-start.1 = (bf16[1,384,2048]{2,1,0:T(8,128)(2,1)S(1)}, bf16[1,384,2048]{2,1,0:T(8,128)(2,1)}, u32[]{:S(2)}) copy-start(bf16[1,384,2048]{2,1,0:T(8,128)(2,1)} %param.13) | copy-start | bytes 4718596
  78.6 4.4 %copy-start = (bf16[1,384,2048]{2,1,0:T(8,128)(2,1)S(1)}, bf16[1,384,2048]{2,1,0:T(8,128)(2,1)}, u32[]{:S(2)}) copy-start(bf16[1,384,2048]{2,1,0:T(8,128)(2,1)} %param.12) | copy-start | bytes 4718596
  78.6 4.4 %copy-start.4 = (bf16[128,2048]{1,0:T(8,128)(2,1)S(1)}, bf16[128,2048]{1,0:T(8,128)(2,1)}, u32[]{:S(2)}) copy-start(bf16[128,2048]{1,0:T(8,128)(2,1)} %refs_0_.3) | copy-start | bytes 1572868
  78.6 17.4 %collective-permute-start.16 = (f32[384,384]{1,0:T(8,128)S(1)}, f32[384,384]{1,0:T(8,128)S(1)}, u32[]{:S(2)}, u32[]{:S(2)}) collective-permute-start(f32[384,384]{1,0:T(8,128)S(1)} %get-tuple-element.54), channel_id=1, source_target_pairs={{0,1},{1,0},{2,3},{3,2},{4,5},{5,4},{6,7},{7,6},{8,9},{9,8},{10,11... | collective-permute-start | bytes 1769480 | tf_op jit(solution)/shard_map/ppermute | solution.py:422
  101.7 2.4 %collective-permute-start.26 = (bf16[384,1024]{1,0:T(8,128)(2,1)S(1)}, bf16[384,1024]{1,0:T(8,128)(2,1)S(1)}, u32[]{:S(2)}, u32[]{:S(2)}) collective-permute-start(bf16[384,1024]{1,0:T(8,128)(2,1)S(1)} %get-tuple-element.75.own_ref), channel_id=1, source_target_pairs={{0,1},{1,0},{2,3},{3,2},{4,5},{5,4},{6,7},{7,6},{8,9},{9,8},{10,11... | collective-permute-start | bytes 2359304 | tf_op jit(solution)/shard_map/ppermute | solution.py:422
  103.2 3.4 %collective-permute-start.17 = (bf16[384,1024]{1,0:T(8,128)(2,1)S(1)}, bf16[384,1024]{1,0:T(8,128)(2,1)S(1)}, u32[]{:S(2)}, u32[]{:S(2)}) collective-permute-start(bf16[384,1024]{1,0:T(8,128)(2,1)S(1)} %prune_next.1.own_ref), channel_id=1, source_target_pairs={{0,1},{1,0},{2,3},{3,2},{4,5},{5,4},{6,7},{7,6},{8,9},{9,8},{10,11... | collective-permute-start | bytes 2359304 | tf_op jit(solution)/shard_map/ppermute | solution.py:422
  104.6 6.4 %collective-permute-start.27 = (bf16[64,1024]{1,0:T(8,128)(2,1)S(1)}, bf16[64,1024]{1,0:T(8,128)(2,1)S(1)}, u32[]{:S(2)}, u32[]{:S(2)}) collective-permute-start(bf16[64,1024]{1,0:T(8,128)(2,1)S(1)} %get-tuple-element.76), channel_id=1, source_target_pairs={{0,2},{1,3},{4,0},{5,1},{8,4},{9,5},{12,8},{13,9},{14,12},{15,13},... | collective-permute-start | bytes 393224 | tf_op jit(solution)/shard_map/ppermute | solution.py:419
  104.6 6.4 %collective-permute-start.28 = (bf16[64,1024]{1,0:T(8,128)(2,1)S(1)}, bf16[64,1024]{1,0:T(8,128)(2,1)S(1)}, u32[]{:S(2)}, u32[]{:S(2)}) collective-permute-start(bf16[64,1024]{1,0:T(8,128)(2,1)S(1)} %get-tuple-element.77), channel_id=1, source_target_pairs={{0,4},{1,5},{4,8},{5,9},{8,12},{9,13},{12,14},{13,15},{14,10},{15,... | collective-permute-start | bytes 393224 | tf_op jit(solution)/shard_map/ppermute | solution.py:419
  107.1 6.7 %collective-permute-start.18 = (bf16[64,1024]{1,0:T(8,128)(2,1)S(1)}, bf16[64,1024]{1,0:T(8,128)(2,1)S(1)}, u32[]{:S(2)}, u32[]{:S(2)}) collective-permute-start(bf16[64,1024]{1,0:T(8,128)(2,1)S(1)} %get-tuple-element.67), channel_id=1, source_target_pairs={{0,2},{1,3},{4,0},{5,1},{8,4},{9,5},{12,8},{13,9},{14,12},{15,13},... | collective-permute-start | bytes 393224 | tf_op jit(solution)/shard_map/ppermute | solution.py:419
  107.2 6.6 %collective-permute-start.19 = (bf16[64,1024]{1,0:T(8,128)(2,1)S(1)}, bf16[64,1024]{1,0:T(8,128)(2,1)S(1)}, u32[]{:S(2)}, u32[]{:S(2)}) collective-permute-start(bf16[64,1024]{1,0:T(8,128)(2,1)S(1)} %get-tuple-element.68), channel_id=1, source_target_pairs={{0,4},{1,5},{4,8},{5,9},{8,12},{9,13},{12,14},{13,15},{14,10},{15,... | collective-permute-start | bytes 393224 | tf_op jit(solution)/shard_map/ppermute | solution.py:419
  111.7 9.3 %collective-permute-start.29 = (bf16[128,1024]{1,0:T(8,128)(2,1)S(1)}, bf16[128,1024]{1,0:T(8,128)(2,1)S(1)}, u32[]{:S(2)}, u32[]{:S(2)}) collective-permute-start(bf16[128,1024]{1,0:T(8,128)(2,1)S(1)} %get-tuple-element.78), channel_id=1, source_target_pairs={{0,2},{1,3},{4,0},{5,1},{8,4},{9,5},{12,8},{13,9},{14,12},{15,13},... | collective-permute-start | bytes 786440 | tf_op jit(solution)/shard_map/ppermute | solution.py:419
  111.8 9.3 %collective-permute-start.30 = (bf16[128,1024]{1,0:T(8,128)(2,1)S(1)}, bf16[128,1024]{1,0:T(8,128)(2,1)S(1)}, u32[]{:S(2)}, u32[]{:S(2)}) collective-permute-start(bf16[128,1024]{1,0:T(8,128)(2,1)S(1)} %get-tuple-element.79), channel_id=1, source_target_pairs={{0,4},{1,5},{4,8},{5,9},{8,12},{9,13},{12,14},{13,15},{14,10},{15,... | collective-permute-start | bytes 786440 | tf_op jit(solution)/shard_map/ppermute | solution.py:419
  114.5 12.1 %collective-permute-start.20 = (bf16[128,1024]{1,0:T(8,128)(2,1)S(1)}, bf16[128,1024]{1,0:T(8,128)(2,1)S(1)}, u32[]{:S(2)}, u32[]{:S(2)}) collective-permute-start(bf16[128,1024]{1,0:T(8,128)(2,1)S(1)} %get-tuple-element.69), channel_id=1, source_target_pairs={{0,2},{1,3},{4,0},{5,1},{8,4},{9,5},{12,8},{13,9},{14,12},{15,13},... | collective-permute-start | bytes 786440 | tf_op jit(solution)/shard_map/ppermute | solution.py:419
  114.6 12.1 %collective-permute-start.21 = (bf16[128,1024]{1,0:T(8,128)(2,1)S(1)}, bf16[128,1024]{1,0:T(8,128)(2,1)S(1)}, u32[]{:S(2)}, u32[]{:S(2)}) collective-permute-start(bf16[128,1024]{1,0:T(8,128)(2,1)S(1)} %get-tuple-element.70), channel_id=1, source_target_pairs={{0,4},{1,5},{4,8},{5,9},{8,12},{9,13},{12,14},{13,15},{14,10},{15,... | collective-permute-start | bytes 786440 | tf_op jit(solution)/shard_map/ppermute | solution.py:419
  121.8 10.5 %collective-permute-start.31 = (bf16[128,1024]{1,0:T(8,128)(2,1)S(1)}, bf16[128,1024]{1,0:T(8,128)(2,1)S(1)}, u32[]{:S(2)}, u32[]{:S(2)}) collective-permute-start(bf16[128,1024]{1,0:T(8,128)(2,1)S(1)} %get-tuple-element.80), channel_id=1, source_target_pairs={{0,2},{1,3},{4,0},{5,1},{8,4},{9,5},{12,8},{13,9},{14,12},{15,13},... | collective-permute-start | bytes 786440 | tf_op jit(solution)/shard_map/ppermute | solution.py:419
  121.9 10.5 %collective-permute-start.32 = (bf16[128,1024]{1,0:T(8,128)(2,1)S(1)}, bf16[128,1024]{1,0:T(8,128)(2,1)S(1)}, u32[]{:S(2)}, u32[]{:S(2)}) collective-permute-start(bf16[128,1024]{1,0:T(8,128)(2,1)S(1)} %get-tuple-element.81), channel_id=1, source_target_pairs={{0,4},{1,5},{4,8},{5,9},{8,12},{9,13},{12,14},{13,15},{14,10},{15,... | collective-permute-start | bytes 786440 | tf_op jit(solution)/shard_map/ppermute | solution.py:419
  127.4 10.5 %collective-permute-start.22 = (bf16[128,1024]{1,0:T(8,128)(2,1)S(1)}, bf16[128,1024]{1,0:T(8,128)(2,1)S(1)}, u32[]{:S(2)}, u32[]{:S(2)}) collective-permute-start(bf16[128,1024]{1,0:T(8,128)(2,1)S(1)} %get-tuple-element.71), channel_id=1, source_target_pairs={{0,2},{1,3},{4,0},{5,1},{8,4},{9,5},{12,8},{13,9},{14,12},{15,13},... | collective-permute-start | bytes 786440 | tf_op jit(solution)/shard_map/ppermute | solution.py:419
  127.5 10.5 %collective-permute-start.23 = (bf16[128,1024]{1,0:T(8,128)(2,1)S(1)}, bf16[128,1024]{1,0:T(8,128)(2,1)S(1)}, u32[]{:S(2)}, u32[]{:S(2)}) collective-permute-start(bf16[128,1024]{1,0:T(8,128)(2,1)S(1)} %get-tuple-element.72), channel_id=1, source_target_pairs={{0,4},{1,5},{4,8},{5,9},{8,12},{9,13},{12,14},{13,15},{14,10},{15,... | collective-permute-start | bytes 786440 | tf_op jit(solution)/shard_map/ppermute | solution.py:419
  133.0 10.5 %collective-permute-start.33 = (bf16[128,1024]{1,0:T(8,128)(2,1)S(1)}, bf16[128,1024]{1,0:T(8,128)(2,1)S(1)}, u32[]{:S(2)}, u32[]{:S(2)}) collective-permute-start(bf16[128,1024]{1,0:T(8,128)(2,1)S(1)} %get-tuple-element.82), channel_id=1, source_target_pairs={{0,2},{1,3},{4,0},{5,1},{8,4},{9,5},{12,8},{13,9},{14,12},{15,13},... | collective-permute-start | bytes 786440 | tf_op jit(solution)/shard_map/ppermute | solution.py:419
  133.1 10.5 %collective-permute-start.34 = (bf16[128,1024]{1,0:T(8,128)(2,1)S(1)}, bf16[128,1024]{1,0:T(8,128)(2,1)S(1)}, u32[]{:S(2)}, u32[]{:S(2)}) collective-permute-start(bf16[128,1024]{1,0:T(8,128)(2,1)S(1)} %get-tuple-element.83), channel_id=1, source_target_pairs={{0,4},{1,5},{4,8},{5,9},{8,12},{9,13},{12,14},{13,15},{14,10},{15,... | collective-permute-start | bytes 786440 | tf_op jit(solution)/shard_map/ppermute | solution.py:419
  138.6 8.4 %collective-permute-start.24 = (bf16[128,1024]{1,0:T(8,128)(2,1)S(1)}, bf16[128,1024]{1,0:T(8,128)(2,1)S(1)}, u32[]{:S(2)}, u32[]{:S(2)}) collective-permute-start(bf16[128,1024]{1,0:T(8,128)(2,1)S(1)} %get-tuple-element.73), channel_id=1, source_target_pairs={{0,2},{1,3},{4,0},{5,1},{8,4},{9,5},{12,8},{13,9},{14,12},{15,13},... | collective-permute-start | bytes 786440 | tf_op jit(solution)/shard_map/ppermute | solution.py:419
  138.7 8.5 %collective-permute-start.25 = (bf16[128,1024]{1,0:T(8,128)(2,1)S(1)}, bf16[128,1024]{1,0:T(8,128)(2,1)S(1)}, u32[]{:S(2)}, u32[]{:S(2)}) collective-permute-start(bf16[128,1024]{1,0:T(8,128)(2,1)S(1)} %get-tuple-element.74), channel_id=1, source_target_pairs={{0,4},{1,5},{4,8},{5,9},{8,12},{9,13},{12,14},{13,15},{14,10},{15,... | collective-permute-start | bytes 786440 | tf_op jit(solution)/shard_map/ppermute | solution.py:419

commit v2 on v1

v2 whole, which is shorter than its diff:
```python
import functools
import jax
import jax.numpy as jnp
import numpy as np
from jax import lax
from jax.experimental import pallas as pl
from jax.experimental.pallas import tpu as pltpu
from jax.sharding import PartitionSpec as P

FF = 384
NS = 4


DAMPING = 0.01
EPSILON = 1e-06


def decode(mask_code):
    first_row = (mask_code <= 2).astype(jnp.float32)
    second_row = ((mask_code == 0) | (mask_code == 3) | (mask_code == 4)).astype(jnp.float32)
    third_row = ((mask_code == 1) | (mask_code == 3) | (mask_code == 5)).astype(jnp.float32)
    fourth_row = ((mask_code == 2) | (mask_code == 4) | (mask_code == 5)).astype(jnp.float32)
    kept_mask = jnp.stack([first_row, second_row, third_row, fourth_row], axis=2)
    return kept_mask.reshape(mask_code.shape[0], mask_code.shape[1] * 4, mask_code.shape[2])


def precise_matmul(left, right):
    return jnp.einsum(
        "jab,jbc->jac",
        left,
        right,
        precision=lax.Precision.HIGHEST,
        preferred_element_type=jnp.float32,
    )


def routed(tokens, expert_ids, route_weights, gate_weight, up_weight, down_weight, mask_code):
    group_count = lax.axis_size(("expert", "mp"))
    experts_here, half_rows, model_width = gate_weight.shape
    tok_rows, top_count = expert_ids.shape
    experts_all = experts_here * group_count
    capacity = min(tok_rows, 5 * tok_rows * top_count // (4 * experts_all))
    slot_total = group_count * capacity
    flat_ids = expert_ids.reshape(-1)
    onehot = (flat_ids[:, None] == jnp.arange(experts_all, dtype=jnp.int32)[None, :]).astype(
        jnp.int32
    )
    slot_rank = jnp.sum((jnp.cumsum(onehot, axis=0) - onehot) * onehot, axis=1)
    local_expert = flat_ids % experts_here
    position = flat_ids // experts_here * capacity + slot_rank
    token_of = jnp.arange(tok_rows * top_count, dtype=jnp.int32) // top_count
    slot_token = (
        jnp.full((experts_here, slot_total), tok_rows, jnp.int32)
        .at[local_expert, position]
        .set(token_of)
    )
    full_rows = lax.all_gather(tokens, "section", axis=1, tiled=True)
    padded_rows = jnp.concatenate(
        [full_rows, jnp.zeros((1, full_rows.shape[1]), full_rows.dtype)], axis=0
    )
    send_rows = padded_rows[slot_token]
    slot_rows = lax.all_to_all(send_rows, ("expert", "mp"), split_axis=1, concat_axis=1, tiled=True)
    gate_pre = jnp.einsum(
        "jfd,jsd->jfs", gate_weight, slot_rows, preferred_element_type=jnp.float32
    )
    up_pre = jnp.einsum("jfd,jsd->jfs", up_weight, slot_rows, preferred_element_type=jnp.float32)
    hidden_half = (jax.nn.silu(gate_pre) * up_pre).astype(jnp.bfloat16)
    hidden_all = lax.all_gather(hidden_half, "section", axis=1, tiled=True)
    hidden_width = hidden_all.shape[1]
    gram_matrix = jnp.einsum(
        "jfs,jgs->jfg", hidden_all, hidden_all, preferred_element_type=jnp.float32
    )
    mean_diag = jnp.mean(jnp.diagonal(gram_matrix, axis1=1, axis2=2), axis=1)
    identity = jnp.eye(hidden_width, dtype=jnp.float32)
    hessian = gram_matrix + (DAMPING * mean_diag + EPSILON)[:, None, None] * identity
    step_size = 1.0 / jnp.max(jnp.sum(jnp.abs(hessian), axis=2), axis=1)
    iterate = (
        2.0 * step_size[:, None, None] * identity - (step_size * step_size)[:, None, None] * hessian
    )
    for iteration in range(NS - 1):
        iterate = 2.0 * iterate - precise_matmul(precise_matmul(iterate, hessian), iterate)
    kept_mask = decode(mask_code)
    weight_wide = down_weight.astype(jnp.float32)
    inverse_diag = jnp.diagonal(iterate, axis1=1, axis2=2)
    scaled_error = weight_wide * (1.0 - kept_mask) / inverse_diag[:, :, None]
    correction = precise_matmul(iterate, scaled_error)
    pruned = (kept_mask * (weight_wide - correction)).astype(jnp.bfloat16)
    expert_out = (
        jnp.einsum("jfs,jfd->jsd", hidden_all, pruned, preferred_element_type=jnp.float32)
        * FF ** (-0.5)
    ).astype(jnp.bfloat16)
    returned = lax.all_to_all(expert_out, ("expert", "mp"), split_axis=1, concat_axis=1, tiled=True)
    picked = returned[local_expert, position].reshape(tok_rows, top_count, -1)
    combined = jnp.einsum("tkd,tk->td", picked.astype(jnp.float32), route_weights)
    return (combined.astype(jnp.bfloat16), pruned)


AXES = ("expert", "mp")
CHUNK = 128
EXTRA = 8
BF = jnp.bfloat16
F32 = jnp.float32


def params(*semantics, mib=16):
    return pltpu.CompilerParams(
        dimension_semantics=semantics or None, vmem_limit_bytes=mib * 1024 * 1024
    )


def whole(shape):
    return pl.BlockSpec(shape, lambda *_: (0,) * len(shape))


def dot(left, right, on=((1,), (0,))):
    return lax.dot_general(left, right, (on, ((), ())), preferred_element_type=F32)


def split_kernel(experts_all, x_ref, ids_ref, weight_ref, *out_refs):
    half = x_ref.shape[0] // 2
    ids, weight = ids_ref[...], weight_ref[...]
    table = [
        jnp.max(jnp.where(ids == e, weight, -1.0), axis=0, keepdims=True)
        for e in range(experts_all)
    ]
    table = jnp.concatenate(table, axis=0)
    high = table.astype(BF).astype(F32)
    both = jnp.concatenate([high, table - high], axis=0)
    parts = [both[i : i + EXTRA] for i in range(0, 2 * experts_all, EXTRA)]
    lanes = both.shape[1]
    rest = x_ref.shape[1] - len(parts) * lanes
    extra = jnp.concatenate(parts + [jnp.zeros((EXTRA, rest), F32)], axis=1).astype(BF)
    for at, (wide, plain) in enumerate(((out_refs[0], out_refs[3]), (out_refs[1], out_refs[2]))):
        value = x_ref[at * half : (at + 1) * half, :]
        wide[:half, :] = value
        wide[half:, :] = extra
        plain[...] = value


def split(tokens, expert_ids, route_weights, experts_all):
    rows, width = tokens.shape
    wide = jax.ShapeDtypeStruct((rows // 2 + EXTRA, width), BF)
    plain = jax.ShapeDtypeStruct((rows // 2, width), BF)
    given = (tokens, expert_ids.T, route_weights.T)
    return pl.pallas_call(
        functools.partial(split_kernel, experts_all),
        out_shape=[wide, wide, plain, plain],
        grid=(1,),
        in_specs=[whole(g.shape) for g in given],
        out_specs=[whole(o.shape) for o in (wide, wide, plain, plain)],
        compiler_params=params("arbitrary", mib=56),
        name="split",
    )(*given)


def token_weights(ref, experts_all, expert):
    half, lanes = ref.shape[0] - EXTRA, 2 * (ref.shape[0] - EXTRA)
    count = 2 * experts_all // EXTRA
    parts = [ref[half:, i * lanes : (i + 1) * lanes].astype(F32) for i in range(count)]
    both = jnp.concatenate(parts, axis=0)
    table = both[:experts_all] + both[experts_all:]
    row = lax.broadcasted_iota(jnp.int32, table.shape, 0)
    return jnp.sum(jnp.where(row == expert, table, 0.0), axis=0, keepdims=True)


def mask_kernel(code_ref, down_ref, kept_ref, error_ref):
    rows, groups = down_ref.shape[0], code_ref.shape[0]
    code = code_ref[...]
    first = code <= 2
    second = (code == 0) | (code == 3) | (code == 4)
    third = (code == 1) | (code == 3) | (code == 5)
    fourth = (code == 2) | (code == 4) | (code == 5)
    planes = [jnp.where(plane, 1.0, 0.0).astype(BF) for plane in (first, second, third, fourth)]
    row = lax.broadcasted_iota(jnp.int32, (rows, rows), 0)
    column = lax.broadcasted_iota(jnp.int32, (rows, rows), 1)
    spread = jnp.where(row % 4 * groups + row // 4 == column, 1.0, 0.0).astype(BF)
    kept = dot(spread, jnp.concatenate(planes, axis=0))
    kept_ref[...] = kept.astype(BF)
    error_ref[...] = jnp.where(kept > 0.5, 0.0, down_ref[...].astype(F32)).astype(BF)


def masks(code, down):
    groups, width = code.shape
    rows = down.shape[0]
    cut = 512
    spec = pl.BlockSpec((rows, cut), lambda i: (0, i))
    return pl.pallas_call(
        mask_kernel,
        out_shape=[jax.ShapeDtypeStruct((rows, width), BF)] * 2,
        grid=(width // cut,),
        in_specs=[pl.BlockSpec((groups, cut), lambda i: (0, i)), spec],
        out_specs=[spec, spec],
        compiler_params=params("arbitrary"),
        cost_estimate=pl.CostEstimate(
            flops=2 * rows * rows * width, bytes_accessed=8 * rows * width, transcendentals=0
        ),
        name="masks",
    )(code, down)


def hidden_kernel(pieces, sources, experts, experts_all, has_gram, place_ref, *refs):
    count = len(experts)
    x_refs, refs = refs[:pieces], refs[pieces:]
    pairs, grams_in = refs[: 2 * count], refs[2 * count : 3 * count]
    out_ref, gram_refs, rows_ref, weight_ref, hidden_ref = (
        refs[-4 - count],
        refs[-3 - count : -3],
        *refs[-3:],
    )
    steps = pl.num_programs(0) // count

    def work(which, step):
        @pl.when(step == 0)
        def _():
            half = min(x.shape[0] for x in x_refs)
            half = half - half % 16
            if which == 0:
                for at, x in enumerate(x_refs):
                    rows_ref[at * half : (at + 1) * half, :] = x[:half, :]
            expert = place_ref[experts[which]]
            weight = [token_weights(x_refs[i], experts_all, expert) for i in sources]
            tok_rows = weight[0].shape[1]
            empty = jnp.zeros((8 - len(sources), tok_rows), F32)
            weight = jnp.concatenate(weight + [empty], axis=0).T
            for at in range(len(sources)):
                weight_ref[at * tok_rows : (at + 1) * tok_rows, :] = jnp.broadcast_to(
                    weight[:, at : at + 1], (tok_rows, CHUNK)
                )

        at = pl.ds(pl.multiple_of(step * CHUNK, CHUNK), CHUNK)
        gate_ref, up_ref = pairs[2 * which], pairs[2 * which + 1]
        both = jnp.concatenate([gate_ref[at, :], up_ref[at, :]], axis=0)
        pre = dot(rows_ref[...], both, ((1,), (1,)))
        gate, up = pre[:, :CHUNK], pre[:, CHUNK:]
        weight = weight_ref[...]
        value = gate / (1.0 + jnp.exp(-gate)) * up
        value = jnp.where(weight >= 0.0, value, 0.0).astype(BF)
        hidden_ref[:, at] = value
        out_ref[...] = (value.astype(F32) * (weight * FF ** (-0.5))).astype(BF)

        @pl.when(step == steps - 1)
        def _():
            hidden = hidden_ref[...]
            gram = dot(hidden, hidden, ((0,), (0,)))
            gram_refs[which][...] = grams_in[which][...] + gram if has_gram else gram

    step = pl.program_id(0)
    if count == 1:
        work(0, step)
    else:
        for which in range(count):
            pl.when(step // steps == which)(functools.partial(work, which, step - which * steps))


def hidden_part(place, experts, experts_all, pieces, sources, pairs, grams):
    half = min(p.shape[0] for p in pieces)
    rows = len(pieces) * (half - half % 16)
    ff, width = pairs[0][0].shape
    count = len(experts)
    resident = pl.BlockSpec(memory_space=pltpu.VMEM)
    given = [*pieces] + [w for pair in pairs for w in pair] + [*grams]
    specs = [resident] * (len(pieces) + 2 * count + len(grams))
    return pl.pallas_call(
        functools.partial(
            hidden_kernel, len(pieces), sources, experts, experts_all, len(grams) > 0
        ),
        out_shape=[jax.ShapeDtypeStruct((rows, count * ff), BF)]
        + [jax.ShapeDtypeStruct((ff, ff), F32)] * count,
        grid_spec=pltpu.PrefetchScalarGridSpec(
            num_scalar_prefetch=1,
            grid=(count * ff // CHUNK,),
            in_specs=specs,
            out_specs=[pl.BlockSpec((rows, CHUNK), lambda i, _: (0, i))]
            + [whole((ff, ff))] * count,
            scratch_shapes=[
                pltpu.VMEM((rows, width), BF),
                pltpu.VMEM((rows, CHUNK), F32),
                pltpu.VMEM((rows, ff), BF),
            ],
        ),
        compiler_params=params("arbitrary"),
        cost_estimate=pl.CostEstimate(
            flops=4 * rows * ff * width * count,
            bytes_accessed=2 * (rows + 2 * ff * count) * width,
            transcendentals=rows * ff * count,
        ),
        name="hidden",
    )(place, *given)


def product(left, right):
    return dot(left.astype(BF), right)


def prune_kernel(own_ref, other_ref, error_ref, down_ref, kept_ref, out_ref, inverse_ref):
    gram = own_ref[...] + other_ref[...]
    size = gram.shape[0]
    row = lax.broadcasted_iota(jnp.int32, (size, size), 0)
    column = lax.broadcasted_iota(jnp.int32, (size, size), 1)
    eye = row == column
    mean_diag = jnp.sum(jnp.where(eye, gram, 0.0)) * (1.0 / size)
    hessian = gram + jnp.where(eye, DAMPING * mean_diag + EPSILON, 0.0)
    step_size = 1.0 / jnp.max(jnp.sum(jnp.abs(hessian), axis=0, keepdims=True))
    scaled = step_size * hessian
    iterate = jnp.where(eye, 2.0, 0.0) - scaled
    right = scaled.astype(BF)
    scaled = 2.0 * scaled - dot(right, right)
    for iteration in range(NS - 1):
        right = scaled.astype(BF)
        following = 2.0 * iterate - product(iterate, right)
        if iteration < NS - 2:
            scaled = 2.0 * scaled - dot(right, right)
        iterate = following
    diag = jnp.sum(jnp.where(eye, iterate, 0.0), axis=0, keepdims=True)
    inverse_ref[...] = (iterate * (1.0 / diag)).astype(BF)
    correct_kernel(inverse_ref, error_ref, down_ref, kept_ref, out_ref)


def correct_kernel(inverse_ref, error_ref, down_ref, kept_ref, out_ref):
    correction = dot(inverse_ref[...], error_ref[...])
    value = kept_ref[...].astype(F32) * (down_ref[...].astype(F32) - correction)
    out_ref[...] = value.astype(BF)


def prune_cost(size, cut, products):
    return pl.CostEstimate(
        flops=2 * size * size * (cut + products * size),
        bytes_accessed=8 * size * cut + 8 * size * size,
        transcendentals=0,
    )


def prune_first(own, other, error, down, kept, cut):
    size = own.shape[0]
    half = pl.BlockSpec((size, cut), lambda i: (0, 0))
    square = whole((size, size))
    return pl.pallas_call(
        prune_kernel,
        out_shape=[
            jax.ShapeDtypeStruct((size, cut), BF),
            jax.ShapeDtypeStruct((size, size), BF),
        ],
        grid=(1,),
        in_specs=[square, square, half, half, half],
        out_specs=[half, square],
        compiler_params=params("arbitrary"),
        cost_estimate=prune_cost(size, cut, 6),
        name="prune",
    )(own, other, error, down, kept)


def prune_next(inverse, error, down, kept, cut, at):
    size = inverse.shape[0]
    half = pl.BlockSpec((size, cut), lambda i: (0, at))
    return pl.pallas_call(
        correct_kernel,
        out_shape=jax.ShapeDtypeStruct((size, cut), BF),
        grid=(1,),
        in_specs=[whole((size, size)), half, half, half],
        out_specs=whole((size, cut)),
        compiler_params=params("arbitrary"),
        cost_estimate=prune_cost(size, cut, 0),
        name="prune_next",
    )(inverse, error, down, kept)


def stage_kernel(*refs):
    count = len(refs) // 2
    for given, out in zip(refs[:count], refs[count:]):
        out[...] = given[...]


def stage(arrays):
    rows, width = arrays[0].shape
    spec = pl.BlockSpec((CHUNK, width), lambda i: (i, 0))
    return pl.pallas_call(
        stage_kernel,
        out_shape=[jax.ShapeDtypeStruct(a.shape, a.dtype) for a in arrays],
        grid=(rows // CHUNK,),
        in_specs=[spec] * len(arrays),
        out_specs=[spec] * len(arrays),
        compiler_params=params("arbitrary"),
        name="stage",
    )(*arrays)


def tied(values):
    return lax.optimization_barrier(values)


def outputs_kernel(block, arrived, own_hidden, other_hidden, own_ref, other_ref, *refs):
    total = dot(own_hidden[...], own_ref[...]) + dot(other_hidden[...], other_ref[...])
    first, second = total[:block], total[block:]
    if arrived:
        size = refs[0].shape[0]
        from_right, from_left = refs[0][...].astype(F32), refs[1][...].astype(F32)
        if size < block:
            empty = jnp.zeros((block - size, total.shape[1]), F32)
            from_left = jnp.concatenate([from_left, empty], axis=0)
            from_right = jnp.concatenate([empty, from_right], axis=0)
        first, second = first + from_right, second + from_left
    refs[-2][...] = first.astype(BF)
    refs[-1][...] = second.astype(BF)


def column_specs(hidden, rows, ff):
    return [pl.BlockSpec((rows, ff), lambda i, at=at: (0, at)) for _, at in hidden]


def outputs(hidden, own, other, arrived):
    rows = hidden[0][0].shape[0]
    ff, cut = own.shape
    given = (hidden[0][0], hidden[1][0], own, other) + arrived
    return pl.pallas_call(
        functools.partial(outputs_kernel, rows // 2, len(arrived)),
        out_shape=[jax.ShapeDtypeStruct((rows // 2, cut), BF)] * 2,
        grid=(1,),
        in_specs=column_specs(hidden, rows, ff) + [whole(g.shape) for g in given[2:]],
        out_specs=[whole((rows // 2, cut))] * 2,
        compiler_params=params("arbitrary"),
        cost_estimate=pl.CostEstimate(
            flops=4 * rows * own.shape[0] * cut,
            bytes_accessed=sum(g.size * 2 for g in given) + rows * cut * 2,
            transcendentals=0,
        ),
        name="outputs",
    )(*given)


def self_kernel(own_hidden, other_hidden, own_ref, other_ref, out_ref):
    out_ref[...] = dot(own_hidden[...], own_ref[...]) + dot(other_hidden[...], other_ref[...])


def self_outputs(hidden, own, other):
    rows, ff, cut = hidden[0][0].shape[0], *own.shape
    given = (hidden[0][0], hidden[1][0], own, other)
    return pl.pallas_call(
        self_kernel,
        out_shape=jax.ShapeDtypeStruct((rows, cut), F32),
        grid=(1,),
        in_specs=column_specs(hidden, rows, ff) + [whole(own.shape)] * 2,
        out_specs=whole((rows, cut)),
        compiler_params=params("arbitrary"),
        name="self_outputs",
    )(*given)


def finish_kernel(own_ref, right_ref, left_ref, *refs):
    total = own_ref[...] + right_ref[...].astype(F32) + left_ref[...].astype(F32)
    refs[-1][...] = total.astype(BF)


def finish(own, right, left, width, at, result):
    rows, cut = own.shape
    given = (own, right, left) + (() if result is None else (result,))
    return pl.pallas_call(
        finish_kernel,
        out_shape=jax.ShapeDtypeStruct((rows, width), BF),
        grid=(1,),
        in_specs=[whole((rows, cut))] * 3
        + ([] if result is None else [pl.BlockSpec(memory_space=pl.ANY)]),
        out_specs=pl.BlockSpec((rows, cut), lambda i: (0, at)),
        input_output_aliases={} if result is None else {3: 0},
        compiler_params=params("arbitrary"),
        name="finish",
    )(*given)


def ring_of(expert_size, mp_size):
    chips = mp_size // 2
    order = [(z, 0) for z in range(expert_size)]
    for z in reversed(range(expert_size)):
        side = list(range(1, chips)) if (expert_size - 1 - z) % 2 == 0 else list(range(chips - 1, 0, -1))
        order += [(z, x) for x in side]
    return [z * mp_size + 2 * x for z, x in order]


def dense(expert_size, mp_size, tokens, expert_ids, route_weights, gate, up, down, code):
    gate, up, down, code = gate[0], up[0], down[0], code[0]
    tok_rows, width = tokens.shape
    devices = expert_size * mp_size
    ring = ring_of(expert_size, mp_size)
    length = len(ring)
    reach = length // 2
    here = lax.axis_index(AXES)

    def shift(value, by):
        pairs = [
            (ring[i] + c, ring[(i + by) % length] + c) for i in range(length) for c in range(2)
        ]
        return lax.ppermute(value, AXES, pairs)

    def swap(value):
        return lax.ppermute(value, AXES, [(i, i ^ 1) for i in range(devices)])

    place = jnp.stack([here, here ^ 1]).astype(jnp.int32)
    top_wide, bottom_wide, bottom, top = split(tokens, expert_ids, route_weights, devices)
    right, left = [top_wide, bottom], [top, bottom_wide]
    groups = [((top_wide, bottom), (0,))]

    def hop_first(hop):
        right[0], left[1] = shift(right[0], 1), shift(left[1], -1)
        if hop == reach:
            groups.append(((right[0], left[1]), (0,)))

    def hop_second(hop):
        right[1], left[0] = shift(right[1], 1), shift(left[0], -1)
        groups.append(((*right, *left), (0, 3)))

    pairs = [(gate, up), (swap(gate), swap(up))]
    grams = []
    hidden = []

    def work(hop):
        value, *after = hidden_part(place, (0, 1), devices, *groups[hop], pairs, grams)
        grams[:] = after
        hidden.append(((value, 0), (value, 1)))

    hop_first(1)
    kept, error = masks(code, down)
    right[1], left[0], kept, error = tied((right[1], left[0], kept, error))
    hop_second(1)
    hop_first(2)
    pairs[1] = stage(pairs[1])
    work(0)
    right[1], left[0], *grams = tied((right[1], left[0], *grams))
    hop_second(2)
    for hop in range(3, reach + 1):
        work(hop - 2)
        right[0], left[1], *grams = tied((right[0], left[1], *grams))
        hop_first(hop)
        if hop < reach:
            hop_second(hop)
    work(reach - 1)
    grams = list(tied(tuple(grams)))
    last_other, gram_other = hidden_part(
        place, (1,), devices, *groups[reach], pairs[1:], grams[1:]
    )
    gram_other = swap(gram_other)
    last_own, gram_own = hidden_part(place, (0,), devices, *groups[reach], pairs[:1], grams[:1])
    hidden.append(((last_own, 0), (last_other, 0)))
    cut = width // 2
    pruned = [None, None]
    pruned[0], inverse = prune_first(gram_own, gram_other, error, down, kept, cut)
    pruned_other = [swap(pruned[0]), None]
    pruned[1] = prune_next(inverse, error, down, kept, cut, 1)
    pruned_other[1] = swap(pruned[1])

    moving = [(), ()]
    for hop in range(reach, 0, -1):
        for at in range(2):
            sent = outputs(hidden[hop], pruned[at], pruned_other[at], moving[at])
            go_left, go_right = sent if hop < reach else (sent[1], sent[0])
            moving[at] = (shift(go_left, -1), shift(go_right, 1))
    mixed = None
    for at in range(2):
        own = self_outputs(hidden[0], pruned[at], pruned_other[at])
        mixed = finish(own, *moving[at], width, at, mixed)
    return mixed, jnp.concatenate(pruned, axis=1)[None]


def local(expert_size, mp_size, section_size, *given):
    tokens, expert_ids, _, gate_weight = given[:4]
    devices = expert_size * mp_size
    if (
        section_size == 1
        and gate_weight.shape[0] == 1
        and 2 * expert_ids.shape[1] >= devices
        and mp_size % 2 == 0
        and devices >= 16
        and devices % EXTRA == 0
        and expert_ids.shape[0] == 128
        and 2 * devices * 128 <= EXTRA * tokens.shape[1]
    ):
        return dense(expert_size, mp_size, *given)
    return routed(*given)


def solution(mesh):
    placed = (
        P(("groups", "expert", "mp"), "section"),
        P(("groups", "expert", "mp"), None),
        P(("groups", "expert", "mp"), None),
        P(("expert", "mp"), "section", None),
        P(("expert", "mp"), "section", None),
        P(("expert", "mp"), None, "section"),
        P(("expert", "mp"), None, "section"),
    )
    sizes = mesh.shape
    return jax.shard_map(
        functools.partial(local, sizes["expert"], sizes["mp"], sizes["section"]),
        mesh=mesh,
        in_specs=placed,
        out_specs=(
            P(("groups", "expert", "mp"), "section"),
            P(("groups", "expert", "mp"), None, "section"),
        ),
        check_vma=False,
    )
```

time: 148 us -> 113 us (0.76)
  blocking collectives: 21 us -> 0 us
  waiting for transfers between devices: 35.2 us -> 27.4 us
  starting transfers between devices: 37.8 us -> 35 us
  between operations: 2.88 us -> 0.93 us
  other arithmetic: 2.88 us -> 1.35 us
    all_gather x1 -> x0, blocking collectives: 21 us -> none  [dense(): table = lax.all_gather(table, AXES, axis=0, tiled=True)]
    ppermute x30, waiting for transfers between devices: 34.4 us -> 26.2 us  [shift(): return lax.ppermute(value, AXES, pairs)]
    pallas_call x11 -> x8, Pallas kernels: 26.5 us -> 31.2 us  [the longest x6 26.2 us: hidden_part(): pl.pallas_call(functools.partial(hidden_kernel, len(pieces), sources, exp...]
    pallas_call x1, Pallas kernels: 5.64 us -> 2.57 us  [prune_first(): pl.pallas_call(prune_kernel, out_shape=[jax.ShapeDtypeStruct((size, cut),...]
    ppermute x30, starting transfers between devices: 36.5 us -> 33.7 us  [shift(): return lax.ppermute(value, AXES, pairs)]
    unnamed x12, local copies, waits for them, and re-layouts: 1.07 us -> 3.51 us
    pallas_call x1, Pallas kernels: 4.23 us -> 2.37 us  [masks(): pl.pallas_call(mask_kernel, out_shape=[jax.ShapeDtypeStruct((rows, width)...]
  transfers between devices with their start and end apart: 35 -> 35, of which waited for: 20 -> 19; matrix products, arithmetic and copies ran while one was open for 4% -> 1% of each run, Pallas kernels for 25% -> 34%
where the time goes in v2:
time: 113 us
  Pallas kernels  44.4 us (39%)
  starting transfers between devices  35 us (31%)
  waiting for transfers between devices  27.4 us (24%)
  local copies, waits for them, and re-layouts  3.51 us (3%)
  other arithmetic  1.35 us (1%)
    ppermute x30, starting transfers between devices, shift(): return lax.ppermute(value, AXES, pairs)  33.7 us
    pallas_call x6, Pallas kernels, hidden_part(): pl.pallas_call(functools.partial(hidden_kernel, len(pieces), sources, exp...  26.2 us
    ppermute x30, waiting for transfers between devices, shift(): return lax.ppermute(value, AXES, pairs)  26.2 us
    pallas_call x8, Pallas kernels, outputs(): pl.pallas_call(functools.partial(outputs_kernel, rows // 2, len(arrived))...  5.16 us
    unnamed x12, local copies, waits for them, and re-layouts  3.51 us
    pallas_call x1, Pallas kernels, stage(): pl.pallas_call(stage_kernel, out_shape=[jax.ShapeDtypeStruct(a.shape, a.d...  2.91 us
    pallas_call x1, Pallas kernels, prune_first(): pl.pallas_call(prune_kernel, out_shape=[jax.ShapeDtypeStruct((size, cut),...  2.57 us
    pallas_call x1, Pallas kernels, masks(): pl.pallas_call(mask_kernel, out_shape=[jax.ShapeDtypeStruct((rows, width)...  2.37 us
  transfers between devices with their start and end apart: 35, of which 19 were waited for; matrix products, arithmetic and copies ran while one was open for 1% of the time, Pallas kernels for 34%

profile of v2, /device:TPU:0, one launch (start us, length us, event | category | flops | bytes accessed | tf_op | source)
XLA Modules:
  0.0 112.7 jit_solution(1289285595291860240)
XLA Ops:
  0.6 0.5 collective-permute-start
  1.2 2.1 %split.1 = (bf16[72,2048]{1,0:T(8,128)(2,1)}, bf16[72,2048]{1,0:T(8,128)(2,1)}, bf16[64,2048]{1,0:T(8,128)(2,1)}, bf16[64,2048]{1,0:T(8,128)(2,1)}) custom-call(bf16[128,2048]{1,0:T(8,128)(2,1)} %x_ref.1, s32[8,128]{1,0:T(8,128)} %bitcast.26, f32[8,128]{1,0:T(8,128)} %bitcast.27), custom_call_target="tpu_custom_call" | custom-call | tf_op jit(solution)/shard_map/split/pallas_call | solution.py:145
  3.3 3.0 %collective-permute-start.2 = (bf16[72,2048]{1,0:T(8,128)(2,1)}, bf16[72,2048]{1,0:T(8,128)(2,1)S(1)}, u32[]{:S(2)}, u32[]{:S(2)}) collective-permute-start(bf16[72,2048]{1,0:T(8,128)(2,1)} %get-tuple-element.62.refs_0_), channel_id=1, source_target_pairs={{0,4},{1,5},{4,8},{5,9},{8,12},{9,13},{12,14},{13,15},{14,10},{15,... | collective-permute-start | bytes 884744 | tf_op jit(solution)/shard_map/ppermute | solution.py:491
  6.3 1.4 %copy-done.2 = bf16[1,384,2048]{2,1,0:T(8,128)(2,1)S(1)} copy-done((bf16[1,384,2048]{2,1,0:T(8,128)(2,1)S(1)}, bf16[1,384,2048]{2,1,0:T(8,128)(2,1)}, u32[]{:S(2)}) %copy-start.2) | copy-done | bytes 1572888
  7.8 1.1 %copy-done.4 = s32[1,96,2048]{2,1,0:T(8,128)S(1)} copy-done((s32[1,96,2048]{2,1,0:T(8,128)S(1)}, s32[1,96,2048]{2,1,0:T(8,128)}, u32[]{:S(2)}) %copy-start.4) | copy-done | bytes 786456
  8.9 2.4 %masks.1 = (bf16[384,2048]{1,0:T(8,128)(2,1)S(1)}, bf16[384,2048]{1,0:T(8,128)(2,1)S(1)}) custom-call(s32[96,2048]{1,0:T(8,128)S(1)} %bitcast.25, bf16[384,2048]{1,0:T(8,128)(2,1)S(1)} %bitcast.22), custom_call_target="tpu_custom_call" | custom-call | flops 603979776 | bytes 6291456 | tf_op jit(solution)/shard_map/masks/pallas_call | solution.py:187
  11.3 2.1 %collective-permute-start.6 = (bf16[64,2048]{1,0:T(8,128)(2,1)}, bf16[64,2048]{1,0:T(8,128)(2,1)}, u32[]{:S(2)}, u32[]{:S(2)}) collective-permute-start(bf16[64,2048]{1,0:T(8,128)(2,1)} %get-tuple-element.71.refs_1_), channel_id=1, source_target_pairs={{0,4},{1,5},{4,8},{5,9},{8,12},{9,13},{12,14},{13,15},{14,10},{15,... | collective-permute-start | bytes 786440 | tf_op jit(solution)/shard_map/ppermute | solution.py:491
  13.7 1.7 %collective-permute-start.7 = (bf16[64,2048]{1,0:T(8,128)(2,1)}, bf16[64,2048]{1,0:T(8,128)(2,1)}, u32[]{:S(2)}, u32[]{:S(2)}) collective-permute-start(bf16[64,2048]{1,0:T(8,128)(2,1)} %get-tuple-element.72), channel_id=1, source_target_pairs={{0,2},{1,3},{4,0},{5,1},{8,4},{9,5},{12,8},{13,9},{14,12},{15,13},... | collective-permute-start | bytes 786440 | tf_op jit(solution)/shard_map/ppermute | solution.py:491
  15.5 1.5 %collective-permute-start.3 = (bf16[72,2048]{1,0:T(8,128)(2,1)S(1)}, bf16[72,2048]{1,0:T(8,128)(2,1)S(1)}, u32[]{:S(2)}, u32[]{:S(2)}) collective-permute-start(bf16[72,2048]{1,0:T(8,128)(2,1)S(1)} %collective-permute-done.2.refs_0_), channel_id=1, source_target_pairs={{0,4},{1,5},{4,8},{5,9},{8,12},{9,13},{12,14},{13,15},{14,10},{15,... | collective-permute-start | bytes 884744 | tf_op jit(solution)/shard_map/ppermute | solution.py:491
  17.0 0.5 collective-permute-start.5
  17.6 2.9 %stage.1 = (bf16[384,2048]{1,0:T(8,128)(2,1)S(1)}, bf16[384,2048]{1,0:T(8,128)(2,1)S(1)}) custom-call(bf16[384,2048]{1,0:T(8,128)(2,1)} %collective-permute-done.refs_0_, bf16[384,2048]{1,0:T(8,128)(2,1)} %collective-permute-done.1.refs_1_), custom_call_target="tpu_custom_call" | custom-call | tf_op jit(solution)/shard_map/stage/pallas_call | solution.py:376
  20.5 1.0 copy-done.5
  21.5 5.6 %hidden.6 = (bf16[128,768]{1,0:T(8,128)(2,1)S(1)}, f32[384,384]{1,0:T(8,128)S(1)}, f32[384,384]{1,0:T(8,128)S(1)}) custom-call(s32[2]{0:T(128)S(1)} %pad_add_fusion.place_ref, bf16[72,2048]{1,0:T(8,128)(2,1)S(1)} %copy-done.5, bf16[64,2048]{1,0:T(8,128)(2,1)} %get-tuple-element.71.refs_1_, bf16[384,2048]{1,0:T(8,128)(2,1)S(1)} %bitcast.11, ...), custom_call_target="tpu_custom_call" | custom-call | flops 805306368 | bytes 6815744 | tf_op jit(solution)/shard_map/hidden/pallas_call | solution.py:263
  27.1 1.5 %collective-permute-start.10 = (bf16[64,2048]{1,0:T(8,128)(2,1)}, bf16[64,2048]{1,0:T(8,128)(2,1)S(1)}, u32[]{:S(2)}, u32[]{:S(2)}) collective-permute-start(bf16[64,2048]{1,0:T(8,128)(2,1)} %collective-permute-done.6.refs_1_), channel_id=1, source_target_pairs={{0,4},{1,5},{4,8},{5,9},{8,12},{9,13},{12,14},{13,15},{14,10},{15,... | collective-permute-start | bytes 786440 | tf_op jit(solution)/shard_map/ppermute | solution.py:491
  28.7 0.5 collective-permute-start.11
  29.2 5.9 %hidden.7 = (bf16[256,768]{1,0:T(8,128)(2,1)S(1)}, f32[384,384]{1,0:T(8,128)S(1)}, f32[384,384]{1,0:T(8,128)S(1)}) custom-call(s32[2]{0:T(128)S(1)} %pad_add_fusion.place_ref, bf16[72,2048]{1,0:T(8,128)(2,1)S(1)} %collective-permute-done.2.refs_0_, bf16[64,2048]{1,0:T(8,128)(2,1)} %collective-permute-done.6.refs_1_, ...), custom_call_target="tpu_custom_call" | custom-call | flops 1610612736 | bytes 7340032 | tf_op jit(solution)/shard_map/hidden/pallas_call | solution.py:263
  35.2 1.5 %collective-permute-start.8 = (bf16[72,2048]{1,0:T(8,128)(2,1)S(1)}, bf16[72,2048]{1,0:T(8,128)(2,1)S(1)}, u32[]{:S(2)}, u32[]{:S(2)}) collective-permute-start(bf16[72,2048]{1,0:T(8,128)(2,1)S(1)} %collective-permute-done.3.refs_0_), channel_id=1, source_target_pairs={{0,4},{1,5},{4,8},{5,9},{8,12},{9,13},{12,14},{13,15},{14,10},{15,... | collective-permute-start | bytes 884744 | tf_op jit(solution)/shard_map/ppermute | solution.py:491
  36.7 0.5 collective-permute-start.9
  37.2 1.5 %collective-permute-start.14 = (bf16[64,2048]{1,0:T(8,128)(2,1)S(1)}, bf16[64,2048]{1,0:T(8,128)(2,1)S(1)}, u32[]{:S(2)}, u32[]{:S(2)}) collective-permute-start(bf16[64,2048]{1,0:T(8,128)(2,1)S(1)} %collective-permute-done.10.refs_1_), channel_id=1, source_target_pairs={{0,4},{1,5},{4,8},{5,9},{8,12},{9,13},{12,14},{13,15},{14,10},{15,... | collective-permute-start | bytes 786440 | tf_op jit(solution)/shard_map/ppermute | solution.py:491
  38.7 0.5 collective-permute-start.15
  39.3 4.8 %hidden.8 = (bf16[256,768]{1,0:T(8,128)(2,1)S(1)}, f32[384,384]{1,0:T(8,128)S(1)}, f32[384,384]{1,0:T(8,128)S(1)}) custom-call(s32[2]{0:T(128)S(1)} %pad_add_fusion.place_ref, bf16[72,2048]{1,0:T(8,128)(2,1)S(1)} %collective-permute-done.3.refs_0_, bf16[64,2048]{1,0:T(8,128)(2,1)S(1)} %collective-permute-done.10.refs_1_, ...), custom_call_target="tpu_custom_call" | custom-call | flops 1610612736 | bytes 7340032 | tf_op jit(solution)/shard_map/hidden/pallas_call | solution.py:263
  44.0 1.1 collective-permute-done.8.refs_0_
  45.1 1.5 %collective-permute-done.9.refs_3_ = bf16[72,2048]{1,0:T(8,128)(2,1)S(1)} collective-permute-done((bf16[72,2048]{1,0:T(8,128)(2,1)S(1)}, bf16[72,2048]{1,0:T(8,128)(2,1)S(1)}, u32[]{:S(2)}, u32[]{:S(2)}) %collective-permute-start.9) | collective-permute-done | bytes 294944 | tf_op jit(solution)/shard_map/ppermute | solution.py:491
  46.6 1.6 %collective-permute-start.12 = (bf16[72,2048]{1,0:T(8,128)(2,1)S(1)}, bf16[72,2048]{1,0:T(8,128)(2,1)S(1)}, u32[]{:S(2)}, u32[]{:S(2)}) collective-permute-start(bf16[72,2048]{1,0:T(8,128)(2,1)S(1)} %collective-permute-done.8.refs_0_), channel_id=1, source_target_pairs={{0,4},{1,5},{4,8},{5,9},{8,12},{9,13},{12,14},{13,15},{14,10},{15,... | collective-permute-start | bytes 884744 | tf_op jit(solution)/shard_map/ppermute | solution.py:491
  48.7 2.1 %collective-permute-done.14.refs_1_ = bf16[64,2048]{1,0:T(8,128)(2,1)S(1)} collective-permute-done((bf16[64,2048]{1,0:T(8,128)(2,1)S(1)}, bf16[64,2048]{1,0:T(8,128)(2,1)S(1)}, u32[]{:S(2)}, u32[]{:S(2)}) %collective-permute-start.14) | collective-permute-done | bytes 262176 | tf_op jit(solution)/shard_map/ppermute | solution.py:491
  50.8 1.1 %collective-permute-done.15.refs_2_ = bf16[64,2048]{1,0:T(8,128)(2,1)S(1)} collective-permute-done((bf16[64,2048]{1,0:T(8,128)(2,1)S(1)}, bf16[64,2048]{1,0:T(8,128)(2,1)S(1)}, u32[]{:S(2)}, u32[]{:S(2)}) %collective-permute-start.15) | collective-permute-done | bytes 262176 | tf_op jit(solution)/shard_map/ppermute | solution.py:491
  51.9 4.8 %hidden.9 = (bf16[256,768]{1,0:T(8,128)(2,1)S(1)}, f32[384,384]{1,0:T(8,128)S(1)}, f32[384,384]{1,0:T(8,128)S(1)}) custom-call(s32[2]{0:T(128)S(1)} %pad_add_fusion.place_ref, bf16[72,2048]{1,0:T(8,128)(2,1)S(1)} %collective-permute-done.8.refs_0_, bf16[64,2048]{1,0:T(8,128)(2,1)S(1)} %collective-permute-done.14.refs_1_, ...), custom_call_target="tpu_custom_call" | custom-call | flops 1610612736 | bytes 7340032 | tf_op jit(solution)/shard_map/hidden/pallas_call | solution.py:263
  56.7 2.6 %hidden.11 = (bf16[128,384]{1,0:T(8,128)(2,1)S(1)}, f32[384,384]{1,0:T(8,128)S(1)}) custom-call(s32[2]{0:T(128)S(1)} %pad_add_fusion.place_ref, bf16[72,2048]{1,0:T(8,128)(2,1)S(1)} %collective-permute-done.12.refs_0_, bf16[72,2048]{1,0:T(8,128)(2,1)S(1)} %collective-permute-done.13.refs_1_, bf16[384,2048]{1,0:T(8,128)(2,1)S(1)} %get-tuple-element.64.refs_4_.refs_6_.refs_2_, ...), custom_call_target="tpu_custom_call" | custom-call | flops 402653184 | bytes 3670016 | tf_op jit(solution)/shard_map/hidden/pallas_call | solution.py:263
  59.4 2.6 %hidden.10 = (bf16[128,384]{1,0:T(8,128)(2,1)S(1)}, f32[384,384]{1,0:T(8,128)S(1)}) custom-call(s32[2]{0:T(128)S(1)} %pad_add_fusion.place_ref, bf16[72,2048]{1,0:T(8,128)(2,1)S(1)} %collective-permute-done.12.refs_0_, bf16[72,2048]{1,0:T(8,128)(2,1)S(1)} %collective-permute-done.13.refs_1_, bf16[384,2048]{1,0:T(8,128)(2,1)S(1)} %bitcast.15, ...), custom_call_target="tpu_custom_call" | custom-call | flops 402653184 | bytes 3670016 | tf_op jit(solution)/shard_map/hidden/pallas_call | solution.py:263
  62.0 2.6 %prune.1 = (bf16[384,1024]{1,0:T(8,128)(2,1)S(1)}, bf16[384,384]{1,0:T(8,128)(2,1)S(1)}) custom-call(f32[384,384]{1,0:T(8,128)S(1)} %get-tuple-element.94.own_ref, f32[384,384]{1,0:T(8,128)S(1)} %collective-permute-done.16.other_ref, bf16[384,2048]{1,0:T(8,128)(2,1)S(1)} %get-tuple-element.97.error_ref, bf16[384,2048]{1,0:T(8,128)(2,1)S(1)} %bitcast.23, ...), custom_call_target="tpu_custom_call" | custom-call | flops 981467136 | bytes 4325376 | tf_op jit(solution)/shard_map/prune/pallas_call | solution.py:337
  64.6 0.6 collective-permute-start.26
  65.1 0.6 prune_next.1.own_ref
  65.8 1.2 %collective-permute-done.26.other_ref = bf16[384,1024]{1,0:T(8,128)(2,1)S(1)} collective-permute-done((bf16[384,1024]{1,0:T(8,128)(2,1)S(1)}, bf16[384,1024]{1,0:T(8,128)(2,1)S(1)}, u32[]{:S(2)}, u32[]{:S(2)}) %collective-permute-start.26) | collective-permute-done | bytes 786464 | tf_op jit(solution)/shard_map/ppermute | solution.py:494
  67.5 0.7 collective-permute-start.27
  68.3 1.3 %collective-permute-start.28 = (bf16[64,1024]{1,0:T(8,128)(2,1)S(1)}, bf16[64,1024]{1,0:T(8,128)(2,1)S(1)}, u32[]{:S(2)}, u32[]{:S(2)}) collective-permute-start(bf16[64,1024]{1,0:T(8,128)(2,1)S(1)} %get-tuple-element.115), channel_id=1, source_target_pairs={{0,4},{1,5},{4,8},{5,9},{8,12},{9,13},{12,14},{13,15},{14,10},{15,... | collective-permute-start | bytes 393224 | tf_op jit(solution)/shard_map/ppermute | solution.py:491
  70.1 0.7 collective-permute-start.18
  70.8 1.3 %collective-permute-start.19 = (bf16[64,1024]{1,0:T(8,128)(2,1)S(1)}, bf16[64,1024]{1,0:T(8,128)(2,1)S(1)}, u32[]{:S(2)}, u32[]{:S(2)}) collective-permute-start(bf16[64,1024]{1,0:T(8,128)(2,1)S(1)} %get-tuple-element.106), channel_id=1, source_target_pairs={{0,4},{1,5},{4,8},{5,9},{8,12},{9,13},{12,14},{13,15},{14,10},{15,... | collective-permute-start | bytes 393224 | tf_op jit(solution)/shard_map/ppermute | solution.py:491
  72.1 1.8 %collective-permute-done.27.refs_0_ = bf16[64,1024]{1,0:T(8,128)(2,1)S(1)} collective-permute-done((bf16[64,1024]{1,0:T(8,128)(2,1)S(1)}, bf16[64,1024]{1,0:T(8,128)(2,1)S(1)}, u32[]{:S(2)}, u32[]{:S(2)}) %collective-permute-start.27) | collective-permute-done | bytes 131104 | tf_op jit(solution)/shard_map/ppermute | solution.py:491
  73.9 0.6 collective-permute-done.28.refs_1_
  74.5 0.7 outputs.13
  75.2 1.6 %collective-permute-start.29 = (bf16[128,1024]{1,0:T(8,128)(2,1)S(1)}, bf16[128,1024]{1,0:T(8,128)(2,1)S(1)}, u32[]{:S(2)}, u32[]{:S(2)}) collective-permute-start(bf16[128,1024]{1,0:T(8,128)(2,1)S(1)} %get-tuple-element.116), channel_id=1, source_target_pairs={{0,2},{1,3},{4,0},{5,1},{8,4},{9,5},{12,8},{13,9},{14,12},{15,13},... | collective-permute-start | bytes 786440 | tf_op jit(solution)/shard_map/ppermute | solution.py:491
  77.3 0.7 outputs.9
  78.0 1.6 %collective-permute-start.20 = (bf16[128,1024]{1,0:T(8,128)(2,1)S(1)}, bf16[128,1024]{1,0:T(8,128)(2,1)S(1)}, u32[]{:S(2)}, u32[]{:S(2)}) collective-permute-start(bf16[128,1024]{1,0:T(8,128)(2,1)S(1)} %get-tuple-element.107), channel_id=1, source_target_pairs={{0,2},{1,3},{4,0},{5,1},{8,4},{9,5},{12,8},{13,9},{14,12},{15,13},... | collective-permute-start | bytes 786440 | tf_op jit(solution)/shard_map/ppermute | solution.py:491
  80.1 4.4 %collective-permute-done.29.refs_0_ = bf16[128,1024]{1,0:T(8,128)(2,1)S(1)} collective-permute-done((bf16[128,1024]{1,0:T(8,128)(2,1)S(1)}, bf16[128,1024]{1,0:T(8,128)(2,1)S(1)}, u32[]{:S(2)}, u32[]{:S(2)}) %collective-permute-start.29) | collective-permute-done | bytes 262176 | tf_op jit(solution)/shard_map/ppermute | solution.py:491
  84.5 1.5 %collective-permute-done.30.refs_1_ = bf16[128,1024]{1,0:T(8,128)(2,1)S(1)} collective-permute-done((bf16[128,1024]{1,0:T(8,128)(2,1)S(1)}, bf16[128,1024]{1,0:T(8,128)(2,1)S(1)}, u32[]{:S(2)}, u32[]{:S(2)}) %collective-permute-start.30) | collective-permute-done | bytes 262176 | tf_op jit(solution)/shard_map/ppermute | solution.py:491
  86.0 0.7 outputs.14
  86.7 1.6 %collective-permute-start.31 = (bf16[128,1024]{1,0:T(8,128)(2,1)S(1)}, bf16[128,1024]{1,0:T(8,128)(2,1)S(1)}, u32[]{:S(2)}, u32[]{:S(2)}) collective-permute-start(bf16[128,1024]{1,0:T(8,128)(2,1)S(1)} %get-tuple-element.118), channel_id=1, source_target_pairs={{0,2},{1,3},{4,0},{5,1},{8,4},{9,5},{12,8},{13,9},{14,12},{15,13},... | collective-permute-start | bytes 786440 | tf_op jit(solution)/shard_map/ppermute | solution.py:491
  88.8 1.4 %collective-permute-done.20.refs_0_ = bf16[128,1024]{1,0:T(8,128)(2,1)S(1)} collective-permute-done((bf16[128,1024]{1,0:T(8,128)(2,1)S(1)}, bf16[128,1024]{1,0:T(8,128)(2,1)S(1)}, u32[]{:S(2)}, u32[]{:S(2)}) %collective-permute-start.20) | collective-permute-done | bytes 262176 | tf_op jit(solution)/shard_map/ppermute | solution.py:491
  90.2 1.5 %collective-permute-done.21.refs_1_ = bf16[128,1024]{1,0:T(8,128)(2,1)S(1)} collective-permute-done((bf16[128,1024]{1,0:T(8,128)(2,1)S(1)}, bf16[128,1024]{1,0:T(8,128)(2,1)S(1)}, u32[]{:S(2)}, u32[]{:S(2)}) %collective-permute-start.21) | collective-permute-done | bytes 262176 | tf_op jit(solution)/shard_map/ppermute | solution.py:491
  91.6 0.7 outputs.10
  92.3 1.6 %collective-permute-start.22 = (bf16[128,1024]{1,0:T(8,128)(2,1)S(1)}, bf16[128,1024]{1,0:T(8,128)(2,1)S(1)}, u32[]{:S(2)}, u32[]{:S(2)}) collective-permute-start(bf16[128,1024]{1,0:T(8,128)(2,1)S(1)} %get-tuple-element.109), channel_id=1, source_target_pairs={{0,2},{1,3},{4,0},{5,1},{8,4},{9,5},{12,8},{13,9},{14,12},{15,13},... | collective-permute-start | bytes 786440 | tf_op jit(solution)/shard_map/ppermute | solution.py:491
  94.4 1.6 %collective-permute-done.31.refs_0_ = bf16[128,1024]{1,0:T(8,128)(2,1)S(1)} collective-permute-done((bf16[128,1024]{1,0:T(8,128)(2,1)S(1)}, bf16[128,1024]{1,0:T(8,128)(2,1)S(1)}, u32[]{:S(2)}, u32[]{:S(2)}) %collective-permute-start.31) | collective-permute-done | bytes 262176 | tf_op jit(solution)/shard_map/ppermute | solution.py:491
  96.0 1.5 %collective-permute-done.32.refs_1_ = bf16[128,1024]{1,0:T(8,128)(2,1)S(1)} collective-permute-done((bf16[128,1024]{1,0:T(8,128)(2,1)S(1)}, bf16[128,1024]{1,0:T(8,128)(2,1)S(1)}, u32[]{:S(2)}, u32[]{:S(2)}) %collective-permute-start.32) | collective-permute-done | bytes 262176 | tf_op jit(solution)/shard_map/ppermute | solution.py:491
  97.5 0.7 outputs.15
  98.2 1.6 %collective-permute-start.33 = (bf16[128,1024]{1,0:T(8,128)(2,1)S(1)}, bf16[128,1024]{1,0:T(8,128)(2,1)S(1)}, u32[]{:S(2)}, u32[]{:S(2)}) collective-permute-start(bf16[128,1024]{1,0:T(8,128)(2,1)S(1)} %get-tuple-element.120), channel_id=1, source_target_pairs={{0,2},{1,3},{4,0},{5,1},{8,4},{9,5},{12,8},{13,9},{14,12},{15,13},... | collective-permute-start | bytes 786440 | tf_op jit(solution)/shard_map/ppermute | solution.py:491
  100.3 1.3 %collective-permute-done.22.refs_0_ = bf16[128,1024]{1,0:T(8,128)(2,1)S(1)} collective-permute-done((bf16[128,1024]{1,0:T(8,128)(2,1)S(1)}, bf16[128,1024]{1,0:T(8,128)(2,1)S(1)}, u32[]{:S(2)}, u32[]{:S(2)}) %collective-permute-start.22) | collective-permute-done | bytes 262176 | tf_op jit(solution)/shard_map/ppermute | solution.py:491
  101.6 1.5 %collective-permute-done.23.refs_1_ = bf16[128,1024]{1,0:T(8,128)(2,1)S(1)} collective-permute-done((bf16[128,1024]{1,0:T(8,128)(2,1)S(1)}, bf16[128,1024]{1,0:T(8,128)(2,1)S(1)}, u32[]{:S(2)}, u32[]{:S(2)}) %collective-permute-start.23) | collective-permute-done | bytes 262176 | tf_op jit(solution)/shard_map/ppermute | solution.py:491
  103.2 0.7 outputs.11
  103.9 1.6 %collective-permute-start.24 = (bf16[128,1024]{1,0:T(8,128)(2,1)S(1)}, bf16[128,1024]{1,0:T(8,128)(2,1)S(1)}, u32[]{:S(2)}, u32[]{:S(2)}) collective-permute-start(bf16[128,1024]{1,0:T(8,128)(2,1)S(1)} %get-tuple-element.111), channel_id=1, source_target_pairs={{0,2},{1,3},{4,0},{5,1},{8,4},{9,5},{12,8},{13,9},{14,12},{15,13},... | collective-permute-start | bytes 786440 | tf_op jit(solution)/shard_map/ppermute | solution.py:491
  106.0 1.3 %maximum_bitcast_fusion = bf16[1,384,2048]{2,1,0:T(8,128)(2,1)} fusion(bf16[384,1024]{1,0:T(8,128)(2,1)S(1)} %prune_next.1.own_ref, bf16[384,1024]{1,0:T(8,128)(2,1)S(1)} %get-tuple-element.113.own_ref), kind=kLoop, calls=%fused_computation | loop fusion | flops 3145728 | bytes 3145728 | tf_op jit(solution)/shard_map/broadcast_in_dim | solution.py:559
  108.5 0.8 finish.2.refs_0_
  109.3 1.0 collective-permute-done.24.right_ref
  110.3 1.6 %collective-permute-done.25.left_ref = bf16[128,1024]{1,0:T(8,128)(2,1)S(1)} collective-permute-done((bf16[128,1024]{1,0:T(8,128)(2,1)S(1)}, bf16[128,1024]{1,0:T(8,128)(2,1)S(1)}, u32[]{:S(2)}, u32[]{:S(2)}) %collective-permute-start.25) | collective-permute-done | bytes 262176 | tf_op jit(solution)/shard_map/ppermute | solution.py:491
  111.9 0.8 finish.3
  (43 shorter events, 6.2 us)
Async XLA Ops:
  0.6 16.3 %collective-permute-start = (bf16[384,2048]{1,0:T(8,128)(2,1)}, bf16[384,2048]{1,0:T(8,128)(2,1)}, u32[]{:S(2)}, u32[]{:S(2)}) collective-permute-start(bf16[384,2048]{1,0:T(8,128)(2,1)} %bitcast.10), channel_id=1, source_target_pairs={{0,1},{1,0},{2,3},{3,2},{4,5},{5,4},{6,7},{7,6},{8,9},{9,8},{10,11... | collective-permute-start | bytes 4718600 | tf_op jit(solution)/shard_map/ppermute | solution.py:494
  1.1 16.4 %collective-permute-start.1 = (bf16[384,2048]{1,0:T(8,128)(2,1)}, bf16[384,2048]{1,0:T(8,128)(2,1)}, u32[]{:S(2)}, u32[]{:S(2)}) collective-permute-start(bf16[384,2048]{1,0:T(8,128)(2,1)} %bitcast.16), channel_id=1, source_target_pairs={{0,1},{1,0},{2,3},{3,2},{4,5},{5,4},{6,7},{7,6},{8,9},{9,8},{10,11... | collective-permute-start | bytes 4718600 | tf_op jit(solution)/shard_map/ppermute | solution.py:494
  3.3 10.4 %collective-permute-start.2 = (bf16[72,2048]{1,0:T(8,128)(2,1)}, bf16[72,2048]{1,0:T(8,128)(2,1)S(1)}, u32[]{:S(2)}, u32[]{:S(2)}) collective-permute-start(bf16[72,2048]{1,0:T(8,128)(2,1)} %get-tuple-element.62.refs_0_), channel_id=1, source_target_pairs={{0,4},{1,5},{4,8},{5,9},{8,12},{9,13},{12,14},{13,15},{14,10},{15,... | collective-permute-start | bytes 884744 | tf_op jit(solution)/shard_map/ppermute | solution.py:491
  6.3 9.1 %collective-permute-start.4 = (bf16[72,2048]{1,0:T(8,128)(2,1)}, bf16[72,2048]{1,0:T(8,128)(2,1)}, u32[]{:S(2)}, u32[]{:S(2)}) collective-permute-start(bf16[72,2048]{1,0:T(8,128)(2,1)} %get-tuple-element.67), channel_id=1, source_target_pairs={{0,2},{1,3},{4,0},{5,1},{8,4},{9,5},{12,8},{13,9},{14,12},{15,13},... | collective-permute-start | bytes 884744 | tf_op jit(solution)/shard_map/ppermute | solution.py:491
  6.3 1.4 %copy-start.2 = (bf16[1,384,2048]{2,1,0:T(8,128)(2,1)S(1)}, bf16[1,384,2048]{2,1,0:T(8,128)(2,1)}, u32[]{:S(2)}) copy-start(bf16[1,384,2048]{2,1,0:T(8,128)(2,1)} %param.12) | copy-start | bytes 4718596
  7.8 1.1 %copy-start.4 = (s32[1,96,2048]{2,1,0:T(8,128)S(1)}, s32[1,96,2048]{2,1,0:T(8,128)}, u32[]{:S(2)}) copy-start(s32[1,96,2048]{2,1,0:T(8,128)} %param.13) | copy-start | bytes 2359300
  11.3 15.8 %collective-permute-start.6 = (bf16[64,2048]{1,0:T(8,128)(2,1)}, bf16[64,2048]{1,0:T(8,128)(2,1)}, u32[]{:S(2)}, u32[]{:S(2)}) collective-permute-start(bf16[64,2048]{1,0:T(8,128)(2,1)} %get-tuple-element.71.refs_1_), channel_id=1, source_target_pairs={{0,4},{1,5},{4,8},{5,9},{8,12},{9,13},{12,14},{13,15},{14,10},{15,... | collective-permute-start | bytes 786440 | tf_op jit(solution)/shard_map/ppermute | solution.py:491
  13.7 13.4 %collective-permute-start.7 = (bf16[64,2048]{1,0:T(8,128)(2,1)}, bf16[64,2048]{1,0:T(8,128)(2,1)}, u32[]{:S(2)}, u32[]{:S(2)}) collective-permute-start(bf16[64,2048]{1,0:T(8,128)(2,1)} %get-tuple-element.72), channel_id=1, source_target_pairs={{0,2},{1,3},{4,0},{5,1},{8,4},{9,5},{12,8},{13,9},{14,12},{15,13},... | collective-permute-start | bytes 786440 | tf_op jit(solution)/shard_map/ppermute | solution.py:491
  15.5 19.7 %collective-permute-start.3 = (bf16[72,2048]{1,0:T(8,128)(2,1)S(1)}, bf16[72,2048]{1,0:T(8,128)(2,1)S(1)}, u32[]{:S(2)}, u32[]{:S(2)}) collective-permute-start(bf16[72,2048]{1,0:T(8,128)(2,1)S(1)} %collective-permute-done.2.refs_0_), channel_id=1, source_target_pairs={{0,4},{1,5},{4,8},{5,9},{8,12},{9,13},{12,14},{13,15},{14,10},{15,... | collective-permute-start | bytes 884744 | tf_op jit(solution)/shard_map/ppermute | solution.py:491
  17.0 18.2 %collective-permute-start.5 = (bf16[72,2048]{1,0:T(8,128)(2,1)}, bf16[72,2048]{1,0:T(8,128)(2,1)S(1)}, u32[]{:S(2)}, u32[]{:S(2)}) collective-permute-start(bf16[72,2048]{1,0:T(8,128)(2,1)} %collective-permute-done.4.refs_3_), channel_id=1, source_target_pairs={{0,2},{1,3},{4,0},{5,1},{8,4},{9,5},{12,8},{13,9},{14,12},{15,13},... | collective-permute-start | bytes 884744 | tf_op jit(solution)/shard_map/ppermute | solution.py:491
  17.6 2.9 %copy-start = (bf16[1,384,2048]{2,1,0:T(8,128)(2,1)S(1)}, bf16[1,384,2048]{2,1,0:T(8,128)(2,1)}, u32[]{:S(2)}) copy-start(bf16[1,384,2048]{2,1,0:T(8,128)(2,1)} %param.10) | copy-start | bytes 4718596
  17.6 2.9 %copy-start.1 = (bf16[1,384,2048]{2,1,0:T(8,128)(2,1)S(1)}, bf16[1,384,2048]{2,1,0:T(8,128)(2,1)}, u32[]{:S(2)}) copy-start(bf16[1,384,2048]{2,1,0:T(8,128)(2,1)} %param.11) | copy-start | bytes 4718596
  20.5 1.0 copy-start.5
  27.1 10.1 %collective-permute-start.10 = (bf16[64,2048]{1,0:T(8,128)(2,1)}, bf16[64,2048]{1,0:T(8,128)(2,1)S(1)}, u32[]{:S(2)}, u32[]{:S(2)}) collective-permute-start(bf16[64,2048]{1,0:T(8,128)(2,1)} %collective-permute-done.6.refs_1_), channel_id=1, source_target_pairs={{0,4},{1,5},{4,8},{5,9},{8,12},{9,13},{12,14},{13,15},{14,10},{15,... | collective-permute-start | bytes 786440 | tf_op jit(solution)/shard_map/ppermute | solution.py:491
  28.7 10.1 %collective-permute-start.11 = (bf16[64,2048]{1,0:T(8,128)(2,1)}, bf16[64,2048]{1,0:T(8,128)(2,1)S(1)}, u32[]{:S(2)}, u32[]{:S(2)}) collective-permute-start(bf16[64,2048]{1,0:T(8,128)(2,1)} %collective-permute-done.7.refs_2_), channel_id=1, source_target_pairs={{0,2},{1,3},{4,0},{5,1},{8,4},{9,5},{12,8},{13,9},{14,12},{15,13},... | collective-permute-start | bytes 786440 | tf_op jit(solution)/shard_map/ppermute | solution.py:491
  35.2 10.0 %collective-permute-start.8 = (bf16[72,2048]{1,0:T(8,128)(2,1)S(1)}, bf16[72,2048]{1,0:T(8,128)(2,1)S(1)}, u32[]{:S(2)}, u32[]{:S(2)}) collective-permute-start(bf16[72,2048]{1,0:T(8,128)(2,1)S(1)} %collective-permute-done.3.refs_0_), channel_id=1, source_target_pairs={{0,4},{1,5},{4,8},{5,9},{8,12},{9,13},{12,14},{13,15},{14,10},{15,... | collective-permute-start | bytes 884744 | tf_op jit(solution)/shard_map/ppermute | solution.py:491
  36.7 9.9 %collective-permute-start.9 = (bf16[72,2048]{1,0:T(8,128)(2,1)S(1)}, bf16[72,2048]{1,0:T(8,128)(2,1)S(1)}, u32[]{:S(2)}, u32[]{:S(2)}) collective-permute-start(bf16[72,2048]{1,0:T(8,128)(2,1)S(1)} %collective-permute-done.5.refs_3_), channel_id=1, source_target_pairs={{0,2},{1,3},{4,0},{5,1},{8,4},{9,5},{12,8},{13,9},{14,12},{15,13},... | collective-permute-start | bytes 884744 | tf_op jit(solution)/shard_map/ppermute | solution.py:491
  37.2 13.5 %collective-permute-start.14 = (bf16[64,2048]{1,0:T(8,128)(2,1)S(1)}, bf16[64,2048]{1,0:T(8,128)(2,1)S(1)}, u32[]{:S(2)}, u32[]{:S(2)}) collective-permute-start(bf16[64,2048]{1,0:T(8,128)(2,1)S(1)} %collective-permute-done.10.refs_1_), channel_id=1, source_target_pairs={{0,4},{1,5},{4,8},{5,9},{8,12},{9,13},{12,14},{13,15},{14,10},{15,... | collective-permute-start | bytes 786440 | tf_op jit(solution)/shard_map/ppermute | solution.py:491
  38.7 13.2 %collective-permute-start.15 = (bf16[64,2048]{1,0:T(8,128)(2,1)S(1)}, bf16[64,2048]{1,0:T(8,128)(2,1)S(1)}, u32[]{:S(2)}, u32[]{:S(2)}) collective-permute-start(bf16[64,2048]{1,0:T(8,128)(2,1)S(1)} %collective-permute-done.11.refs_2_), channel_id=1, source_target_pairs={{0,2},{1,3},{4,0},{5,1},{8,4},{9,5},{12,8},{13,9},{14,12},{15,13},... | collective-permute-start | bytes 786440 | tf_op jit(solution)/shard_map/ppermute | solution.py:491
  46.6 10.1 %collective-permute-start.12 = (bf16[72,2048]{1,0:T(8,128)(2,1)S(1)}, bf16[72,2048]{1,0:T(8,128)(2,1)S(1)}, u32[]{:S(2)}, u32[]{:S(2)}) collective-permute-start(bf16[72,2048]{1,0:T(8,128)(2,1)S(1)} %collective-permute-done.8.refs_0_), channel_id=1, source_target_pairs={{0,4},{1,5},{4,8},{5,9},{8,12},{9,13},{12,14},{13,15},{14,10},{15,... | collective-permute-start | bytes 884744 | tf_op jit(solution)/shard_map/ppermute | solution.py:491
  48.2 8.5 %collective-permute-start.13 = (bf16[72,2048]{1,0:T(8,128)(2,1)S(1)}, bf16[72,2048]{1,0:T(8,128)(2,1)S(1)}, u32[]{:S(2)}, u32[]{:S(2)}) collective-permute-start(bf16[72,2048]{1,0:T(8,128)(2,1)S(1)} %collective-permute-done.9.refs_3_), channel_id=1, source_target_pairs={{0,2},{1,3},{4,0},{5,1},{8,4},{9,5},{12,8},{13,9},{14,12},{15,13},... | collective-permute-start | bytes 884744 | tf_op jit(solution)/shard_map/ppermute | solution.py:491
  59.3 2.7 %copy-start.3 = (bf16[1,384,2048]{2,1,0:T(8,128)(2,1)S(1)}, bf16[1,384,2048]{2,1,0:T(8,128)(2,1)}, u32[]{:S(2)}) copy-start(bf16[1,384,2048]{2,1,0:T(8,128)(2,1)} %param.12) | copy-start | bytes 4718596
  59.3 2.7 %collective-permute-start.16 = (f32[384,384]{1,0:T(8,128)S(1)}, f32[384,384]{1,0:T(8,128)S(1)}, u32[]{:S(2)}, u32[]{:S(2)}) collective-permute-start(f32[384,384]{1,0:T(8,128)S(1)} %get-tuple-element.96), channel_id=1, source_target_pairs={{0,1},{1,0},{2,3},{3,2},{4,5},{5,4},{6,7},{7,6},{8,9},{9,8},{10,11... | collective-permute-start | bytes 1769480 | tf_op jit(solution)/shard_map/ppermute | solution.py:494
  64.6 2.5 %collective-permute-start.26 = (bf16[384,1024]{1,0:T(8,128)(2,1)S(1)}, bf16[384,1024]{1,0:T(8,128)(2,1)S(1)}, u32[]{:S(2)}, u32[]{:S(2)}) collective-permute-start(bf16[384,1024]{1,0:T(8,128)(2,1)S(1)} %get-tuple-element.113.own_ref), channel_id=1, source_target_pairs={{0,1},{1,0},{2,3},{3,2},{4,5},{5,4},{6,7},{7,6},{8,9},{9,8},{10,11... | collective-permute-start | bytes 2359304 | tf_op jit(solution)/shard_map/ppermute | solution.py:494
  65.7 3.9 %collective-permute-start.17 = (bf16[384,1024]{1,0:T(8,128)(2,1)S(1)}, bf16[384,1024]{1,0:T(8,128)(2,1)S(1)}, u32[]{:S(2)}, u32[]{:S(2)}) collective-permute-start(bf16[384,1024]{1,0:T(8,128)(2,1)S(1)} %prune_next.1.own_ref), channel_id=1, source_target_pairs={{0,1},{1,0},{2,3},{3,2},{4,5},{5,4},{6,7},{7,6},{8,9},{9,8},{10,11... | collective-permute-start | bytes 2359304 | tf_op jit(solution)/shard_map/ppermute | solution.py:494
  67.5 6.4 %collective-permute-start.27 = (bf16[64,1024]{1,0:T(8,128)(2,1)S(1)}, bf16[64,1024]{1,0:T(8,128)(2,1)S(1)}, u32[]{:S(2)}, u32[]{:S(2)}) collective-permute-start(bf16[64,1024]{1,0:T(8,128)(2,1)S(1)} %get-tuple-element.114), channel_id=1, source_target_pairs={{0,2},{1,3},{4,0},{5,1},{8,4},{9,5},{12,8},{13,9},{14,12},{15,13},... | collective-permute-start | bytes 393224 | tf_op jit(solution)/shard_map/ppermute | solution.py:491
  68.3 6.3 %collective-permute-start.28 = (bf16[64,1024]{1,0:T(8,128)(2,1)S(1)}, bf16[64,1024]{1,0:T(8,128)(2,1)S(1)}, u32[]{:S(2)}, u32[]{:S(2)}) collective-permute-start(bf16[64,1024]{1,0:T(8,128)(2,1)S(1)} %get-tuple-element.115), channel_id=1, source_target_pairs={{0,4},{1,5},{4,8},{5,9},{8,12},{9,13},{12,14},{13,15},{14,10},{15,... | collective-permute-start | bytes 393224 | tf_op jit(solution)/shard_map/ppermute | solution.py:491
  70.1 7.3 %collective-permute-start.18 = (bf16[64,1024]{1,0:T(8,128)(2,1)S(1)}, bf16[64,1024]{1,0:T(8,128)(2,1)S(1)}, u32[]{:S(2)}, u32[]{:S(2)}) collective-permute-start(bf16[64,1024]{1,0:T(8,128)(2,1)S(1)} %get-tuple-element.105), channel_id=1, source_target_pairs={{0,2},{1,3},{4,0},{5,1},{8,4},{9,5},{12,8},{13,9},{14,12},{15,13},... | collective-permute-start | bytes 393224 | tf_op jit(solution)/shard_map/ppermute | solution.py:491
  70.8 6.5 %collective-permute-start.19 = (bf16[64,1024]{1,0:T(8,128)(2,1)S(1)}, bf16[64,1024]{1,0:T(8,128)(2,1)S(1)}, u32[]{:S(2)}, u32[]{:S(2)}) collective-permute-start(bf16[64,1024]{1,0:T(8,128)(2,1)S(1)} %get-tuple-element.106), channel_id=1, source_target_pairs={{0,4},{1,5},{4,8},{5,9},{8,12},{9,13},{12,14},{13,15},{14,10},{15,... | collective-permute-start | bytes 393224 | tf_op jit(solution)/shard_map/ppermute | solution.py:491
  75.2 9.3 %collective-permute-start.29 = (bf16[128,1024]{1,0:T(8,128)(2,1)S(1)}, bf16[128,1024]{1,0:T(8,128)(2,1)S(1)}, u32[]{:S(2)}, u32[]{:S(2)}) collective-permute-start(bf16[128,1024]{1,0:T(8,128)(2,1)S(1)} %get-tuple-element.116), channel_id=1, source_target_pairs={{0,2},{1,3},{4,0},{5,1},{8,4},{9,5},{12,8},{13,9},{14,12},{15,13},... | collective-permute-start | bytes 786440 | tf_op jit(solution)/shard_map/ppermute | solution.py:491
  76.9 9.1 %collective-permute-start.30 = (bf16[128,1024]{1,0:T(8,128)(2,1)S(1)}, bf16[128,1024]{1,0:T(8,128)(2,1)S(1)}, u32[]{:S(2)}, u32[]{:S(2)}) collective-permute-start(bf16[128,1024]{1,0:T(8,128)(2,1)S(1)} %get-tuple-element.117), channel_id=1, source_target_pairs={{0,4},{1,5},{4,8},{5,9},{8,12},{9,13},{12,14},{13,15},{14,10},{15,... | collective-permute-start | bytes 786440 | tf_op jit(solution)/shard_map/ppermute | solution.py:491
  78.0 12.1 %collective-permute-start.20 = (bf16[128,1024]{1,0:T(8,128)(2,1)S(1)}, bf16[128,1024]{1,0:T(8,128)(2,1)S(1)}, u32[]{:S(2)}, u32[]{:S(2)}) collective-permute-start(bf16[128,1024]{1,0:T(8,128)(2,1)S(1)} %get-tuple-element.107), channel_id=1, source_target_pairs={{0,2},{1,3},{4,0},{5,1},{8,4},{9,5},{12,8},{13,9},{14,12},{15,13},... | collective-permute-start | bytes 786440 | tf_op jit(solution)/shard_map/ppermute | solution.py:491
  79.7 11.9 %collective-permute-start.21 = (bf16[128,1024]{1,0:T(8,128)(2,1)S(1)}, bf16[128,1024]{1,0:T(8,128)(2,1)S(1)}, u32[]{:S(2)}, u32[]{:S(2)}) collective-permute-start(bf16[128,1024]{1,0:T(8,128)(2,1)S(1)} %get-tuple-element.108), channel_id=1, source_target_pairs={{0,4},{1,5},{4,8},{5,9},{8,12},{9,13},{12,14},{13,15},{14,10},{15,... | collective-permute-start | bytes 786440 | tf_op jit(solution)/shard_map/ppermute | solution.py:491
  86.7 9.3 %collective-permute-start.31 = (bf16[128,1024]{1,0:T(8,128)(2,1)S(1)}, bf16[128,1024]{1,0:T(8,128)(2,1)S(1)}, u32[]{:S(2)}, u32[]{:S(2)}) collective-permute-start(bf16[128,1024]{1,0:T(8,128)(2,1)S(1)} %get-tuple-element.118), channel_id=1, source_target_pairs={{0,2},{1,3},{4,0},{5,1},{8,4},{9,5},{12,8},{13,9},{14,12},{15,13},... | collective-permute-start | bytes 786440 | tf_op jit(solution)/shard_map/ppermute | solution.py:491
  88.3 9.2 %collective-permute-start.32 = (bf16[128,1024]{1,0:T(8,128)(2,1)S(1)}, bf16[128,1024]{1,0:T(8,128)(2,1)S(1)}, u32[]{:S(2)}, u32[]{:S(2)}) collective-permute-start(bf16[128,1024]{1,0:T(8,128)(2,1)S(1)} %get-tuple-element.119), channel_id=1, source_target_pairs={{0,4},{1,5},{4,8},{5,9},{8,12},{9,13},{12,14},{13,15},{14,10},{15,... | collective-permute-start | bytes 786440 | tf_op jit(solution)/shard_map/ppermute | solution.py:491
  92.3 9.3 %collective-permute-start.22 = (bf16[128,1024]{1,0:T(8,128)(2,1)S(1)}, bf16[128,1024]{1,0:T(8,128)(2,1)S(1)}, u32[]{:S(2)}, u32[]{:S(2)}) collective-permute-start(bf16[128,1024]{1,0:T(8,128)(2,1)S(1)} %get-tuple-element.109), channel_id=1, source_target_pairs={{0,2},{1,3},{4,0},{5,1},{8,4},{9,5},{12,8},{13,9},{14,12},{15,13},... | collective-permute-start | bytes 786440 | tf_op jit(solution)/shard_map/ppermute | solution.py:491
  93.9 9.2 %collective-permute-start.23 = (bf16[128,1024]{1,0:T(8,128)(2,1)S(1)}, bf16[128,1024]{1,0:T(8,128)(2,1)S(1)}, u32[]{:S(2)}, u32[]{:S(2)}) collective-permute-start(bf16[128,1024]{1,0:T(8,128)(2,1)S(1)} %get-tuple-element.110), channel_id=1, source_target_pairs={{0,4},{1,5},{4,8},{5,9},{8,12},{9,13},{12,14},{13,15},{14,10},{15,... | collective-permute-start | bytes 786440 | tf_op jit(solution)/shard_map/ppermute | solution.py:491
  98.2 9.9 %collective-permute-start.33 = (bf16[128,1024]{1,0:T(8,128)(2,1)S(1)}, bf16[128,1024]{1,0:T(8,128)(2,1)S(1)}, u32[]{:S(2)}, u32[]{:S(2)}) collective-permute-start(bf16[128,1024]{1,0:T(8,128)(2,1)S(1)} %get-tuple-element.120), channel_id=1, source_target_pairs={{0,2},{1,3},{4,0},{5,1},{8,4},{9,5},{12,8},{13,9},{14,12},{15,13},... | collective-permute-start | bytes 786440 | tf_op jit(solution)/shard_map/ppermute | solution.py:491
  99.9 8.7 %collective-permute-start.34 = (bf16[128,1024]{1,0:T(8,128)(2,1)S(1)}, bf16[128,1024]{1,0:T(8,128)(2,1)S(1)}, u32[]{:S(2)}, u32[]{:S(2)}) collective-permute-start(bf16[128,1024]{1,0:T(8,128)(2,1)S(1)} %get-tuple-element.121), channel_id=1, source_target_pairs={{0,4},{1,5},{4,8},{5,9},{8,12},{9,13},{12,14},{13,15},{14,10},{15,... | collective-permute-start | bytes 786440 | tf_op jit(solution)/shard_map/ppermute | solution.py:491
  103.9 6.4 %collective-permute-start.24 = (bf16[128,1024]{1,0:T(8,128)(2,1)S(1)}, bf16[128,1024]{1,0:T(8,128)(2,1)S(1)}, u32[]{:S(2)}, u32[]{:S(2)}) collective-permute-start(bf16[128,1024]{1,0:T(8,128)(2,1)S(1)} %get-tuple-element.111), channel_id=1, source_target_pairs={{0,2},{1,3},{4,0},{5,1},{8,4},{9,5},{12,8},{13,9},{14,12},{15,13},... | collective-permute-start | bytes 786440 | tf_op jit(solution)/shard_map/ppermute | solution.py:491
  105.5 6.4 %collective-permute-start.25 = (bf16[128,1024]{1,0:T(8,128)(2,1)S(1)}, bf16[128,1024]{1,0:T(8,128)(2,1)S(1)}, u32[]{:S(2)}, u32[]{:S(2)}) collective-permute-start(bf16[128,1024]{1,0:T(8,128)(2,1)S(1)} %get-tuple-element.112), channel_id=1, source_target_pairs={{0,4},{1,5},{4,8},{5,9},{8,12},{9,13},{12,14},{13,15},{14,10},{15,... | collective-permute-start | bytes 786440 | tf_op jit(solution)/shard_map/ppermute | solution.py:491

commit v3 on v2

--- a/solution.py
+++ b/solution.py
@@ -202,54 +202,35 @@
     count = len(experts)
     x_refs, refs = refs[:pieces], refs[pieces:]
     pairs, grams_in = refs[: 2 * count], refs[2 * count : 3 * count]
-    out_ref, gram_refs, rows_ref, weight_ref, hidden_ref = (
-        refs[-4 - count],
-        refs[-3 - count : -3],
-        *refs[-3:],
-    )
-    steps = pl.num_programs(0) // count
-
-    def work(which, step):
-        @pl.when(step == 0)
-        def _():
-            half = min(x.shape[0] for x in x_refs)
-            half = half - half % 16
-            if which == 0:
-                for at, x in enumerate(x_refs):
-                    rows_ref[at * half : (at + 1) * half, :] = x[:half, :]
-            expert = place_ref[experts[which]]
-            weight = [token_weights(x_refs[i], experts_all, expert) for i in sources]
-            tok_rows = weight[0].shape[1]
-            empty = jnp.zeros((8 - len(sources), tok_rows), F32)
-            weight = jnp.concatenate(weight + [empty], axis=0).T
-            for at in range(len(sources)):
-                weight_ref[at * tok_rows : (at + 1) * tok_rows, :] = jnp.broadcast_to(
-                    weight[:, at : at + 1], (tok_rows, CHUNK)
-                )
-
-        at = pl.ds(pl.multiple_of(step * CHUNK, CHUNK), CHUNK)
+    out_ref, gram_refs, rows_ref = refs[-2 - count], refs[-1 - count : -1], refs[-1]
+    half = min(x.shape[0] for x in x_refs)
+    half = half - half % 16
+    for at, x in enumerate(x_refs):
+        rows_ref[at * half : (at + 1) * half, :] = x[:half, :]
+    for which in range(count):
         gate_ref, up_ref = pairs[2 * which], pairs[2 * which + 1]
-        both = jnp.concatenate([gate_ref[at, :], up_ref[at, :]], axis=0)
-        pre = dot(rows_ref[...], both, ((1,), (1,)))
-        gate, up = pre[:, :CHUNK], pre[:, CHUNK:]
-        weight = weight_ref[...]
-        value = gate / (1.0 + jnp.exp(-gate)) * up
-        value = jnp.where(weight >= 0.0, value, 0.0).astype(BF)
-        hidden_ref[:, at] = value
-        out_ref[...] = (value.astype(F32) * (weight * FF ** (-0.5))).astype(BF)
-
-        @pl.when(step == steps - 1)
-        def _():
-            hidden = hidden_ref[...]
-            gram = dot(hidden, hidden, ((0,), (0,)))
-            gram_refs[which][...] = grams_in[which][...] + gram if has_gram else gram
-
-    step = pl.program_id(0)
-    if count == 1:
-        work(0, step)
-    else:
-        for which in range(count):
-            pl.when(step // steps == which)(functools.partial(work, which, step - which * steps))
+        ff = gate_ref.shape[0]
+        weight = [
+            token_weights(x_refs[i], experts_all, place_ref[experts[which]]) for i in sources
+        ]
+        empty = jnp.zeros((8 - len(sources), weight[0].shape[1]), F32)
+        weight = jnp.concatenate(weight + [empty], axis=0).T
+        weight = jnp.concatenate([weight[:, at : at + 1] for at in range(len(sources))], axis=0)
+        parts = []
+        for at in range(0, ff, CHUNK):
+            both = [gate_ref[at : at + CHUNK, :], up_ref[at : at + CHUNK, :]]
+            pre = dot(rows_ref[...], jnp.concatenate(both, axis=0), ((1,), (1,)))
+            gate, up = pre[:, :CHUNK], pre[:, CHUNK:]
+            value = gate / (1.0 + jnp.exp(-gate)) * up
+            value = jnp.where(weight >= 0.0, value, 0.0).astype(BF)
+            column = which * ff + at
+            out_ref[:, column : column + CHUNK] = (
+                value.astype(F32) * (weight * FF ** (-0.5))
+            ).astype(BF)
+            parts.append(value)
+        hidden = jnp.concatenate(parts, axis=1)
+        gram = dot(hidden, hidden, ((0,), (0,)))
+        gram_refs[which][...] = grams_in[which][...] + gram if has_gram else gram
 
 
 def hidden_part(place, experts, experts_all, pieces, sources, pairs, grams):
@@ -259,26 +240,16 @@
     count = len(experts)
     resident = pl.BlockSpec(memory_space=pltpu.VMEM)
     given = [*pieces] + [w for pair in pairs for w in pair] + [*grams]
-    specs = [resident] * (len(pieces) + 2 * count + len(grams))
     return pl.pallas_call(
         functools.partial(
             hidden_kernel, len(pieces), sources, experts, experts_all, len(grams) > 0
         ),
         out_shape=[jax.ShapeDtypeStruct((rows, count * ff), BF)]
         + [jax.ShapeDtypeStruct((ff, ff), F32)] * count,
-        grid_spec=pltpu.PrefetchScalarGridSpec(
-            num_scalar_prefetch=1,
-            grid=(count * ff // CHUNK,),
-            in_specs=specs,
-            out_specs=[pl.BlockSpec((rows, CHUNK), lambda i, _: (0, i))]
-            + [whole((ff, ff))] * count,
-            scratch_shapes=[
-                pltpu.VMEM((rows, width), BF),
-                pltpu.VMEM((rows, CHUNK), F32),
-                pltpu.VMEM((rows, ff), BF),
-            ],
-        ),
-        compiler_params=params("arbitrary"),
+        in_specs=[pl.BlockSpec(memory_space=pltpu.SMEM)] + [resident] * len(given),
+        out_specs=[resident] * (1 + count),
+        scratch_shapes=[pltpu.VMEM((rows, width), BF)],
+        compiler_params=params(),
         cost_estimate=pl.CostEstimate(
             flops=4 * rows * ff * width * count,
             bytes_accessed=2 * (rows + 2 * ff * count) * width,
@@ -495,8 +466,6 @@
 
     place = jnp.stack([here, here ^ 1]).astype(jnp.int32)
     top_wide, bottom_wide, bottom, top = split(tokens, expert_ids, route_weights, devices)
-    right, left = [top_wide, bottom], [top, bottom_wide]
-    groups = [((top_wide, bottom), (0,))]
 
     def hop_first(hop):
         right[0], left[1] = shift(right[0], 1), shift(left[1], -1)
@@ -507,7 +476,10 @@
         right[1], left[0] = shift(right[1], 1), shift(left[0], -1)
         groups.append(((*right, *left), (0, 3)))
 
-    pairs = [(gate, up), (swap(gate), swap(up))]
+    top_wide, bottom_wide, gate_sent, up_sent = tied((top_wide, bottom_wide, gate, up))
+    pairs = [(gate, up), (swap(gate_sent), swap(up_sent))]
+    right, left = [top_wide, bottom], [top, bottom_wide]
+    groups = [((top_wide, bottom), (0,))]
     grams = []
     hidden = []
 

time: 113 us -> 108 us (0.956)
  Pallas kernels: 44.4 us -> 37.5 us
  waiting for transfers between devices: 27.4 us -> 29 us
    pallas_call x6, Pallas kernels: 26.2 us -> 19.3 us  [hidden_part(): pl.pallas_call(functools.partial(hidden_kernel, len(pieces), sources, exp...]
    ppermute x30, waiting for transfers between devices: 26.2 us -> 27.8 us  [shift(): return lax.ppermute(value, AXES, pairs)]
  transfers between devices with their start and end apart: 35 -> 35, of which waited for: 19 -> 19; matrix products, arithmetic and copies ran while one was open for 1% -> 1% of each run, Pallas kernels for 34% -> 28%
where the time goes in v3:
time: 108 us; the launch traced here: 107 us
  Pallas kernels  37.5 us (35%)
  starting transfers between devices  35.1 us (32%)
  waiting for transfers between devices  29 us (27%)
  local copies, waits for them, and re-layouts  3.51 us (3%)
  other arithmetic  1.35 us (1%)
    ppermute x30, starting transfers between devices, shift(): return lax.ppermute(value, AXES, pairs)  33.9 us
    ppermute x30, waiting for transfers between devices, shift(): return lax.ppermute(value, AXES, pairs)  27.8 us
    pallas_call x6, Pallas kernels, hidden_part(): pl.pallas_call(functools.partial(hidden_kernel, len(pieces), sources, exp...  19.3 us
    pallas_call x8, Pallas kernels, outputs(): pl.pallas_call(functools.partial(outputs_kernel, rows // 2, len(arrived))...  5.16 us
    unnamed x12, local copies, waits for them, and re-layouts  3.51 us
    pallas_call x1, Pallas kernels, stage(): pl.pallas_call(stage_kernel, out_shape=[jax.ShapeDtypeStruct(a.shape, a.d...  2.91 us
    pallas_call x1, Pallas kernels, prune_first(): pl.pallas_call(prune_kernel, out_shape=[jax.ShapeDtypeStruct((size, cut),...  2.55 us
    pallas_call x1, Pallas kernels, masks(): pl.pallas_call(mask_kernel, out_shape=[jax.ShapeDtypeStruct((rows, width)...  2.37 us
  transfers between devices with their start and end apart: 35, of which 19 were waited for; matrix products, arithmetic and copies ran while one was open for 1% of the time, Pallas kernels for 28%

profile of v3, /device:TPU:0, one launch (start us, length us, event | category | flops | bytes accessed | tf_op | source)
XLA Modules:
  0.0 107.3 jit_solution(14070004764018657520)
XLA Ops:
  0.6 2.1 %split.1 = (bf16[72,2048]{1,0:T(8,128)(2,1)}, bf16[72,2048]{1,0:T(8,128)(2,1)}, bf16[64,2048]{1,0:T(8,128)(2,1)}, bf16[64,2048]{1,0:T(8,128)(2,1)}) custom-call(bf16[128,2048]{1,0:T(8,128)(2,1)} %x_ref.1, s32[8,128]{1,0:T(8,128)} %bitcast.26, f32[8,128]{1,0:T(8,128)} %bitcast.27), custom_call_target="tpu_custom_call" | custom-call | tf_op jit(solution)/shard_map/split/pallas_call | solution.py:145
  3.3 3.0 %collective-permute-start.2 = (bf16[72,2048]{1,0:T(8,128)(2,1)}, bf16[72,2048]{1,0:T(8,128)(2,1)S(1)}, u32[]{:S(2)}, u32[]{:S(2)}) collective-permute-start(bf16[72,2048]{1,0:T(8,128)(2,1)} %get-tuple-element.68.refs_0_), channel_id=1, source_target_pairs={{0,4},{1,5},{4,8},{5,9},{8,12},{9,13},{12,14},{13,15},{14,10},{15,... | collective-permute-start | bytes 884744 | tf_op jit(solution)/shard_map/ppermute | solution.py:462
  6.3 1.4 %copy-done.2 = bf16[1,384,2048]{2,1,0:T(8,128)(2,1)S(1)} copy-done((bf16[1,384,2048]{2,1,0:T(8,128)(2,1)S(1)}, bf16[1,384,2048]{2,1,0:T(8,128)(2,1)}, u32[]{:S(2)}) %copy-start.2) | copy-done | bytes 1572888
  7.7 1.1 %copy-done.4 = s32[1,96,2048]{2,1,0:T(8,128)S(1)} copy-done((s32[1,96,2048]{2,1,0:T(8,128)S(1)}, s32[1,96,2048]{2,1,0:T(8,128)}, u32[]{:S(2)}) %copy-start.4) | copy-done | bytes 786456
  8.8 2.4 %masks.1 = (bf16[384,2048]{1,0:T(8,128)(2,1)S(1)}, bf16[384,2048]{1,0:T(8,128)(2,1)S(1)}) custom-call(s32[96,2048]{1,0:T(8,128)S(1)} %bitcast.25, bf16[384,2048]{1,0:T(8,128)(2,1)S(1)} %bitcast.22), custom_call_target="tpu_custom_call" | custom-call | flops 603979776 | bytes 6291456 | tf_op jit(solution)/shard_map/masks/pallas_call | solution.py:187
  11.2 2.1 %collective-permute-start.6 = (bf16[64,2048]{1,0:T(8,128)(2,1)}, bf16[64,2048]{1,0:T(8,128)(2,1)}, u32[]{:S(2)}, u32[]{:S(2)}) collective-permute-start(bf16[64,2048]{1,0:T(8,128)(2,1)} %get-tuple-element.79.refs_1_), channel_id=1, source_target_pairs={{0,4},{1,5},{4,8},{5,9},{8,12},{9,13},{12,14},{13,15},{14,10},{15,... | collective-permute-start | bytes 786440 | tf_op jit(solution)/shard_map/ppermute | solution.py:462
  13.6 1.7 %collective-permute-start.7 = (bf16[64,2048]{1,0:T(8,128)(2,1)}, bf16[64,2048]{1,0:T(8,128)(2,1)}, u32[]{:S(2)}, u32[]{:S(2)}) collective-permute-start(bf16[64,2048]{1,0:T(8,128)(2,1)} %get-tuple-element.80), channel_id=1, source_target_pairs={{0,2},{1,3},{4,0},{5,1},{8,4},{9,5},{12,8},{13,9},{14,12},{15,13},... | collective-permute-start | bytes 786440 | tf_op jit(solution)/shard_map/ppermute | solution.py:462
  15.3 1.5 %collective-permute-start.3 = (bf16[72,2048]{1,0:T(8,128)(2,1)S(1)}, bf16[72,2048]{1,0:T(8,128)(2,1)S(1)}, u32[]{:S(2)}, u32[]{:S(2)}) collective-permute-start(bf16[72,2048]{1,0:T(8,128)(2,1)S(1)} %collective-permute-done.2.refs_0_), channel_id=1, source_target_pairs={{0,4},{1,5},{4,8},{5,9},{8,12},{9,13},{12,14},{13,15},{14,10},{15,... | collective-permute-start | bytes 884744 | tf_op jit(solution)/shard_map/ppermute | solution.py:462
  16.8 0.5 collective-permute-start.5
  17.4 2.9 %stage.1 = (bf16[384,2048]{1,0:T(8,128)(2,1)S(1)}, bf16[384,2048]{1,0:T(8,128)(2,1)S(1)}) custom-call(bf16[384,2048]{1,0:T(8,128)(2,1)} %collective-permute-done.refs_0_, bf16[384,2048]{1,0:T(8,128)(2,1)} %collective-permute-done.1.refs_1_), custom_call_target="tpu_custom_call" | custom-call | tf_op jit(solution)/shard_map/stage/pallas_call | solution.py:347
  20.4 1.0 copy-done.5
  21.3 4.0 %hidden.6 = (bf16[128,768]{1,0:T(8,128)(2,1)S(1)}, f32[384,384]{1,0:T(8,128)S(1)}, f32[384,384]{1,0:T(8,128)S(1)}) custom-call(s32[2]{0:T(128)S(1)} %pad_add_fusion.place_ref, bf16[72,2048]{1,0:T(8,128)(2,1)S(1)} %copy-done.5, bf16[64,2048]{1,0:T(8,128)(2,1)} %get-tuple-element.79.refs_1_, bf16[384,2048]{1,0:T(8,128)(2,1)S(1)} %bitcast.11, ...), custom_call_target="tpu_custom_call" | custom-call | flops 805306368 | bytes 6815744 | tf_op jit(solution)/shard_map/hidden/pallas_call | solution.py:243
  25.4 1.5 %collective-permute-start.10 = (bf16[64,2048]{1,0:T(8,128)(2,1)}, bf16[64,2048]{1,0:T(8,128)(2,1)S(1)}, u32[]{:S(2)}, u32[]{:S(2)}) collective-permute-start(bf16[64,2048]{1,0:T(8,128)(2,1)} %collective-permute-done.6.refs_1_), channel_id=1, source_target_pairs={{0,4},{1,5},{4,8},{5,9},{8,12},{9,13},{12,14},{13,15},{14,10},{15,... | collective-permute-start | bytes 786440 | tf_op jit(solution)/shard_map/ppermute | solution.py:462
  26.9 0.5 collective-permute-start.11
  27.4 4.1 %hidden.7 = (bf16[256,768]{1,0:T(8,128)(2,1)S(1)}, f32[384,384]{1,0:T(8,128)S(1)}, f32[384,384]{1,0:T(8,128)S(1)}) custom-call(s32[2]{0:T(128)S(1)} %pad_add_fusion.place_ref, bf16[72,2048]{1,0:T(8,128)(2,1)S(1)} %collective-permute-done.2.refs_0_, bf16[64,2048]{1,0:T(8,128)(2,1)} %collective-permute-done.6.refs_1_, ...), custom_call_target="tpu_custom_call" | custom-call | flops 1610612736 | bytes 7340032 | tf_op jit(solution)/shard_map/hidden/pallas_call | solution.py:243
  31.6 1.5 %collective-permute-start.8 = (bf16[72,2048]{1,0:T(8,128)(2,1)S(1)}, bf16[72,2048]{1,0:T(8,128)(2,1)S(1)}, u32[]{:S(2)}, u32[]{:S(2)}) collective-permute-start(bf16[72,2048]{1,0:T(8,128)(2,1)S(1)} %collective-permute-done.3.refs_0_), channel_id=1, source_target_pairs={{0,4},{1,5},{4,8},{5,9},{8,12},{9,13},{12,14},{13,15},{14,10},{15,... | collective-permute-start | bytes 884744 | tf_op jit(solution)/shard_map/ppermute | solution.py:462
  33.1 0.5 collective-permute-start.9
  33.7 1.5 %collective-permute-start.14 = (bf16[64,2048]{1,0:T(8,128)(2,1)S(1)}, bf16[64,2048]{1,0:T(8,128)(2,1)S(1)}, u32[]{:S(2)}, u32[]{:S(2)}) collective-permute-start(bf16[64,2048]{1,0:T(8,128)(2,1)S(1)} %collective-permute-done.10.refs_1_), channel_id=1, source_target_pairs={{0,4},{1,5},{4,8},{5,9},{8,12},{9,13},{12,14},{13,15},{14,10},{15,... | collective-permute-start | bytes 786440 | tf_op jit(solution)/shard_map/ppermute | solution.py:462
  35.2 0.8 collective-permute-start.15
  35.9 3.6 %hidden.8 = (bf16[256,768]{1,0:T(8,128)(2,1)S(1)}, f32[384,384]{1,0:T(8,128)S(1)}, f32[384,384]{1,0:T(8,128)S(1)}) custom-call(s32[2]{0:T(128)S(1)} %pad_add_fusion.place_ref, bf16[72,2048]{1,0:T(8,128)(2,1)S(1)} %collective-permute-done.3.refs_0_, bf16[64,2048]{1,0:T(8,128)(2,1)S(1)} %collective-permute-done.10.refs_1_, ...), custom_call_target="tpu_custom_call" | custom-call | flops 1610612736 | bytes 7340032 | tf_op jit(solution)/shard_map/hidden/pallas_call | solution.py:243
  39.5 2.1 %collective-permute-done.8.refs_0_ = bf16[72,2048]{1,0:T(8,128)(2,1)S(1)} collective-permute-done((bf16[72,2048]{1,0:T(8,128)(2,1)S(1)}, bf16[72,2048]{1,0:T(8,128)(2,1)S(1)}, u32[]{:S(2)}, u32[]{:S(2)}) %collective-permute-start.8) | collective-permute-done | bytes 294944 | tf_op jit(solution)/shard_map/ppermute | solution.py:462
  41.6 1.5 %collective-permute-done.9.refs_3_ = bf16[72,2048]{1,0:T(8,128)(2,1)S(1)} collective-permute-done((bf16[72,2048]{1,0:T(8,128)(2,1)S(1)}, bf16[72,2048]{1,0:T(8,128)(2,1)S(1)}, u32[]{:S(2)}, u32[]{:S(2)}) %collective-permute-start.9) | collective-permute-done | bytes 294944 | tf_op jit(solution)/shard_map/ppermute | solution.py:462
  43.1 1.6 %collective-permute-start.12 = (bf16[72,2048]{1,0:T(8,128)(2,1)S(1)}, bf16[72,2048]{1,0:T(8,128)(2,1)S(1)}, u32[]{:S(2)}, u32[]{:S(2)}) collective-permute-start(bf16[72,2048]{1,0:T(8,128)(2,1)S(1)} %collective-permute-done.8.refs_0_), channel_id=1, source_target_pairs={{0,4},{1,5},{4,8},{5,9},{8,12},{9,13},{12,14},{13,15},{14,10},{15,... | collective-permute-start | bytes 884744 | tf_op jit(solution)/shard_map/ppermute | solution.py:462
  45.1 2.1 %collective-permute-done.14.refs_1_ = bf16[64,2048]{1,0:T(8,128)(2,1)S(1)} collective-permute-done((bf16[64,2048]{1,0:T(8,128)(2,1)S(1)}, bf16[64,2048]{1,0:T(8,128)(2,1)S(1)}, u32[]{:S(2)}, u32[]{:S(2)}) %collective-permute-start.14) | collective-permute-done | bytes 262176 | tf_op jit(solution)/shard_map/ppermute | solution.py:462
  47.2 1.4 %collective-permute-done.15.refs_2_ = bf16[64,2048]{1,0:T(8,128)(2,1)S(1)} collective-permute-done((bf16[64,2048]{1,0:T(8,128)(2,1)S(1)}, bf16[64,2048]{1,0:T(8,128)(2,1)S(1)}, u32[]{:S(2)}, u32[]{:S(2)}) %collective-permute-start.15) | collective-permute-done | bytes 262176 | tf_op jit(solution)/shard_map/ppermute | solution.py:462
  48.6 3.6 %hidden.9 = (bf16[256,768]{1,0:T(8,128)(2,1)S(1)}, f32[384,384]{1,0:T(8,128)S(1)}, f32[384,384]{1,0:T(8,128)S(1)}) custom-call(s32[2]{0:T(128)S(1)} %pad_add_fusion.place_ref, bf16[72,2048]{1,0:T(8,128)(2,1)S(1)} %collective-permute-done.8.refs_0_, bf16[64,2048]{1,0:T(8,128)(2,1)S(1)} %collective-permute-done.14.refs_1_, ...), custom_call_target="tpu_custom_call" | custom-call | flops 1610612736 | bytes 7340032 | tf_op jit(solution)/shard_map/hidden/pallas_call | solution.py:243
  52.2 2.0 %hidden.11 = (bf16[128,384]{1,0:T(8,128)(2,1)S(1)}, f32[384,384]{1,0:T(8,128)S(1)}) custom-call(s32[2]{0:T(128)S(1)} %pad_add_fusion.place_ref, bf16[72,2048]{1,0:T(8,128)(2,1)S(1)} %collective-permute-done.12.refs_0_, bf16[72,2048]{1,0:T(8,128)(2,1)S(1)} %collective-permute-done.13.refs_1_, bf16[384,2048]{1,0:T(8,128)(2,1)S(1)} %get-tuple-element.72.refs_4_.refs_6_.refs_2_, ...), custom_call_target="tpu_custom_call" | custom-call | flops 402653184 | bytes 3670016 | tf_op jit(solution)/shard_map/hidden/pallas_call | solution.py:243
  54.3 2.0 %hidden.10 = (bf16[128,384]{1,0:T(8,128)(2,1)S(1)}, f32[384,384]{1,0:T(8,128)S(1)}) custom-call(s32[2]{0:T(128)S(1)} %pad_add_fusion.place_ref, bf16[72,2048]{1,0:T(8,128)(2,1)S(1)} %collective-permute-done.12.refs_0_, bf16[72,2048]{1,0:T(8,128)(2,1)S(1)} %collective-permute-done.13.refs_1_, bf16[384,2048]{1,0:T(8,128)(2,1)S(1)} %bitcast.15, ...), custom_call_target="tpu_custom_call" | custom-call | flops 402653184 | bytes 3670016 | tf_op jit(solution)/shard_map/hidden/pallas_call | solution.py:243
  56.3 2.6 %prune.1 = (bf16[384,1024]{1,0:T(8,128)(2,1)S(1)}, bf16[384,384]{1,0:T(8,128)(2,1)S(1)}) custom-call(f32[384,384]{1,0:T(8,128)S(1)} %get-tuple-element.102.own_ref, f32[384,384]{1,0:T(8,128)S(1)} %collective-permute-done.16.other_ref, bf16[384,2048]{1,0:T(8,128)(2,1)S(1)} %get-tuple-element.105.error_ref, bf16[384,2048]{1,0:T(8,128)(2,1)S(1)} %bitcast.23, ...), custom_call_target="tpu_custom_call" | custom-call | flops 981467136 | bytes 4325376 | tf_op jit(solution)/shard_map/prune/pallas_call | solution.py:308
  58.9 0.6 collective-permute-start.26
  59.5 0.6 prune_next.1.own_ref
  60.2 1.2 %collective-permute-done.26.other_ref = bf16[384,1024]{1,0:T(8,128)(2,1)S(1)} collective-permute-done((bf16[384,1024]{1,0:T(8,128)(2,1)S(1)}, bf16[384,1024]{1,0:T(8,128)(2,1)S(1)}, u32[]{:S(2)}, u32[]{:S(2)}) %collective-permute-start.26) | collective-permute-done | bytes 786464 | tf_op jit(solution)/shard_map/ppermute | solution.py:465
  61.4 0.5 outputs.12
  61.8 1.0 collective-permute-start.27
  62.9 1.0 collective-permute-start.28
  64.4 1.0 collective-permute-start.18
  65.4 1.0 collective-permute-start.19
  66.5 1.7 %collective-permute-done.27.refs_0_ = bf16[64,1024]{1,0:T(8,128)(2,1)S(1)} collective-permute-done((bf16[64,1024]{1,0:T(8,128)(2,1)S(1)}, bf16[64,1024]{1,0:T(8,128)(2,1)S(1)}, u32[]{:S(2)}, u32[]{:S(2)}) %collective-permute-start.27) | collective-permute-done | bytes 131104 | tf_op jit(solution)/shard_map/ppermute | solution.py:462
  68.2 1.0 collective-permute-done.28.refs_1_
  69.2 0.7 outputs.13
  69.9 1.6 %collective-permute-start.29 = (bf16[128,1024]{1,0:T(8,128)(2,1)S(1)}, bf16[128,1024]{1,0:T(8,128)(2,1)S(1)}, u32[]{:S(2)}, u32[]{:S(2)}) collective-permute-start(bf16[128,1024]{1,0:T(8,128)(2,1)S(1)} %get-tuple-element.124), channel_id=1, source_target_pairs={{0,2},{1,3},{4,0},{5,1},{8,4},{9,5},{12,8},{13,9},{14,12},{15,13},... | collective-permute-start | bytes 786440 | tf_op jit(solution)/shard_map/ppermute | solution.py:462
  72.0 0.7 outputs.9
  72.7 1.6 %collective-permute-start.20 = (bf16[128,1024]{1,0:T(8,128)(2,1)S(1)}, bf16[128,1024]{1,0:T(8,128)(2,1)S(1)}, u32[]{:S(2)}, u32[]{:S(2)}) collective-permute-start(bf16[128,1024]{1,0:T(8,128)(2,1)S(1)} %get-tuple-element.115), channel_id=1, source_target_pairs={{0,2},{1,3},{4,0},{5,1},{8,4},{9,5},{12,8},{13,9},{14,12},{15,13},... | collective-permute-start | bytes 786440 | tf_op jit(solution)/shard_map/ppermute | solution.py:462
  74.8 4.4 %collective-permute-done.29.refs_0_ = bf16[128,1024]{1,0:T(8,128)(2,1)S(1)} collective-permute-done((bf16[128,1024]{1,0:T(8,128)(2,1)S(1)}, bf16[128,1024]{1,0:T(8,128)(2,1)S(1)}, u32[]{:S(2)}, u32[]{:S(2)}) %collective-permute-start.29) | collective-permute-done | bytes 262176 | tf_op jit(solution)/shard_map/ppermute | solution.py:462
  79.2 1.5 %collective-permute-done.30.refs_1_ = bf16[128,1024]{1,0:T(8,128)(2,1)S(1)} collective-permute-done((bf16[128,1024]{1,0:T(8,128)(2,1)S(1)}, bf16[128,1024]{1,0:T(8,128)(2,1)S(1)}, u32[]{:S(2)}, u32[]{:S(2)}) %collective-permute-start.30) | collective-permute-done | bytes 262176 | tf_op jit(solution)/shard_map/ppermute | solution.py:462
  80.6 0.7 outputs.14
  81.3 1.6 %collective-permute-start.31 = (bf16[128,1024]{1,0:T(8,128)(2,1)S(1)}, bf16[128,1024]{1,0:T(8,128)(2,1)S(1)}, u32[]{:S(2)}, u32[]{:S(2)}) collective-permute-start(bf16[128,1024]{1,0:T(8,128)(2,1)S(1)} %get-tuple-element.126), channel_id=1, source_target_pairs={{0,2},{1,3},{4,0},{5,1},{8,4},{9,5},{12,8},{13,9},{14,12},{15,13},... | collective-permute-start | bytes 786440 | tf_op jit(solution)/shard_map/ppermute | solution.py:462
  83.4 1.4 %collective-permute-done.20.refs_0_ = bf16[128,1024]{1,0:T(8,128)(2,1)S(1)} collective-permute-done((bf16[128,1024]{1,0:T(8,128)(2,1)S(1)}, bf16[128,1024]{1,0:T(8,128)(2,1)S(1)}, u32[]{:S(2)}, u32[]{:S(2)}) %collective-permute-start.20) | collective-permute-done | bytes 262176 | tf_op jit(solution)/shard_map/ppermute | solution.py:462
  84.8 1.5 %collective-permute-done.21.refs_1_ = bf16[128,1024]{1,0:T(8,128)(2,1)S(1)} collective-permute-done((bf16[128,1024]{1,0:T(8,128)(2,1)S(1)}, bf16[128,1024]{1,0:T(8,128)(2,1)S(1)}, u32[]{:S(2)}, u32[]{:S(2)}) %collective-permute-start.21) | collective-permute-done | bytes 262176 | tf_op jit(solution)/shard_map/ppermute | solution.py:462
  86.3 0.7 outputs.10
  87.0 1.6 %collective-permute-start.22 = (bf16[128,1024]{1,0:T(8,128)(2,1)S(1)}, bf16[128,1024]{1,0:T(8,128)(2,1)S(1)}, u32[]{:S(2)}, u32[]{:S(2)}) collective-permute-start(bf16[128,1024]{1,0:T(8,128)(2,1)S(1)} %get-tuple-element.117), channel_id=1, source_target_pairs={{0,2},{1,3},{4,0},{5,1},{8,4},{9,5},{12,8},{13,9},{14,12},{15,13},... | collective-permute-start | bytes 786440 | tf_op jit(solution)/shard_map/ppermute | solution.py:462
  89.0 1.6 %collective-permute-done.31.refs_0_ = bf16[128,1024]{1,0:T(8,128)(2,1)S(1)} collective-permute-done((bf16[128,1024]{1,0:T(8,128)(2,1)S(1)}, bf16[128,1024]{1,0:T(8,128)(2,1)S(1)}, u32[]{:S(2)}, u32[]{:S(2)}) %collective-permute-start.31) | collective-permute-done | bytes 262176 | tf_op jit(solution)/shard_map/ppermute | solution.py:462
  90.6 1.6 %collective-permute-done.32.refs_1_ = bf16[128,1024]{1,0:T(8,128)(2,1)S(1)} collective-permute-done((bf16[128,1024]{1,0:T(8,128)(2,1)S(1)}, bf16[128,1024]{1,0:T(8,128)(2,1)S(1)}, u32[]{:S(2)}, u32[]{:S(2)}) %collective-permute-start.32) | collective-permute-done | bytes 262176 | tf_op jit(solution)/shard_map/ppermute | solution.py:462
  92.2 0.7 outputs.15
  92.9 1.6 %collective-permute-start.33 = (bf16[128,1024]{1,0:T(8,128)(2,1)S(1)}, bf16[128,1024]{1,0:T(8,128)(2,1)S(1)}, u32[]{:S(2)}, u32[]{:S(2)}) collective-permute-start(bf16[128,1024]{1,0:T(8,128)(2,1)S(1)} %get-tuple-element.128), channel_id=1, source_target_pairs={{0,2},{1,3},{4,0},{5,1},{8,4},{9,5},{12,8},{13,9},{14,12},{15,13},... | collective-permute-start | bytes 786440 | tf_op jit(solution)/shard_map/ppermute | solution.py:462
  95.0 1.2 %collective-permute-done.22.refs_0_ = bf16[128,1024]{1,0:T(8,128)(2,1)S(1)} collective-permute-done((bf16[128,1024]{1,0:T(8,128)(2,1)S(1)}, bf16[128,1024]{1,0:T(8,128)(2,1)S(1)}, u32[]{:S(2)}, u32[]{:S(2)}) %collective-permute-start.22) | collective-permute-done | bytes 262176 | tf_op jit(solution)/shard_map/ppermute | solution.py:462
  96.3 1.6 %collective-permute-done.23.refs_1_ = bf16[128,1024]{1,0:T(8,128)(2,1)S(1)} collective-permute-done((bf16[128,1024]{1,0:T(8,128)(2,1)S(1)}, bf16[128,1024]{1,0:T(8,128)(2,1)S(1)}, u32[]{:S(2)}, u32[]{:S(2)}) %collective-permute-start.23) | collective-permute-done | bytes 262176 | tf_op jit(solution)/shard_map/ppermute | solution.py:462
  97.8 0.7 outputs.11
  98.6 1.6 %collective-permute-start.24 = (bf16[128,1024]{1,0:T(8,128)(2,1)S(1)}, bf16[128,1024]{1,0:T(8,128)(2,1)S(1)}, u32[]{:S(2)}, u32[]{:S(2)}) collective-permute-start(bf16[128,1024]{1,0:T(8,128)(2,1)S(1)} %get-tuple-element.119), channel_id=1, source_target_pairs={{0,2},{1,3},{4,0},{5,1},{8,4},{9,5},{12,8},{13,9},{14,12},{15,13},... | collective-permute-start | bytes 786440 | tf_op jit(solution)/shard_map/ppermute | solution.py:462
  100.6 1.3 %maximum_bitcast_fusion = bf16[1,384,2048]{2,1,0:T(8,128)(2,1)} fusion(bf16[384,1024]{1,0:T(8,128)(2,1)S(1)} %prune_next.1.own_ref, bf16[384,1024]{1,0:T(8,128)(2,1)S(1)} %get-tuple-element.121.own_ref), kind=kLoop, calls=%fused_computation | loop fusion | flops 3145728 | bytes 3145728 | tf_op jit(solution)/shard_map/broadcast_in_dim | solution.py:531
  103.2 0.8 finish.2.refs_0_
  104.0 1.0 collective-permute-done.24.right_ref
  105.0 1.6 %collective-permute-done.25.left_ref = bf16[128,1024]{1,0:T(8,128)(2,1)S(1)} collective-permute-done((bf16[128,1024]{1,0:T(8,128)(2,1)S(1)}, bf16[128,1024]{1,0:T(8,128)(2,1)S(1)}, u32[]{:S(2)}, u32[]{:S(2)}) %collective-permute-start.25) | collective-permute-done | bytes 262176 | tf_op jit(solution)/shard_map/ppermute | solution.py:462
  106.6 0.8 finish.3
  (43 shorter events, 5.9 us)
Async XLA Ops:
  2.7 14.1 %collective-permute-start = (bf16[384,2048]{1,0:T(8,128)(2,1)}, bf16[384,2048]{1,0:T(8,128)(2,1)}, u32[]{:S(2)}, u32[]{:S(2)}) collective-permute-start(bf16[384,2048]{1,0:T(8,128)(2,1)} %bitcast.10), channel_id=1, source_target_pairs={{0,1},{1,0},{2,3},{3,2},{4,5},{5,4},{6,7},{7,6},{8,9},{9,8},{10,11... | collective-permute-start | bytes 4718600 | tf_op jit(solution)/shard_map/ppermute | solution.py:465
  3.2 14.2 %collective-permute-start.1 = (bf16[384,2048]{1,0:T(8,128)(2,1)}, bf16[384,2048]{1,0:T(8,128)(2,1)}, u32[]{:S(2)}, u32[]{:S(2)}) collective-permute-start(bf16[384,2048]{1,0:T(8,128)(2,1)} %bitcast.16), channel_id=1, source_target_pairs={{0,1},{1,0},{2,3},{3,2},{4,5},{5,4},{6,7},{7,6},{8,9},{9,8},{10,11... | collective-permute-start | bytes 4718600 | tf_op jit(solution)/shard_map/ppermute | solution.py:465
  3.3 10.3 %collective-permute-start.2 = (bf16[72,2048]{1,0:T(8,128)(2,1)}, bf16[72,2048]{1,0:T(8,128)(2,1)S(1)}, u32[]{:S(2)}, u32[]{:S(2)}) collective-permute-start(bf16[72,2048]{1,0:T(8,128)(2,1)} %get-tuple-element.68.refs_0_), channel_id=1, source_target_pairs={{0,4},{1,5},{4,8},{5,9},{8,12},{9,13},{12,14},{13,15},{14,10},{15,... | collective-permute-start | bytes 884744 | tf_op jit(solution)/shard_map/ppermute | solution.py:462
  6.3 9.0 %collective-permute-start.4 = (bf16[72,2048]{1,0:T(8,128)(2,1)}, bf16[72,2048]{1,0:T(8,128)(2,1)}, u32[]{:S(2)}, u32[]{:S(2)}) collective-permute-start(bf16[72,2048]{1,0:T(8,128)(2,1)} %get-tuple-element.75), channel_id=1, source_target_pairs={{0,2},{1,3},{4,0},{5,1},{8,4},{9,5},{12,8},{13,9},{14,12},{15,13},... | collective-permute-start | bytes 884744 | tf_op jit(solution)/shard_map/ppermute | solution.py:462
  6.3 1.4 %copy-start.2 = (bf16[1,384,2048]{2,1,0:T(8,128)(2,1)S(1)}, bf16[1,384,2048]{2,1,0:T(8,128)(2,1)}, u32[]{:S(2)}) copy-start(bf16[1,384,2048]{2,1,0:T(8,128)(2,1)} %param.12) | copy-start | bytes 4718596
  7.7 1.1 %copy-start.4 = (s32[1,96,2048]{2,1,0:T(8,128)S(1)}, s32[1,96,2048]{2,1,0:T(8,128)}, u32[]{:S(2)}) copy-start(s32[1,96,2048]{2,1,0:T(8,128)} %param.13) | copy-start | bytes 2359300
  11.2 14.1 %collective-permute-start.6 = (bf16[64,2048]{1,0:T(8,128)(2,1)}, bf16[64,2048]{1,0:T(8,128)(2,1)}, u32[]{:S(2)}, u32[]{:S(2)}) collective-permute-start(bf16[64,2048]{1,0:T(8,128)(2,1)} %get-tuple-element.79.refs_1_), channel_id=1, source_target_pairs={{0,4},{1,5},{4,8},{5,9},{8,12},{9,13},{12,14},{13,15},{14,10},{15,... | collective-permute-start | bytes 786440 | tf_op jit(solution)/shard_map/ppermute | solution.py:462
  13.6 11.8 %collective-permute-start.7 = (bf16[64,2048]{1,0:T(8,128)(2,1)}, bf16[64,2048]{1,0:T(8,128)(2,1)}, u32[]{:S(2)}, u32[]{:S(2)}) collective-permute-start(bf16[64,2048]{1,0:T(8,128)(2,1)} %get-tuple-element.80), channel_id=1, source_target_pairs={{0,2},{1,3},{4,0},{5,1},{8,4},{9,5},{12,8},{13,9},{14,12},{15,13},... | collective-permute-start | bytes 786440 | tf_op jit(solution)/shard_map/ppermute | solution.py:462
  15.3 16.3 %collective-permute-start.3 = (bf16[72,2048]{1,0:T(8,128)(2,1)S(1)}, bf16[72,2048]{1,0:T(8,128)(2,1)S(1)}, u32[]{:S(2)}, u32[]{:S(2)}) collective-permute-start(bf16[72,2048]{1,0:T(8,128)(2,1)S(1)} %collective-permute-done.2.refs_0_), channel_id=1, source_target_pairs={{0,4},{1,5},{4,8},{5,9},{8,12},{9,13},{12,14},{13,15},{14,10},{15,... | collective-permute-start | bytes 884744 | tf_op jit(solution)/shard_map/ppermute | solution.py:462
  16.8 14.8 %collective-permute-start.5 = (bf16[72,2048]{1,0:T(8,128)(2,1)}, bf16[72,2048]{1,0:T(8,128)(2,1)S(1)}, u32[]{:S(2)}, u32[]{:S(2)}) collective-permute-start(bf16[72,2048]{1,0:T(8,128)(2,1)} %collective-permute-done.4.refs_3_), channel_id=1, source_target_pairs={{0,2},{1,3},{4,0},{5,1},{8,4},{9,5},{12,8},{13,9},{14,12},{15,13},... | collective-permute-start | bytes 884744 | tf_op jit(solution)/shard_map/ppermute | solution.py:462
  17.4 2.9 %copy-start = (bf16[1,384,2048]{2,1,0:T(8,128)(2,1)S(1)}, bf16[1,384,2048]{2,1,0:T(8,128)(2,1)}, u32[]{:S(2)}) copy-start(bf16[1,384,2048]{2,1,0:T(8,128)(2,1)} %param.10) | copy-start | bytes 4718596
  17.4 2.9 %copy-start.1 = (bf16[1,384,2048]{2,1,0:T(8,128)(2,1)S(1)}, bf16[1,384,2048]{2,1,0:T(8,128)(2,1)}, u32[]{:S(2)}) copy-start(bf16[1,384,2048]{2,1,0:T(8,128)(2,1)} %param.11) | copy-start | bytes 4718596
  20.4 1.0 copy-start.5
  25.4 8.3 %collective-permute-start.10 = (bf16[64,2048]{1,0:T(8,128)(2,1)}, bf16[64,2048]{1,0:T(8,128)(2,1)S(1)}, u32[]{:S(2)}, u32[]{:S(2)}) collective-permute-start(bf16[64,2048]{1,0:T(8,128)(2,1)} %collective-permute-done.6.refs_1_), channel_id=1, source_target_pairs={{0,4},{1,5},{4,8},{5,9},{8,12},{9,13},{12,14},{13,15},{14,10},{15,... | collective-permute-start | bytes 786440 | tf_op jit(solution)/shard_map/ppermute | solution.py:462
  26.9 8.3 %collective-permute-start.11 = (bf16[64,2048]{1,0:T(8,128)(2,1)}, bf16[64,2048]{1,0:T(8,128)(2,1)S(1)}, u32[]{:S(2)}, u32[]{:S(2)}) collective-permute-start(bf16[64,2048]{1,0:T(8,128)(2,1)} %collective-permute-done.7.refs_2_), channel_id=1, source_target_pairs={{0,2},{1,3},{4,0},{5,1},{8,4},{9,5},{12,8},{13,9},{14,12},{15,13},... | collective-permute-start | bytes 786440 | tf_op jit(solution)/shard_map/ppermute | solution.py:462
  31.6 10.0 %collective-permute-start.8 = (bf16[72,2048]{1,0:T(8,128)(2,1)S(1)}, bf16[72,2048]{1,0:T(8,128)(2,1)S(1)}, u32[]{:S(2)}, u32[]{:S(2)}) collective-permute-start(bf16[72,2048]{1,0:T(8,128)(2,1)S(1)} %collective-permute-done.3.refs_0_), channel_id=1, source_target_pairs={{0,4},{1,5},{4,8},{5,9},{8,12},{9,13},{12,14},{13,15},{14,10},{15,... | collective-permute-start | bytes 884744 | tf_op jit(solution)/shard_map/ppermute | solution.py:462
  33.1 9.9 %collective-permute-start.9 = (bf16[72,2048]{1,0:T(8,128)(2,1)S(1)}, bf16[72,2048]{1,0:T(8,128)(2,1)S(1)}, u32[]{:S(2)}, u32[]{:S(2)}) collective-permute-start(bf16[72,2048]{1,0:T(8,128)(2,1)S(1)} %collective-permute-done.5.refs_3_), channel_id=1, source_target_pairs={{0,2},{1,3},{4,0},{5,1},{8,4},{9,5},{12,8},{13,9},{14,12},{15,13},... | collective-permute-start | bytes 884744 | tf_op jit(solution)/shard_map/ppermute | solution.py:462
  33.7 13.5 %collective-permute-start.14 = (bf16[64,2048]{1,0:T(8,128)(2,1)S(1)}, bf16[64,2048]{1,0:T(8,128)(2,1)S(1)}, u32[]{:S(2)}, u32[]{:S(2)}) collective-permute-start(bf16[64,2048]{1,0:T(8,128)(2,1)S(1)} %collective-permute-done.10.refs_1_), channel_id=1, source_target_pairs={{0,4},{1,5},{4,8},{5,9},{8,12},{9,13},{12,14},{13,15},{14,10},{15,... | collective-permute-start | bytes 786440 | tf_op jit(solution)/shard_map/ppermute | solution.py:462
  35.2 13.4 %collective-permute-start.15 = (bf16[64,2048]{1,0:T(8,128)(2,1)S(1)}, bf16[64,2048]{1,0:T(8,128)(2,1)S(1)}, u32[]{:S(2)}, u32[]{:S(2)}) collective-permute-start(bf16[64,2048]{1,0:T(8,128)(2,1)S(1)} %collective-permute-done.11.refs_2_), channel_id=1, source_target_pairs={{0,2},{1,3},{4,0},{5,1},{8,4},{9,5},{12,8},{13,9},{14,12},{15,13},... | collective-permute-start | bytes 786440 | tf_op jit(solution)/shard_map/ppermute | solution.py:462
  43.1 9.1 %collective-permute-start.12 = (bf16[72,2048]{1,0:T(8,128)(2,1)S(1)}, bf16[72,2048]{1,0:T(8,128)(2,1)S(1)}, u32[]{:S(2)}, u32[]{:S(2)}) collective-permute-start(bf16[72,2048]{1,0:T(8,128)(2,1)S(1)} %collective-permute-done.8.refs_0_), channel_id=1, source_target_pairs={{0,4},{1,5},{4,8},{5,9},{8,12},{9,13},{12,14},{13,15},{14,10},{15,... | collective-permute-start | bytes 884744 | tf_op jit(solution)/shard_map/ppermute | solution.py:462
  44.7 7.5 %collective-permute-start.13 = (bf16[72,2048]{1,0:T(8,128)(2,1)S(1)}, bf16[72,2048]{1,0:T(8,128)(2,1)S(1)}, u32[]{:S(2)}, u32[]{:S(2)}) collective-permute-start(bf16[72,2048]{1,0:T(8,128)(2,1)S(1)} %collective-permute-done.9.refs_3_), channel_id=1, source_target_pairs={{0,2},{1,3},{4,0},{5,1},{8,4},{9,5},{12,8},{13,9},{14,12},{15,13},... | collective-permute-start | bytes 884744 | tf_op jit(solution)/shard_map/ppermute | solution.py:462
  54.2 2.1 %copy-start.3 = (bf16[1,384,2048]{2,1,0:T(8,128)(2,1)S(1)}, bf16[1,384,2048]{2,1,0:T(8,128)(2,1)}, u32[]{:S(2)}) copy-start(bf16[1,384,2048]{2,1,0:T(8,128)(2,1)} %param.12) | copy-start | bytes 4718596
  54.2 2.1 %collective-permute-start.16 = (f32[384,384]{1,0:T(8,128)S(1)}, f32[384,384]{1,0:T(8,128)S(1)}, u32[]{:S(2)}, u32[]{:S(2)}) collective-permute-start(f32[384,384]{1,0:T(8,128)S(1)} %get-tuple-element.104), channel_id=1, source_target_pairs={{0,1},{1,0},{2,3},{3,2},{4,5},{5,4},{6,7},{7,6},{8,9},{9,8},{10,11... | collective-permute-start | bytes 1769480 | tf_op jit(solution)/shard_map/ppermute | solution.py:465
  58.9 2.5 %collective-permute-start.26 = (bf16[384,1024]{1,0:T(8,128)(2,1)S(1)}, bf16[384,1024]{1,0:T(8,128)(2,1)S(1)}, u32[]{:S(2)}, u32[]{:S(2)}) collective-permute-start(bf16[384,1024]{1,0:T(8,128)(2,1)S(1)} %get-tuple-element.121.own_ref), channel_id=1, source_target_pairs={{0,1},{1,0},{2,3},{3,2},{4,5},{5,4},{6,7},{7,6},{8,9},{9,8},{10,11... | collective-permute-start | bytes 2359304 | tf_op jit(solution)/shard_map/ppermute | solution.py:465
  60.1 3.8 %collective-permute-start.17 = (bf16[384,1024]{1,0:T(8,128)(2,1)S(1)}, bf16[384,1024]{1,0:T(8,128)(2,1)S(1)}, u32[]{:S(2)}, u32[]{:S(2)}) collective-permute-start(bf16[384,1024]{1,0:T(8,128)(2,1)S(1)} %prune_next.1.own_ref), channel_id=1, source_target_pairs={{0,1},{1,0},{2,3},{3,2},{4,5},{5,4},{6,7},{7,6},{8,9},{9,8},{10,11... | collective-permute-start | bytes 2359304 | tf_op jit(solution)/shard_map/ppermute | solution.py:465
  61.8 6.4 %collective-permute-start.27 = (bf16[64,1024]{1,0:T(8,128)(2,1)S(1)}, bf16[64,1024]{1,0:T(8,128)(2,1)S(1)}, u32[]{:S(2)}, u32[]{:S(2)}) collective-permute-start(bf16[64,1024]{1,0:T(8,128)(2,1)S(1)} %get-tuple-element.122), channel_id=1, source_target_pairs={{0,2},{1,3},{4,0},{5,1},{8,4},{9,5},{12,8},{13,9},{14,12},{15,13},... | collective-permute-start | bytes 393224 | tf_op jit(solution)/shard_map/ppermute | solution.py:462
  62.9 6.3 %collective-permute-start.28 = (bf16[64,1024]{1,0:T(8,128)(2,1)S(1)}, bf16[64,1024]{1,0:T(8,128)(2,1)S(1)}, u32[]{:S(2)}, u32[]{:S(2)}) collective-permute-start(bf16[64,1024]{1,0:T(8,128)(2,1)S(1)} %get-tuple-element.123), channel_id=1, source_target_pairs={{0,4},{1,5},{4,8},{5,9},{8,12},{9,13},{12,14},{13,15},{14,10},{15,... | collective-permute-start | bytes 393224 | tf_op jit(solution)/shard_map/ppermute | solution.py:462
  64.4 7.6 %collective-permute-start.18 = (bf16[64,1024]{1,0:T(8,128)(2,1)S(1)}, bf16[64,1024]{1,0:T(8,128)(2,1)S(1)}, u32[]{:S(2)}, u32[]{:S(2)}) collective-permute-start(bf16[64,1024]{1,0:T(8,128)(2,1)S(1)} %get-tuple-element.113), channel_id=1, source_target_pairs={{0,2},{1,3},{4,0},{5,1},{8,4},{9,5},{12,8},{13,9},{14,12},{15,13},... | collective-permute-start | bytes 393224 | tf_op jit(solution)/shard_map/ppermute | solution.py:462
  65.4 6.5 %collective-permute-start.19 = (bf16[64,1024]{1,0:T(8,128)(2,1)S(1)}, bf16[64,1024]{1,0:T(8,128)(2,1)S(1)}, u32[]{:S(2)}, u32[]{:S(2)}) collective-permute-start(bf16[64,1024]{1,0:T(8,128)(2,1)S(1)} %get-tuple-element.114), channel_id=1, source_target_pairs={{0,4},{1,5},{4,8},{5,9},{8,12},{9,13},{12,14},{13,15},{14,10},{15,... | collective-permute-start | bytes 393224 | tf_op jit(solution)/shard_map/ppermute | solution.py:462
  69.9 9.3 %collective-permute-start.29 = (bf16[128,1024]{1,0:T(8,128)(2,1)S(1)}, bf16[128,1024]{1,0:T(8,128)(2,1)S(1)}, u32[]{:S(2)}, u32[]{:S(2)}) collective-permute-start(bf16[128,1024]{1,0:T(8,128)(2,1)S(1)} %get-tuple-element.124), channel_id=1, source_target_pairs={{0,2},{1,3},{4,0},{5,1},{8,4},{9,5},{12,8},{13,9},{14,12},{15,13},... | collective-permute-start | bytes 786440 | tf_op jit(solution)/shard_map/ppermute | solution.py:462
  71.5 9.1 %collective-permute-start.30 = (bf16[128,1024]{1,0:T(8,128)(2,1)S(1)}, bf16[128,1024]{1,0:T(8,128)(2,1)S(1)}, u32[]{:S(2)}, u32[]{:S(2)}) collective-permute-start(bf16[128,1024]{1,0:T(8,128)(2,1)S(1)} %get-tuple-element.125), channel_id=1, source_target_pairs={{0,4},{1,5},{4,8},{5,9},{8,12},{9,13},{12,14},{13,15},{14,10},{15,... | collective-permute-start | bytes 786440 | tf_op jit(solution)/shard_map/ppermute | solution.py:462
  72.7 12.1 %collective-permute-start.20 = (bf16[128,1024]{1,0:T(8,128)(2,1)S(1)}, bf16[128,1024]{1,0:T(8,128)(2,1)S(1)}, u32[]{:S(2)}, u32[]{:S(2)}) collective-permute-start(bf16[128,1024]{1,0:T(8,128)(2,1)S(1)} %get-tuple-element.115), channel_id=1, source_target_pairs={{0,2},{1,3},{4,0},{5,1},{8,4},{9,5},{12,8},{13,9},{14,12},{15,13},... | collective-permute-start | bytes 786440 | tf_op jit(solution)/shard_map/ppermute | solution.py:462
  74.3 11.9 %collective-permute-start.21 = (bf16[128,1024]{1,0:T(8,128)(2,1)S(1)}, bf16[128,1024]{1,0:T(8,128)(2,1)S(1)}, u32[]{:S(2)}, u32[]{:S(2)}) collective-permute-start(bf16[128,1024]{1,0:T(8,128)(2,1)S(1)} %get-tuple-element.116), channel_id=1, source_target_pairs={{0,4},{1,5},{4,8},{5,9},{8,12},{9,13},{12,14},{13,15},{14,10},{15,... | collective-permute-start | bytes 786440 | tf_op jit(solution)/shard_map/ppermute | solution.py:462
  81.3 9.3 %collective-permute-start.31 = (bf16[128,1024]{1,0:T(8,128)(2,1)S(1)}, bf16[128,1024]{1,0:T(8,128)(2,1)S(1)}, u32[]{:S(2)}, u32[]{:S(2)}) collective-permute-start(bf16[128,1024]{1,0:T(8,128)(2,1)S(1)} %get-tuple-element.126), channel_id=1, source_target_pairs={{0,2},{1,3},{4,0},{5,1},{8,4},{9,5},{12,8},{13,9},{14,12},{15,13},... | collective-permute-start | bytes 786440 | tf_op jit(solution)/shard_map/ppermute | solution.py:462
  83.0 9.2 %collective-permute-start.32 = (bf16[128,1024]{1,0:T(8,128)(2,1)S(1)}, bf16[128,1024]{1,0:T(8,128)(2,1)S(1)}, u32[]{:S(2)}, u32[]{:S(2)}) collective-permute-start(bf16[128,1024]{1,0:T(8,128)(2,1)S(1)} %get-tuple-element.127), channel_id=1, source_target_pairs={{0,4},{1,5},{4,8},{5,9},{8,12},{9,13},{12,14},{13,15},{14,10},{15,... | collective-permute-start | bytes 786440 | tf_op jit(solution)/shard_map/ppermute | solution.py:462
  87.0 9.3 %collective-permute-start.22 = (bf16[128,1024]{1,0:T(8,128)(2,1)S(1)}, bf16[128,1024]{1,0:T(8,128)(2,1)S(1)}, u32[]{:S(2)}, u32[]{:S(2)}) collective-permute-start(bf16[128,1024]{1,0:T(8,128)(2,1)S(1)} %get-tuple-element.117), channel_id=1, source_target_pairs={{0,2},{1,3},{4,0},{5,1},{8,4},{9,5},{12,8},{13,9},{14,12},{15,13},... | collective-permute-start | bytes 786440 | tf_op jit(solution)/shard_map/ppermute | solution.py:462
  88.6 9.2 %collective-permute-start.23 = (bf16[128,1024]{1,0:T(8,128)(2,1)S(1)}, bf16[128,1024]{1,0:T(8,128)(2,1)S(1)}, u32[]{:S(2)}, u32[]{:S(2)}) collective-permute-start(bf16[128,1024]{1,0:T(8,128)(2,1)S(1)} %get-tuple-element.118), channel_id=1, source_target_pairs={{0,4},{1,5},{4,8},{5,9},{8,12},{9,13},{12,14},{13,15},{14,10},{15,... | collective-permute-start | bytes 786440 | tf_op jit(solution)/shard_map/ppermute | solution.py:462
  92.9 9.9 %collective-permute-start.33 = (bf16[128,1024]{1,0:T(8,128)(2,1)S(1)}, bf16[128,1024]{1,0:T(8,128)(2,1)S(1)}, u32[]{:S(2)}, u32[]{:S(2)}) collective-permute-start(bf16[128,1024]{1,0:T(8,128)(2,1)S(1)} %get-tuple-element.128), channel_id=1, source_target_pairs={{0,2},{1,3},{4,0},{5,1},{8,4},{9,5},{12,8},{13,9},{14,12},{15,13},... | collective-permute-start | bytes 786440 | tf_op jit(solution)/shard_map/ppermute | solution.py:462
  94.6 8.6 %collective-permute-start.34 = (bf16[128,1024]{1,0:T(8,128)(2,1)S(1)}, bf16[128,1024]{1,0:T(8,128)(2,1)S(1)}, u32[]{:S(2)}, u32[]{:S(2)}) collective-permute-start(bf16[128,1024]{1,0:T(8,128)(2,1)S(1)} %get-tuple-element.129), channel_id=1, source_target_pairs={{0,4},{1,5},{4,8},{5,9},{8,12},{9,13},{12,14},{13,15},{14,10},{15,... | collective-permute-start | bytes 786440 | tf_op jit(solution)/shard_map/ppermute | solution.py:462
  98.6 6.4 %collective-permute-start.24 = (bf16[128,1024]{1,0:T(8,128)(2,1)S(1)}, bf16[128,1024]{1,0:T(8,128)(2,1)S(1)}, u32[]{:S(2)}, u32[]{:S(2)}) collective-permute-start(bf16[128,1024]{1,0:T(8,128)(2,1)S(1)} %get-tuple-element.119), channel_id=1, source_target_pairs={{0,2},{1,3},{4,0},{5,1},{8,4},{9,5},{12,8},{13,9},{14,12},{15,13},... | collective-permute-start | bytes 786440 | tf_op jit(solution)/shard_map/ppermute | solution.py:462
  100.2 6.4 %collective-permute-start.25 = (bf16[128,1024]{1,0:T(8,128)(2,1)S(1)}, bf16[128,1024]{1,0:T(8,128)(2,1)S(1)}, u32[]{:S(2)}, u32[]{:S(2)}) collective-permute-start(bf16[128,1024]{1,0:T(8,128)(2,1)S(1)} %get-tuple-element.120), channel_id=1, source_target_pairs={{0,4},{1,5},{4,8},{5,9},{8,12},{9,13},{12,14},{13,15},{14,10},{15,... | collective-permute-start | bytes 786440 | tf_op jit(solution)/shard_map/ppermute | solution.py:462

commit v4 on v3

--- a/solution.py
+++ b/solution.py
@@ -179,20 +179,22 @@
     error_ref[...] = jnp.where(kept > 0.5, 0.0, down_ref[...].astype(F32)).astype(BF)
 
 
-def masks(code, down):
+def masks(code, down, cut, at, mib):
     groups, width = code.shape
     rows = down.shape[0]
-    cut = 512
-    spec = pl.BlockSpec((rows, cut), lambda i: (0, i))
+    step = cut // 2
+    first = at * 2
+    taken = pl.BlockSpec((rows, step), lambda i: (0, i + first))
+    given = pl.BlockSpec((rows, step), lambda i: (0, i))
     return pl.pallas_call(
         mask_kernel,
-        out_shape=[jax.ShapeDtypeStruct((rows, width), BF)] * 2,
-        grid=(width // cut,),
-        in_specs=[pl.BlockSpec((groups, cut), lambda i: (0, i)), spec],
-        out_specs=[spec, spec],
-        compiler_params=params("arbitrary"),
+        out_shape=[jax.ShapeDtypeStruct((rows, cut), BF)] * 2,
+        grid=(2,),
+        in_specs=[pl.BlockSpec((groups, step), lambda i: (0, i + first)), taken],
+        out_specs=[given, given],
+        compiler_params=params("arbitrary", mib=mib),
         cost_estimate=pl.CostEstimate(
-            flops=2 * rows * rows * width, bytes_accessed=8 * rows * width, transcendentals=0
+            flops=2 * rows * rows * cut, bytes_accessed=8 * rows * cut, transcendentals=0
         ),
         name="masks",
     )(code, down)
@@ -312,7 +314,7 @@
             jax.ShapeDtypeStruct((size, size), BF),
         ],
         grid=(1,),
-        in_specs=[square, square, half, half, half],
+        in_specs=[square, square, whole((size, cut)), half, whole((size, cut))],
         out_specs=[half, square],
         compiler_params=params("arbitrary"),
         cost_estimate=prune_cost(size, cut, 6),
@@ -327,7 +329,7 @@
         correct_kernel,
         out_shape=jax.ShapeDtypeStruct((size, cut), BF),
         grid=(1,),
-        in_specs=[whole((size, size)), half, half, half],
+        in_specs=[whole((size, size)), whole((size, cut)), half, whole((size, cut))],
         out_specs=whole((size, cut)),
         compiler_params=params("arbitrary"),
         cost_estimate=prune_cost(size, cut, 0),
@@ -489,21 +491,28 @@
         hidden.append(((value, 0), (value, 1)))
 
     hop_first(1)
-    kept, error = masks(code, down)
-    right[1], left[0], kept, error = tied((right[1], left[0], kept, error))
+    cut = width // 2
+    masked = [None, None]
+    right[1], left[0], *pairs[1] = tied((right[1], left[0], *pairs[1]))
     hop_second(1)
     hop_first(2)
     pairs[1] = stage(pairs[1])
-    work(0)
-    right[1], left[0], *grams = tied((right[1], left[0], *grams))
+    right[1], left[0], *_ = tied((right[1], left[0], *pairs[1]))
     hop_second(2)
     for hop in range(3, reach + 1):
-        work(hop - 2)
+        while len(hidden) < (1 if hop == 3 else hop - 1):
+            work(len(hidden))
         right[0], left[1], *grams = tied((right[0], left[1], *grams))
         hop_first(hop)
         if hop < reach:
+            while len(hidden) < hop - 1:
+                work(len(hidden))
+            right[1], left[0], *grams = tied((right[1], left[0], *grams))
             hop_second(hop)
-    work(reach - 1)
+    masked = [masks(code, down, cut, at, 16) for at in range(2)]
+    grams[0], *_ = tied((grams[0], *masked[0], *masked[1]))
+    while len(hidden) < reach:
+        work(len(hidden))
     grams = list(tied(tuple(grams)))
     last_other, gram_other = hidden_part(
         place, (1,), devices, *groups[reach], pairs[1:], grams[1:]
@@ -511,11 +520,11 @@
     gram_other = swap(gram_other)
     last_own, gram_own = hidden_part(place, (0,), devices, *groups[reach], pairs[:1], grams[:1])
     hidden.append(((last_own, 0), (last_other, 0)))
-    cut = width // 2
     pruned = [None, None]
+    (kept, error), (kept_next, error_next) = masked
     pruned[0], inverse = prune_first(gram_own, gram_other, error, down, kept, cut)
     pruned_other = [swap(pruned[0]), None]
-    pruned[1] = prune_next(inverse, error, down, kept, cut, 1)
+    pruned[1] = prune_next(inverse, error_next, down, kept_next, cut, 1)
     pruned_other[1] = swap(pruned[1])
 
     moving = [(), ()]

time: 108 us -> 106 us (0.981)
  waiting for transfers between devices: 29 us -> 32.3 us
  Pallas kernels: 37.5 us -> 34.9 us
  local copies, waits for them, and re-layouts: 3.51 us -> 1.93 us
    pallas_call x1, Pallas kernels: 2.91 us -> 0.24 us  [stage(): pl.pallas_call(stage_kernel, out_shape=[jax.ShapeDtypeStruct(a.shape, a.d...]
    ppermute x5, waiting for transfers between devices: 1.22 us -> 3.62 us  [swap(): return lax.ppermute(value, AXES, [(i, i ^ 1) for i in range(devices)])]
    unnamed x12, local copies, waits for them, and re-layouts: 3.51 us -> 1.93 us
    pallas_call x1 -> x2, Pallas kernels: 2.37 us -> 2.42 us  [masks(): pl.pallas_call(mask_kernel, out_shape=[jax.ShapeDtypeStruct((rows, cut),...]
  transfers between devices with their start and end apart: 35 -> 35, of which waited for: 19 -> 21; matrix products, arithmetic and copies ran while one was open for 1% -> 1% of each run, Pallas kernels for 28% -> 26%
where the time goes in v4:
time: 106 us
  Pallas kernels  34.9 us (33%)
  starting transfers between devices  34.1 us (32%)
  waiting for transfers between devices  32.3 us (30%)
  local copies, waits for them, and re-layouts  1.93 us (2%)
  other arithmetic  1.34 us (1%)
    ppermute x30, starting transfers between devices, shift(): return lax.ppermute(value, AXES, pairs)  32.9 us
    ppermute x30, waiting for transfers between devices, shift(): return lax.ppermute(value, AXES, pairs)  28.7 us
    pallas_call x6, Pallas kernels, hidden_part(): pl.pallas_call(functools.partial(hidden_kernel, len(pieces), sources, exp...  19.4 us
    pallas_call x8, Pallas kernels, outputs(): pl.pallas_call(functools.partial(outputs_kernel, rows // 2, len(arrived))...  5.13 us
    ppermute x5, waiting for transfers between devices, swap(): return lax.ppermute(value, AXES, [(i, i ^ 1) for i in range(devices)])  3.62 us
    pallas_call x1, Pallas kernels, prune_first(): pl.pallas_call(prune_kernel, out_shape=[jax.ShapeDtypeStruct((size, cut),...  2.57 us
    pallas_call x2, Pallas kernels, masks(): pl.pallas_call(mask_kernel, out_shape=[jax.ShapeDtypeStruct((rows, cut),...  2.42 us
  transfers between devices with their start and end apart: 35, of which 21 were waited for; matrix products, arithmetic and copies ran while one was open for 1% of the time, Pallas kernels for 26%

profile of v4, /device:TPU:0, one launch (start us, length us, event | category | flops | bytes accessed | tf_op | source)
XLA Modules:
  0.0 105.5 jit_solution(554060747120353607)
XLA Ops:
  0.6 2.1 %split.1 = (bf16[72,2048]{1,0:T(8,128)(2,1)}, bf16[72,2048]{1,0:T(8,128)(2,1)}, bf16[64,2048]{1,0:T(8,128)(2,1)}, bf16[64,2048]{1,0:T(8,128)(2,1)}) custom-call(bf16[128,2048]{1,0:T(8,128)(2,1)} %x_ref.1, s32[8,128]{1,0:T(8,128)} %bitcast.28, f32[8,128]{1,0:T(8,128)} %bitcast.29), custom_call_target="tpu_custom_call" | custom-call | tf_op jit(solution)/shard_map/split/pallas_call | solution.py:145
  2.7 0.5 collective-permute-start
  3.3 3.0 %collective-permute-start.2 = (bf16[72,2048]{1,0:T(8,128)(2,1)}, bf16[72,2048]{1,0:T(8,128)(2,1)S(1)}, u32[]{:S(2)}, u32[]{:S(2)}) collective-permute-start(bf16[72,2048]{1,0:T(8,128)(2,1)} %get-tuple-element.73.refs_0_), channel_id=1, source_target_pairs={{0,4},{1,5},{4,8},{5,9},{8,12},{9,13},{12,14},{13,15},{14,10},{15,... | collective-permute-start | bytes 884744 | tf_op jit(solution)/shard_map/ppermute | solution.py:464
  6.4 2.2 %collective-permute-done.1.refs_1_ = bf16[384,2048]{1,0:T(8,128)(2,1)S(1)} collective-permute-done((bf16[384,2048]{1,0:T(8,128)(2,1)}, bf16[384,2048]{1,0:T(8,128)(2,1)S(1)}, u32[]{:S(2)}, u32[]{:S(2)}) %collective-permute-start.1) | collective-permute-done | bytes 1572896 | tf_op jit(solution)/shard_map/ppermute | solution.py:467
  8.7 2.9 %collective-permute-start.8 = (bf16[64,2048]{1,0:T(8,128)(2,1)}, bf16[64,2048]{1,0:T(8,128)(2,1)}, u32[]{:S(2)}, u32[]{:S(2)}) collective-permute-start(bf16[64,2048]{1,0:T(8,128)(2,1)} %get-tuple-element.88.refs_1_), channel_id=1, source_target_pairs={{0,4},{1,5},{4,8},{5,9},{8,12},{9,13},{12,14},{13,15},{14,10},{15,... | collective-permute-start | bytes 786440 | tf_op jit(solution)/shard_map/ppermute | solution.py:464
  11.6 2.6 %collective-permute-done.2.refs_0_ = bf16[72,2048]{1,0:T(8,128)(2,1)S(1)} collective-permute-done((bf16[72,2048]{1,0:T(8,128)(2,1)}, bf16[72,2048]{1,0:T(8,128)(2,1)S(1)}, u32[]{:S(2)}, u32[]{:S(2)}) %collective-permute-start.2) | collective-permute-done | bytes 294944 | tf_op jit(solution)/shard_map/ppermute | solution.py:464
  14.2 1.9 %collective-permute-start.3 = (bf16[72,2048]{1,0:T(8,128)(2,1)S(1)}, bf16[72,2048]{1,0:T(8,128)(2,1)}, u32[]{:S(2)}, u32[]{:S(2)}) collective-permute-start(bf16[72,2048]{1,0:T(8,128)(2,1)S(1)} %collective-permute-done.2.refs_0_), channel_id=1, source_target_pairs={{0,4},{1,5},{4,8},{5,9},{8,12},{9,13},{12,14},{13,15},{14,10},{15,... | collective-permute-start | bytes 884744 | tf_op jit(solution)/shard_map/ppermute | solution.py:464
  16.5 3.4 %collective-permute-done.8.refs_1_ = bf16[64,2048]{1,0:T(8,128)(2,1)} collective-permute-done((bf16[64,2048]{1,0:T(8,128)(2,1)}, bf16[64,2048]{1,0:T(8,128)(2,1)}, u32[]{:S(2)}, u32[]{:S(2)}) %collective-permute-start.8) | collective-permute-done | bytes 262176 | tf_op jit(solution)/shard_map/ppermute | solution.py:464
  19.9 1.7 %collective-permute-done.9.refs_2_ = bf16[64,2048]{1,0:T(8,128)(2,1)} collective-permute-done((bf16[64,2048]{1,0:T(8,128)(2,1)}, bf16[64,2048]{1,0:T(8,128)(2,1)}, u32[]{:S(2)}, u32[]{:S(2)}) %collective-permute-start.9) | collective-permute-done | bytes 262176 | tf_op jit(solution)/shard_map/ppermute | solution.py:464
  21.6 1.6 %collective-permute-start.10 = (bf16[64,2048]{1,0:T(8,128)(2,1)}, bf16[64,2048]{1,0:T(8,128)(2,1)S(1)}, u32[]{:S(2)}, u32[]{:S(2)}) collective-permute-start(bf16[64,2048]{1,0:T(8,128)(2,1)} %collective-permute-done.8.refs_1_), channel_id=1, source_target_pairs={{0,4},{1,5},{4,8},{5,9},{8,12},{9,13},{12,14},{13,15},{14,10},{15,... | collective-permute-start | bytes 786440 | tf_op jit(solution)/shard_map/ppermute | solution.py:464
  23.2 0.4 collective-permute-start.11
  23.7 1.0 copy-done.4
  24.7 0.9 copy-done.5
  25.6 3.6 %hidden.6 = (bf16[128,768]{1,0:T(8,128)(2,1)S(1)}, f32[384,384]{1,0:T(8,128)S(1)}, f32[384,384]{1,0:T(8,128)S(1)}) custom-call(s32[2]{0:T(128)S(1)} %pad_add_fusion.place_ref, bf16[72,2048]{1,0:T(8,128)(2,1)S(1)} %copy-done.4, bf16[64,2048]{1,0:T(8,128)(2,1)S(1)} %copy-done.5, bf16[384,2048]{1,0:T(8,128)(2,1)S(1)} %bitcast.11, ...), custom_call_target="tpu_custom_call" | custom-call | flops 805306368 | bytes 6815744 | tf_op jit(solution)/shard_map/hidden/pallas_call | solution.py:245
  29.2 1.6 %collective-permute-start.6 = (bf16[72,2048]{1,0:T(8,128)(2,1)}, bf16[72,2048]{1,0:T(8,128)(2,1)S(1)}, u32[]{:S(2)}, u32[]{:S(2)}) collective-permute-start(bf16[72,2048]{1,0:T(8,128)(2,1)} %collective-permute-done.3.refs_0_), channel_id=1, source_target_pairs={{0,4},{1,5},{4,8},{5,9},{8,12},{9,13},{12,14},{13,15},{14,10},{15,... | collective-permute-start | bytes 884744 | tf_op jit(solution)/shard_map/ppermute | solution.py:464
  30.9 0.4 collective-permute-start.7
  31.3 4.1 %hidden.7 = (bf16[256,768]{1,0:T(8,128)(2,1)S(1)}, f32[384,384]{1,0:T(8,128)S(1)}, f32[384,384]{1,0:T(8,128)S(1)}) custom-call(s32[2]{0:T(128)S(1)} %pad_add_fusion.place_ref, bf16[72,2048]{1,0:T(8,128)(2,1)S(1)} %collective-permute-done.2.refs_0_, bf16[64,2048]{1,0:T(8,128)(2,1)} %collective-permute-done.8.refs_1_, ...), custom_call_target="tpu_custom_call" | custom-call | flops 1610612736 | bytes 7340032 | tf_op jit(solution)/shard_map/hidden/pallas_call | solution.py:245
  35.5 1.6 %collective-permute-start.14 = (bf16[64,2048]{1,0:T(8,128)(2,1)S(1)}, bf16[64,2048]{1,0:T(8,128)(2,1)S(1)}, u32[]{:S(2)}, u32[]{:S(2)}) collective-permute-start(bf16[64,2048]{1,0:T(8,128)(2,1)S(1)} %collective-permute-done.10.refs_1_), channel_id=1, source_target_pairs={{0,4},{1,5},{4,8},{5,9},{8,12},{9,13},{12,14},{13,15},{14,10},{15,... | collective-permute-start | bytes 786440 | tf_op jit(solution)/shard_map/ppermute | solution.py:464
  37.1 0.4 collective-permute-start.15
  37.6 4.1 %hidden.8 = (bf16[256,768]{1,0:T(8,128)(2,1)S(1)}, f32[384,384]{1,0:T(8,128)S(1)}, f32[384,384]{1,0:T(8,128)S(1)}) custom-call(s32[2]{0:T(128)S(1)} %pad_add_fusion.place_ref, bf16[72,2048]{1,0:T(8,128)(2,1)} %collective-permute-done.3.refs_0_, bf16[64,2048]{1,0:T(8,128)(2,1)S(1)} %collective-permute-done.10.refs_1_, ...), custom_call_target="tpu_custom_call" | custom-call | flops 1610612736 | bytes 7340032 | tf_op jit(solution)/shard_map/hidden/pallas_call | solution.py:245
  41.7 1.6 %collective-permute-start.12 = (bf16[72,2048]{1,0:T(8,128)(2,1)S(1)}, bf16[72,2048]{1,0:T(8,128)(2,1)S(1)}, u32[]{:S(2)}, u32[]{:S(2)}) collective-permute-start(bf16[72,2048]{1,0:T(8,128)(2,1)S(1)} %collective-permute-done.6.refs_0_), channel_id=1, source_target_pairs={{0,4},{1,5},{4,8},{5,9},{8,12},{9,13},{12,14},{13,15},{14,10},{15,... | collective-permute-start | bytes 884744 | tf_op jit(solution)/shard_map/ppermute | solution.py:464
  43.3 0.4 collective-permute-start.13
  43.8 1.2 %masks.2 = (bf16[384,1024]{1,0:T(8,128)(2,1)S(1)}, bf16[384,1024]{1,0:T(8,128)(2,1)S(1)}) custom-call(s32[96,2048]{1,0:T(8,128)S(1)} %bitcast.26, bf16[384,2048]{1,0:T(8,128)(2,1)S(1)} %bitcast.22), custom_call_target="tpu_custom_call" | custom-call | flops 301989888 | bytes 3145728 | tf_op jit(solution)/shard_map/masks/pallas_call | solution.py:189
  45.0 1.2 %masks.3 = (bf16[384,1024]{1,0:T(8,128)(2,1)S(1)}, bf16[384,1024]{1,0:T(8,128)(2,1)S(1)}) custom-call(s32[96,2048]{1,0:T(8,128)S(1)} %bitcast.27, bf16[384,2048]{1,0:T(8,128)(2,1)S(1)} %bitcast.23), custom_call_target="tpu_custom_call" | custom-call | flops 301989888 | bytes 3145728 | tf_op jit(solution)/shard_map/masks/pallas_call | solution.py:189
  46.6 3.6 %hidden.9 = (bf16[256,768]{1,0:T(8,128)(2,1)S(1)}, f32[384,384]{1,0:T(8,128)S(1)}, f32[384,384]{1,0:T(8,128)S(1)}) custom-call(s32[2]{0:T(128)S(1)} %pad_add_fusion.place_ref, bf16[72,2048]{1,0:T(8,128)(2,1)S(1)} %collective-permute-done.6.refs_0_, bf16[64,2048]{1,0:T(8,128)(2,1)S(1)} %collective-permute-done.14.refs_1_, ...), custom_call_target="tpu_custom_call" | custom-call | flops 1610612736 | bytes 7340032 | tf_op jit(solution)/shard_map/hidden/pallas_call | solution.py:245
  50.2 0.7 collective-permute-done.13.refs_1_
  50.9 2.0 %hidden.11 = (bf16[128,384]{1,0:T(8,128)(2,1)S(1)}, f32[384,384]{1,0:T(8,128)S(1)}) custom-call(s32[2]{0:T(128)S(1)} %pad_add_fusion.place_ref, bf16[72,2048]{1,0:T(8,128)(2,1)S(1)} %collective-permute-done.12.refs_0_, bf16[72,2048]{1,0:T(8,128)(2,1)S(1)} %collective-permute-done.13.refs_1_, bf16[384,2048]{1,0:T(8,128)(2,1)S(1)} %get-tuple-element.80.refs_4_.refs_6_.refs_2_, ...), custom_call_target="tpu_custom_call" | custom-call | flops 402653184 | bytes 3670016 | tf_op jit(solution)/shard_map/hidden/pallas_call | solution.py:245
  53.0 2.0 %hidden.10 = (bf16[128,384]{1,0:T(8,128)(2,1)S(1)}, f32[384,384]{1,0:T(8,128)S(1)}) custom-call(s32[2]{0:T(128)S(1)} %pad_add_fusion.place_ref, bf16[72,2048]{1,0:T(8,128)(2,1)S(1)} %collective-permute-done.12.refs_0_, bf16[72,2048]{1,0:T(8,128)(2,1)S(1)} %collective-permute-done.13.refs_1_, bf16[384,2048]{1,0:T(8,128)(2,1)S(1)} %bitcast.15, ...), custom_call_target="tpu_custom_call" | custom-call | flops 402653184 | bytes 3670016 | tf_op jit(solution)/shard_map/hidden/pallas_call | solution.py:245
  55.1 2.6 %prune.1 = (bf16[384,1024]{1,0:T(8,128)(2,1)S(1)}, bf16[384,384]{1,0:T(8,128)(2,1)S(1)}) custom-call(f32[384,384]{1,0:T(8,128)S(1)} %get-tuple-element.114.own_ref, f32[384,384]{1,0:T(8,128)S(1)} %collective-permute-done.16.other_ref, bf16[384,1024]{1,0:T(8,128)(2,1)S(1)} %get-tuple-element.106.error_ref, bf16[384,2048]{1,0:T(8,128)(2,1)S(1)} %bitcast.24, ...), custom_call_target="tpu_custom_call" | custom-call | flops 981467136 | bytes 4325376 | tf_op jit(solution)/shard_map/prune/pallas_call | solution.py:310
  57.6 0.6 collective-permute-start.26
  58.2 0.6 prune_next.1.own_ref
  58.9 1.2 %collective-permute-done.26.other_ref = bf16[384,1024]{1,0:T(8,128)(2,1)S(1)} collective-permute-done((bf16[384,1024]{1,0:T(8,128)(2,1)S(1)}, bf16[384,1024]{1,0:T(8,128)(2,1)S(1)}, u32[]{:S(2)}, u32[]{:S(2)}) %collective-permute-start.26) | collective-permute-done | bytes 786464 | tf_op jit(solution)/shard_map/ppermute | solution.py:467
  60.1 0.5 outputs.12
  60.9 1.7 %collective-permute-start.28 = (bf16[64,1024]{1,0:T(8,128)(2,1)S(1)}, bf16[64,1024]{1,0:T(8,128)(2,1)S(1)}, u32[]{:S(2)}, u32[]{:S(2)}) collective-permute-start(bf16[64,1024]{1,0:T(8,128)(2,1)S(1)} %get-tuple-element.133), channel_id=1, source_target_pairs={{0,4},{1,5},{4,8},{5,9},{8,12},{9,13},{12,14},{13,15},{14,10},{15,... | collective-permute-start | bytes 393224 | tf_op jit(solution)/shard_map/ppermute | solution.py:464
  63.4 1.7 %collective-permute-start.19 = (bf16[64,1024]{1,0:T(8,128)(2,1)S(1)}, bf16[64,1024]{1,0:T(8,128)(2,1)S(1)}, u32[]{:S(2)}, u32[]{:S(2)}) collective-permute-start(bf16[64,1024]{1,0:T(8,128)(2,1)S(1)} %get-tuple-element.124), channel_id=1, source_target_pairs={{0,4},{1,5},{4,8},{5,9},{8,12},{9,13},{12,14},{13,15},{14,10},{15,... | collective-permute-start | bytes 393224 | tf_op jit(solution)/shard_map/ppermute | solution.py:464
  65.2 1.8 %collective-permute-done.27.refs_0_ = bf16[64,1024]{1,0:T(8,128)(2,1)S(1)} collective-permute-done((bf16[64,1024]{1,0:T(8,128)(2,1)S(1)}, bf16[64,1024]{1,0:T(8,128)(2,1)S(1)}, u32[]{:S(2)}, u32[]{:S(2)}) %collective-permute-start.27) | collective-permute-done | bytes 131104 | tf_op jit(solution)/shard_map/ppermute | solution.py:464
  67.3 0.7 outputs.13
  68.0 1.7 %collective-permute-start.29 = (bf16[128,1024]{1,0:T(8,128)(2,1)S(1)}, bf16[128,1024]{1,0:T(8,128)(2,1)S(1)}, u32[]{:S(2)}, u32[]{:S(2)}) collective-permute-start(bf16[128,1024]{1,0:T(8,128)(2,1)S(1)} %get-tuple-element.134), channel_id=1, source_target_pairs={{0,2},{1,3},{4,0},{5,1},{8,4},{9,5},{12,8},{13,9},{14,12},{15,13},... | collective-permute-start | bytes 786440 | tf_op jit(solution)/shard_map/ppermute | solution.py:464
  70.0 0.7 outputs.9
  70.8 1.7 %collective-permute-start.20 = (bf16[128,1024]{1,0:T(8,128)(2,1)S(1)}, bf16[128,1024]{1,0:T(8,128)(2,1)S(1)}, u32[]{:S(2)}, u32[]{:S(2)}) collective-permute-start(bf16[128,1024]{1,0:T(8,128)(2,1)S(1)} %get-tuple-element.125), channel_id=1, source_target_pairs={{0,2},{1,3},{4,0},{5,1},{8,4},{9,5},{12,8},{13,9},{14,12},{15,13},... | collective-permute-start | bytes 786440 | tf_op jit(solution)/shard_map/ppermute | solution.py:464
  72.8 4.4 %collective-permute-done.29.refs_0_ = bf16[128,1024]{1,0:T(8,128)(2,1)S(1)} collective-permute-done((bf16[128,1024]{1,0:T(8,128)(2,1)S(1)}, bf16[128,1024]{1,0:T(8,128)(2,1)S(1)}, u32[]{:S(2)}, u32[]{:S(2)}) %collective-permute-start.29) | collective-permute-done | bytes 262176 | tf_op jit(solution)/shard_map/ppermute | solution.py:464
  77.3 1.6 %collective-permute-done.30.refs_1_ = bf16[128,1024]{1,0:T(8,128)(2,1)S(1)} collective-permute-done((bf16[128,1024]{1,0:T(8,128)(2,1)S(1)}, bf16[128,1024]{1,0:T(8,128)(2,1)S(1)}, u32[]{:S(2)}, u32[]{:S(2)}) %collective-permute-start.30) | collective-permute-done | bytes 262176 | tf_op jit(solution)/shard_map/ppermute | solution.py:464
  78.8 0.7 outputs.14
  79.5 1.6 %collective-permute-start.31 = (bf16[128,1024]{1,0:T(8,128)(2,1)S(1)}, bf16[128,1024]{1,0:T(8,128)(2,1)S(1)}, u32[]{:S(2)}, u32[]{:S(2)}) collective-permute-start(bf16[128,1024]{1,0:T(8,128)(2,1)S(1)} %get-tuple-element.136), channel_id=1, source_target_pairs={{0,2},{1,3},{4,0},{5,1},{8,4},{9,5},{12,8},{13,9},{14,12},{15,13},... | collective-permute-start | bytes 786440 | tf_op jit(solution)/shard_map/ppermute | solution.py:464
  81.2 0.4 collective-permute-start.32
  81.6 1.3 %collective-permute-done.20.refs_0_ = bf16[128,1024]{1,0:T(8,128)(2,1)S(1)} collective-permute-done((bf16[128,1024]{1,0:T(8,128)(2,1)S(1)}, bf16[128,1024]{1,0:T(8,128)(2,1)S(1)}, u32[]{:S(2)}, u32[]{:S(2)}) %collective-permute-start.20) | collective-permute-done | bytes 262176 | tf_op jit(solution)/shard_map/ppermute | solution.py:464
  82.9 1.6 %collective-permute-done.21.refs_1_ = bf16[128,1024]{1,0:T(8,128)(2,1)S(1)} collective-permute-done((bf16[128,1024]{1,0:T(8,128)(2,1)S(1)}, bf16[128,1024]{1,0:T(8,128)(2,1)S(1)}, u32[]{:S(2)}, u32[]{:S(2)}) %collective-permute-start.21) | collective-permute-done | bytes 262176 | tf_op jit(solution)/shard_map/ppermute | solution.py:464
  84.4 0.7 outputs.10
  85.1 1.6 %collective-permute-start.22 = (bf16[128,1024]{1,0:T(8,128)(2,1)S(1)}, bf16[128,1024]{1,0:T(8,128)(2,1)S(1)}, u32[]{:S(2)}, u32[]{:S(2)}) collective-permute-start(bf16[128,1024]{1,0:T(8,128)(2,1)S(1)} %get-tuple-element.127), channel_id=1, source_target_pairs={{0,2},{1,3},{4,0},{5,1},{8,4},{9,5},{12,8},{13,9},{14,12},{15,13},... | collective-permute-start | bytes 786440 | tf_op jit(solution)/shard_map/ppermute | solution.py:464
  86.8 0.4 collective-permute-start.23
  87.2 1.6 %collective-permute-done.31.refs_0_ = bf16[128,1024]{1,0:T(8,128)(2,1)S(1)} collective-permute-done((bf16[128,1024]{1,0:T(8,128)(2,1)S(1)}, bf16[128,1024]{1,0:T(8,128)(2,1)S(1)}, u32[]{:S(2)}, u32[]{:S(2)}) %collective-permute-start.31) | collective-permute-done | bytes 262176 | tf_op jit(solution)/shard_map/ppermute | solution.py:464
  88.8 1.6 %collective-permute-done.32.refs_1_ = bf16[128,1024]{1,0:T(8,128)(2,1)S(1)} collective-permute-done((bf16[128,1024]{1,0:T(8,128)(2,1)S(1)}, bf16[128,1024]{1,0:T(8,128)(2,1)S(1)}, u32[]{:S(2)}, u32[]{:S(2)}) %collective-permute-start.32) | collective-permute-done | bytes 262176 | tf_op jit(solution)/shard_map/ppermute | solution.py:464
  90.4 0.7 outputs.15
  91.1 1.6 %collective-permute-start.33 = (bf16[128,1024]{1,0:T(8,128)(2,1)S(1)}, bf16[128,1024]{1,0:T(8,128)(2,1)S(1)}, u32[]{:S(2)}, u32[]{:S(2)}) collective-permute-start(bf16[128,1024]{1,0:T(8,128)(2,1)S(1)} %get-tuple-element.138), channel_id=1, source_target_pairs={{0,2},{1,3},{4,0},{5,1},{8,4},{9,5},{12,8},{13,9},{14,12},{15,13},... | collective-permute-start | bytes 786440 | tf_op jit(solution)/shard_map/ppermute | solution.py:464
  92.7 0.4 collective-permute-start.34
  93.2 1.3 %collective-permute-done.22.refs_0_ = bf16[128,1024]{1,0:T(8,128)(2,1)S(1)} collective-permute-done((bf16[128,1024]{1,0:T(8,128)(2,1)S(1)}, bf16[128,1024]{1,0:T(8,128)(2,1)S(1)}, u32[]{:S(2)}, u32[]{:S(2)}) %collective-permute-start.22) | collective-permute-done | bytes 262176 | tf_op jit(solution)/shard_map/ppermute | solution.py:464
  94.4 1.6 %collective-permute-done.23.refs_1_ = bf16[128,1024]{1,0:T(8,128)(2,1)S(1)} collective-permute-done((bf16[128,1024]{1,0:T(8,128)(2,1)S(1)}, bf16[128,1024]{1,0:T(8,128)(2,1)S(1)}, u32[]{:S(2)}, u32[]{:S(2)}) %collective-permute-start.23) | collective-permute-done | bytes 262176 | tf_op jit(solution)/shard_map/ppermute | solution.py:464
  96.0 0.7 outputs.11
  96.7 1.6 %collective-permute-start.24 = (bf16[128,1024]{1,0:T(8,128)(2,1)S(1)}, bf16[128,1024]{1,0:T(8,128)(2,1)S(1)}, u32[]{:S(2)}, u32[]{:S(2)}) collective-permute-start(bf16[128,1024]{1,0:T(8,128)(2,1)S(1)} %get-tuple-element.129), channel_id=1, source_target_pairs={{0,2},{1,3},{4,0},{5,1},{8,4},{9,5},{12,8},{13,9},{14,12},{15,13},... | collective-permute-start | bytes 786440 | tf_op jit(solution)/shard_map/ppermute | solution.py:464
  98.8 1.3 %maximum_bitcast_fusion = bf16[1,384,2048]{2,1,0:T(8,128)(2,1)} fusion(bf16[384,1024]{1,0:T(8,128)(2,1)S(1)} %prune_next.1.own_ref, bf16[384,1024]{1,0:T(8,128)(2,1)S(1)} %get-tuple-element.131.own_ref), kind=kLoop, calls=%fused_computation | loop fusion | flops 3145728 | bytes 3145728 | tf_op jit(solution)/shard_map/broadcast_in_dim | solution.py:540
  101.3 0.8 finish.2.refs_0_
  102.1 1.1 %collective-permute-done.24.right_ref = bf16[128,1024]{1,0:T(8,128)(2,1)S(1)} collective-permute-done((bf16[128,1024]{1,0:T(8,128)(2,1)S(1)}, bf16[128,1024]{1,0:T(8,128)(2,1)S(1)}, u32[]{:S(2)}, u32[]{:S(2)}) %collective-permute-start.24) | collective-permute-done | bytes 262176 | tf_op jit(solution)/shard_map/ppermute | solution.py:464
  103.2 1.6 %collective-permute-done.25.left_ref = bf16[128,1024]{1,0:T(8,128)(2,1)S(1)} collective-permute-done((bf16[128,1024]{1,0:T(8,128)(2,1)S(1)}, bf16[128,1024]{1,0:T(8,128)(2,1)S(1)}, u32[]{:S(2)}, u32[]{:S(2)}) %collective-permute-start.25) | collective-permute-done | bytes 262176 | tf_op jit(solution)/shard_map/ppermute | solution.py:464
  104.7 0.8 finish.3
  (44 shorter events, 5.1 us)
Async XLA Ops:
  2.7 3.7 %collective-permute-start = (bf16[384,2048]{1,0:T(8,128)(2,1)}, bf16[384,2048]{1,0:T(8,128)(2,1)S(1)}, u32[]{:S(2)}, u32[]{:S(2)}) collective-permute-start(bf16[384,2048]{1,0:T(8,128)(2,1)} %bitcast.10), channel_id=1, source_target_pairs={{0,1},{1,0},{2,3},{3,2},{4,5},{5,4},{6,7},{7,6},{8,9},{9,8},{10,11... | collective-permute-start | bytes 4718600 | tf_op jit(solution)/shard_map/ppermute | solution.py:467
  3.2 5.5 %collective-permute-start.1 = (bf16[384,2048]{1,0:T(8,128)(2,1)}, bf16[384,2048]{1,0:T(8,128)(2,1)S(1)}, u32[]{:S(2)}, u32[]{:S(2)}) collective-permute-start(bf16[384,2048]{1,0:T(8,128)(2,1)} %bitcast.16), channel_id=1, source_target_pairs={{0,1},{1,0},{2,3},{3,2},{4,5},{5,4},{6,7},{7,6},{8,9},{9,8},{10,11... | collective-permute-start | bytes 4718600 | tf_op jit(solution)/shard_map/ppermute | solution.py:467
  3.3 11.0 %collective-permute-start.2 = (bf16[72,2048]{1,0:T(8,128)(2,1)}, bf16[72,2048]{1,0:T(8,128)(2,1)S(1)}, u32[]{:S(2)}, u32[]{:S(2)}) collective-permute-start(bf16[72,2048]{1,0:T(8,128)(2,1)} %get-tuple-element.73.refs_0_), channel_id=1, source_target_pairs={{0,4},{1,5},{4,8},{5,9},{8,12},{9,13},{12,14},{13,15},{14,10},{15,... | collective-permute-start | bytes 884744 | tf_op jit(solution)/shard_map/ppermute | solution.py:464
  6.3 9.9 %collective-permute-start.4 = (bf16[72,2048]{1,0:T(8,128)(2,1)}, bf16[72,2048]{1,0:T(8,128)(2,1)}, u32[]{:S(2)}, u32[]{:S(2)}) collective-permute-start(bf16[72,2048]{1,0:T(8,128)(2,1)} %get-tuple-element.83), channel_id=1, source_target_pairs={{0,2},{1,3},{4,0},{5,1},{8,4},{9,5},{12,8},{13,9},{14,12},{15,13},... | collective-permute-start | bytes 884744 | tf_op jit(solution)/shard_map/ppermute | solution.py:464
  8.7 11.2 %collective-permute-start.8 = (bf16[64,2048]{1,0:T(8,128)(2,1)}, bf16[64,2048]{1,0:T(8,128)(2,1)}, u32[]{:S(2)}, u32[]{:S(2)}) collective-permute-start(bf16[64,2048]{1,0:T(8,128)(2,1)} %get-tuple-element.88.refs_1_), channel_id=1, source_target_pairs={{0,4},{1,5},{4,8},{5,9},{8,12},{9,13},{12,14},{13,15},{14,10},{15,... | collective-permute-start | bytes 786440 | tf_op jit(solution)/shard_map/ppermute | solution.py:464
  11.6 10.0 %collective-permute-start.9 = (bf16[64,2048]{1,0:T(8,128)(2,1)}, bf16[64,2048]{1,0:T(8,128)(2,1)}, u32[]{:S(2)}, u32[]{:S(2)}) collective-permute-start(bf16[64,2048]{1,0:T(8,128)(2,1)} %get-tuple-element.89), channel_id=1, source_target_pairs={{0,2},{1,3},{4,0},{5,1},{8,4},{9,5},{12,8},{13,9},{14,12},{15,13},... | collective-permute-start | bytes 786440 | tf_op jit(solution)/shard_map/ppermute | solution.py:464
  14.2 15.0 %collective-permute-start.3 = (bf16[72,2048]{1,0:T(8,128)(2,1)S(1)}, bf16[72,2048]{1,0:T(8,128)(2,1)}, u32[]{:S(2)}, u32[]{:S(2)}) collective-permute-start(bf16[72,2048]{1,0:T(8,128)(2,1)S(1)} %collective-permute-done.2.refs_0_), channel_id=1, source_target_pairs={{0,4},{1,5},{4,8},{5,9},{8,12},{9,13},{12,14},{13,15},{14,10},{15,... | collective-permute-start | bytes 884744 | tf_op jit(solution)/shard_map/ppermute | solution.py:464
  16.2 13.1 %collective-permute-start.5 = (bf16[72,2048]{1,0:T(8,128)(2,1)}, bf16[72,2048]{1,0:T(8,128)(2,1)}, u32[]{:S(2)}, u32[]{:S(2)}) collective-permute-start(bf16[72,2048]{1,0:T(8,128)(2,1)} %collective-permute-done.4.refs_3_), channel_id=1, source_target_pairs={{0,2},{1,3},{4,0},{5,1},{8,4},{9,5},{12,8},{13,9},{14,12},{15,13},... | collective-permute-start | bytes 884744 | tf_op jit(solution)/shard_map/ppermute | solution.py:464
  16.3 7.4 %copy-start = (bf16[1,384,2048]{2,1,0:T(8,128)(2,1)S(1)}, bf16[1,384,2048]{2,1,0:T(8,128)(2,1)}, u32[]{:S(2)}) copy-start(bf16[1,384,2048]{2,1,0:T(8,128)(2,1)} %param.10) | copy-start | bytes 4718596
  16.3 7.4 %copy-start.1 = (bf16[1,384,2048]{2,1,0:T(8,128)(2,1)S(1)}, bf16[1,384,2048]{2,1,0:T(8,128)(2,1)}, u32[]{:S(2)}) copy-start(bf16[1,384,2048]{2,1,0:T(8,128)(2,1)} %param.11) | copy-start | bytes 4718596
  21.6 13.8 %collective-permute-start.10 = (bf16[64,2048]{1,0:T(8,128)(2,1)}, bf16[64,2048]{1,0:T(8,128)(2,1)S(1)}, u32[]{:S(2)}, u32[]{:S(2)}) collective-permute-start(bf16[64,2048]{1,0:T(8,128)(2,1)} %collective-permute-done.8.refs_1_), channel_id=1, source_target_pairs={{0,4},{1,5},{4,8},{5,9},{8,12},{9,13},{12,14},{13,15},{14,10},{15,... | collective-permute-start | bytes 786440 | tf_op jit(solution)/shard_map/ppermute | solution.py:464
  23.2 12.3 %collective-permute-start.11 = (bf16[64,2048]{1,0:T(8,128)(2,1)}, bf16[64,2048]{1,0:T(8,128)(2,1)S(1)}, u32[]{:S(2)}, u32[]{:S(2)}) collective-permute-start(bf16[64,2048]{1,0:T(8,128)(2,1)} %collective-permute-done.9.refs_2_), channel_id=1, source_target_pairs={{0,2},{1,3},{4,0},{5,1},{8,4},{9,5},{12,8},{13,9},{14,12},{15,13},... | collective-permute-start | bytes 786440 | tf_op jit(solution)/shard_map/ppermute | solution.py:464
  23.7 1.0 copy-start.4
  24.7 0.9 copy-start.5
  29.2 12.4 %collective-permute-start.6 = (bf16[72,2048]{1,0:T(8,128)(2,1)}, bf16[72,2048]{1,0:T(8,128)(2,1)S(1)}, u32[]{:S(2)}, u32[]{:S(2)}) collective-permute-start(bf16[72,2048]{1,0:T(8,128)(2,1)} %collective-permute-done.3.refs_0_), channel_id=1, source_target_pairs={{0,4},{1,5},{4,8},{5,9},{8,12},{9,13},{12,14},{13,15},{14,10},{15,... | collective-permute-start | bytes 884744 | tf_op jit(solution)/shard_map/ppermute | solution.py:464
  30.9 10.8 %collective-permute-start.7 = (bf16[72,2048]{1,0:T(8,128)(2,1)}, bf16[72,2048]{1,0:T(8,128)(2,1)S(1)}, u32[]{:S(2)}, u32[]{:S(2)}) collective-permute-start(bf16[72,2048]{1,0:T(8,128)(2,1)} %collective-permute-done.5.refs_3_), channel_id=1, source_target_pairs={{0,2},{1,3},{4,0},{5,1},{8,4},{9,5},{12,8},{13,9},{14,12},{15,13},... | collective-permute-start | bytes 884744 | tf_op jit(solution)/shard_map/ppermute | solution.py:464
  35.5 8.3 %copy-start.2 = (bf16[1,384,2048]{2,1,0:T(8,128)(2,1)S(1)}, bf16[1,384,2048]{2,1,0:T(8,128)(2,1)}, u32[]{:S(2)}) copy-start(bf16[1,384,2048]{2,1,0:T(8,128)(2,1)} %param.12) | copy-start | bytes 4718596
  35.5 8.3 %copy-start.3 = (s32[1,96,2048]{2,1,0:T(8,128)S(1)}, s32[1,96,2048]{2,1,0:T(8,128)}, u32[]{:S(2)}) copy-start(s32[1,96,2048]{2,1,0:T(8,128)} %param.13) | copy-start | bytes 2359300
  35.5 10.7 %collective-permute-start.14 = (bf16[64,2048]{1,0:T(8,128)(2,1)S(1)}, bf16[64,2048]{1,0:T(8,128)(2,1)S(1)}, u32[]{:S(2)}, u32[]{:S(2)}) collective-permute-start(bf16[64,2048]{1,0:T(8,128)(2,1)S(1)} %collective-permute-done.10.refs_1_), channel_id=1, source_target_pairs={{0,4},{1,5},{4,8},{5,9},{8,12},{9,13},{12,14},{13,15},{14,10},{15,... | collective-permute-start | bytes 786440 | tf_op jit(solution)/shard_map/ppermute | solution.py:464
  37.1 9.5 %collective-permute-start.15 = (bf16[64,2048]{1,0:T(8,128)(2,1)S(1)}, bf16[64,2048]{1,0:T(8,128)(2,1)S(1)}, u32[]{:S(2)}, u32[]{:S(2)}) collective-permute-start(bf16[64,2048]{1,0:T(8,128)(2,1)S(1)} %collective-permute-done.11.refs_2_), channel_id=1, source_target_pairs={{0,2},{1,3},{4,0},{5,1},{8,4},{9,5},{12,8},{13,9},{14,12},{15,13},... | collective-permute-start | bytes 786440 | tf_op jit(solution)/shard_map/ppermute | solution.py:464
  41.7 8.5 %collective-permute-start.12 = (bf16[72,2048]{1,0:T(8,128)(2,1)S(1)}, bf16[72,2048]{1,0:T(8,128)(2,1)S(1)}, u32[]{:S(2)}, u32[]{:S(2)}) collective-permute-start(bf16[72,2048]{1,0:T(8,128)(2,1)S(1)} %collective-permute-done.6.refs_0_), channel_id=1, source_target_pairs={{0,4},{1,5},{4,8},{5,9},{8,12},{9,13},{12,14},{13,15},{14,10},{15,... | collective-permute-start | bytes 884744 | tf_op jit(solution)/shard_map/ppermute | solution.py:464
  43.3 7.6 %collective-permute-start.13 = (bf16[72,2048]{1,0:T(8,128)(2,1)S(1)}, bf16[72,2048]{1,0:T(8,128)(2,1)S(1)}, u32[]{:S(2)}, u32[]{:S(2)}) collective-permute-start(bf16[72,2048]{1,0:T(8,128)(2,1)S(1)} %collective-permute-done.7.refs_3_), channel_id=1, source_target_pairs={{0,2},{1,3},{4,0},{5,1},{8,4},{9,5},{12,8},{13,9},{14,12},{15,13},... | collective-permute-start | bytes 884744 | tf_op jit(solution)/shard_map/ppermute | solution.py:464
  53.0 2.1 %collective-permute-start.16 = (f32[384,384]{1,0:T(8,128)S(1)}, f32[384,384]{1,0:T(8,128)S(1)}, u32[]{:S(2)}, u32[]{:S(2)}) collective-permute-start(f32[384,384]{1,0:T(8,128)S(1)} %get-tuple-element.116), channel_id=1, source_target_pairs={{0,1},{1,0},{2,3},{3,2},{4,5},{5,4},{6,7},{7,6},{8,9},{9,8},{10,11... | collective-permute-start | bytes 1769480 | tf_op jit(solution)/shard_map/ppermute | solution.py:467
  57.6 2.5 %collective-permute-start.26 = (bf16[384,1024]{1,0:T(8,128)(2,1)S(1)}, bf16[384,1024]{1,0:T(8,128)(2,1)S(1)}, u32[]{:S(2)}, u32[]{:S(2)}) collective-permute-start(bf16[384,1024]{1,0:T(8,128)(2,1)S(1)} %get-tuple-element.131.own_ref), channel_id=1, source_target_pairs={{0,1},{1,0},{2,3},{3,2},{4,5},{5,4},{6,7},{7,6},{8,9},{9,8},{10,11... | collective-permute-start | bytes 2359304 | tf_op jit(solution)/shard_map/ppermute | solution.py:467
  58.8 3.8 %collective-permute-start.17 = (bf16[384,1024]{1,0:T(8,128)(2,1)S(1)}, bf16[384,1024]{1,0:T(8,128)(2,1)S(1)}, u32[]{:S(2)}, u32[]{:S(2)}) collective-permute-start(bf16[384,1024]{1,0:T(8,128)(2,1)S(1)} %prune_next.1.own_ref), channel_id=1, source_target_pairs={{0,1},{1,0},{2,3},{3,2},{4,5},{5,4},{6,7},{7,6},{8,9},{9,8},{10,11... | collective-permute-start | bytes 2359304 | tf_op jit(solution)/shard_map/ppermute | solution.py:467
  60.6 6.4 %collective-permute-start.27 = (bf16[64,1024]{1,0:T(8,128)(2,1)S(1)}, bf16[64,1024]{1,0:T(8,128)(2,1)S(1)}, u32[]{:S(2)}, u32[]{:S(2)}) collective-permute-start(bf16[64,1024]{1,0:T(8,128)(2,1)S(1)} %get-tuple-element.132), channel_id=1, source_target_pairs={{0,2},{1,3},{4,0},{5,1},{8,4},{9,5},{12,8},{13,9},{14,12},{15,13},... | collective-permute-start | bytes 393224 | tf_op jit(solution)/shard_map/ppermute | solution.py:464
  60.9 6.3 %collective-permute-start.28 = (bf16[64,1024]{1,0:T(8,128)(2,1)S(1)}, bf16[64,1024]{1,0:T(8,128)(2,1)S(1)}, u32[]{:S(2)}, u32[]{:S(2)}) collective-permute-start(bf16[64,1024]{1,0:T(8,128)(2,1)S(1)} %get-tuple-element.133), channel_id=1, source_target_pairs={{0,4},{1,5},{4,8},{5,9},{8,12},{9,13},{12,14},{13,15},{14,10},{15,... | collective-permute-start | bytes 393224 | tf_op jit(solution)/shard_map/ppermute | solution.py:464
  63.1 6.9 %collective-permute-start.18 = (bf16[64,1024]{1,0:T(8,128)(2,1)S(1)}, bf16[64,1024]{1,0:T(8,128)(2,1)S(1)}, u32[]{:S(2)}, u32[]{:S(2)}) collective-permute-start(bf16[64,1024]{1,0:T(8,128)(2,1)S(1)} %get-tuple-element.123), channel_id=1, source_target_pairs={{0,2},{1,3},{4,0},{5,1},{8,4},{9,5},{12,8},{13,9},{14,12},{15,13},... | collective-permute-start | bytes 393224 | tf_op jit(solution)/shard_map/ppermute | solution.py:464
  63.4 6.6 %collective-permute-start.19 = (bf16[64,1024]{1,0:T(8,128)(2,1)S(1)}, bf16[64,1024]{1,0:T(8,128)(2,1)S(1)}, u32[]{:S(2)}, u32[]{:S(2)}) collective-permute-start(bf16[64,1024]{1,0:T(8,128)(2,1)S(1)} %get-tuple-element.124), channel_id=1, source_target_pairs={{0,4},{1,5},{4,8},{5,9},{8,12},{9,13},{12,14},{13,15},{14,10},{15,... | collective-permute-start | bytes 393224 | tf_op jit(solution)/shard_map/ppermute | solution.py:464
  68.0 9.3 %collective-permute-start.29 = (bf16[128,1024]{1,0:T(8,128)(2,1)S(1)}, bf16[128,1024]{1,0:T(8,128)(2,1)S(1)}, u32[]{:S(2)}, u32[]{:S(2)}) collective-permute-start(bf16[128,1024]{1,0:T(8,128)(2,1)S(1)} %get-tuple-element.134), channel_id=1, source_target_pairs={{0,2},{1,3},{4,0},{5,1},{8,4},{9,5},{12,8},{13,9},{14,12},{15,13},... | collective-permute-start | bytes 786440 | tf_op jit(solution)/shard_map/ppermute | solution.py:464
  69.6 9.2 %collective-permute-start.30 = (bf16[128,1024]{1,0:T(8,128)(2,1)S(1)}, bf16[128,1024]{1,0:T(8,128)(2,1)S(1)}, u32[]{:S(2)}, u32[]{:S(2)}) collective-permute-start(bf16[128,1024]{1,0:T(8,128)(2,1)S(1)} %get-tuple-element.135), channel_id=1, source_target_pairs={{0,4},{1,5},{4,8},{5,9},{8,12},{9,13},{12,14},{13,15},{14,10},{15,... | collective-permute-start | bytes 786440 | tf_op jit(solution)/shard_map/ppermute | solution.py:464
  70.8 12.1 %collective-permute-start.20 = (bf16[128,1024]{1,0:T(8,128)(2,1)S(1)}, bf16[128,1024]{1,0:T(8,128)(2,1)S(1)}, u32[]{:S(2)}, u32[]{:S(2)}) collective-permute-start(bf16[128,1024]{1,0:T(8,128)(2,1)S(1)} %get-tuple-element.125), channel_id=1, source_target_pairs={{0,2},{1,3},{4,0},{5,1},{8,4},{9,5},{12,8},{13,9},{14,12},{15,13},... | collective-permute-start | bytes 786440 | tf_op jit(solution)/shard_map/ppermute | solution.py:464
  72.4 12.0 %collective-permute-start.21 = (bf16[128,1024]{1,0:T(8,128)(2,1)S(1)}, bf16[128,1024]{1,0:T(8,128)(2,1)S(1)}, u32[]{:S(2)}, u32[]{:S(2)}) collective-permute-start(bf16[128,1024]{1,0:T(8,128)(2,1)S(1)} %get-tuple-element.126), channel_id=1, source_target_pairs={{0,4},{1,5},{4,8},{5,9},{8,12},{9,13},{12,14},{13,15},{14,10},{15,... | collective-permute-start | bytes 786440 | tf_op jit(solution)/shard_map/ppermute | solution.py:464
  79.5 9.3 %collective-permute-start.31 = (bf16[128,1024]{1,0:T(8,128)(2,1)S(1)}, bf16[128,1024]{1,0:T(8,128)(2,1)S(1)}, u32[]{:S(2)}, u32[]{:S(2)}) collective-permute-start(bf16[128,1024]{1,0:T(8,128)(2,1)S(1)} %get-tuple-element.136), channel_id=1, source_target_pairs={{0,2},{1,3},{4,0},{5,1},{8,4},{9,5},{12,8},{13,9},{14,12},{15,13},... | collective-permute-start | bytes 786440 | tf_op jit(solution)/shard_map/ppermute | solution.py:464
  81.2 9.2 %collective-permute-start.32 = (bf16[128,1024]{1,0:T(8,128)(2,1)S(1)}, bf16[128,1024]{1,0:T(8,128)(2,1)S(1)}, u32[]{:S(2)}, u32[]{:S(2)}) collective-permute-start(bf16[128,1024]{1,0:T(8,128)(2,1)S(1)} %get-tuple-element.137), channel_id=1, source_target_pairs={{0,4},{1,5},{4,8},{5,9},{8,12},{9,13},{12,14},{13,15},{14,10},{15,... | collective-permute-start | bytes 786440 | tf_op jit(solution)/shard_map/ppermute | solution.py:464
  85.1 9.3 %collective-permute-start.22 = (bf16[128,1024]{1,0:T(8,128)(2,1)S(1)}, bf16[128,1024]{1,0:T(8,128)(2,1)S(1)}, u32[]{:S(2)}, u32[]{:S(2)}) collective-permute-start(bf16[128,1024]{1,0:T(8,128)(2,1)S(1)} %get-tuple-element.127), channel_id=1, source_target_pairs={{0,2},{1,3},{4,0},{5,1},{8,4},{9,5},{12,8},{13,9},{14,12},{15,13},... | collective-permute-start | bytes 786440 | tf_op jit(solution)/shard_map/ppermute | solution.py:464
  86.8 9.2 %collective-permute-start.23 = (bf16[128,1024]{1,0:T(8,128)(2,1)S(1)}, bf16[128,1024]{1,0:T(8,128)(2,1)S(1)}, u32[]{:S(2)}, u32[]{:S(2)}) collective-permute-start(bf16[128,1024]{1,0:T(8,128)(2,1)S(1)} %get-tuple-element.128), channel_id=1, source_target_pairs={{0,4},{1,5},{4,8},{5,9},{8,12},{9,13},{12,14},{13,15},{14,10},{15,... | collective-permute-start | bytes 786440 | tf_op jit(solution)/shard_map/ppermute | solution.py:464
  91.1 9.9 %collective-permute-start.33 = (bf16[128,1024]{1,0:T(8,128)(2,1)S(1)}, bf16[128,1024]{1,0:T(8,128)(2,1)S(1)}, u32[]{:S(2)}, u32[]{:S(2)}) collective-permute-start(bf16[128,1024]{1,0:T(8,128)(2,1)S(1)} %get-tuple-element.138), channel_id=1, source_target_pairs={{0,2},{1,3},{4,0},{5,1},{8,4},{9,5},{12,8},{13,9},{14,12},{15,13},... | collective-permute-start | bytes 786440 | tf_op jit(solution)/shard_map/ppermute | solution.py:464
  92.7 8.6 %collective-permute-start.34 = (bf16[128,1024]{1,0:T(8,128)(2,1)S(1)}, bf16[128,1024]{1,0:T(8,128)(2,1)S(1)}, u32[]{:S(2)}, u32[]{:S(2)}) collective-permute-start(bf16[128,1024]{1,0:T(8,128)(2,1)S(1)} %get-tuple-element.139), channel_id=1, source_target_pairs={{0,4},{1,5},{4,8},{5,9},{8,12},{9,13},{12,14},{13,15},{14,10},{15,... | collective-permute-start | bytes 786440 | tf_op jit(solution)/shard_map/ppermute | solution.py:464
  96.7 6.4 %collective-permute-start.24 = (bf16[128,1024]{1,0:T(8,128)(2,1)S(1)}, bf16[128,1024]{1,0:T(8,128)(2,1)S(1)}, u32[]{:S(2)}, u32[]{:S(2)}) collective-permute-start(bf16[128,1024]{1,0:T(8,128)(2,1)S(1)} %get-tuple-element.129), channel_id=1, source_target_pairs={{0,2},{1,3},{4,0},{5,1},{8,4},{9,5},{12,8},{13,9},{14,12},{15,13},... | collective-permute-start | bytes 786440 | tf_op jit(solution)/shard_map/ppermute | solution.py:464
  98.4 6.4 %collective-permute-start.25 = (bf16[128,1024]{1,0:T(8,128)(2,1)S(1)}, bf16[128,1024]{1,0:T(8,128)(2,1)S(1)}, u32[]{:S(2)}, u32[]{:S(2)}) collective-permute-start(bf16[128,1024]{1,0:T(8,128)(2,1)S(1)} %get-tuple-element.130), channel_id=1, source_target_pairs={{0,4},{1,5},{4,8},{5,9},{8,12},{9,13},{12,14},{13,15},{14,10},{15,... | collective-permute-start | bytes 786440 | tf_op jit(solution)/shard_map/ppermute | solution.py:464

commit v5 on v4

--- a/solution.py
+++ b/solution.py
@@ -497,8 +497,12 @@
     hop_second(1)
     hop_first(2)
     pairs[1] = stage(pairs[1])
-    right[1], left[0], *_ = tied((right[1], left[0], *pairs[1]))
+    own, gram_own = hidden_part(place, (0,), devices, *groups[0], pairs[:1], [])
+    right[1], left[0], gram_own, *_ = tied((right[1], left[0], gram_own, *pairs[1]))
     hop_second(2)
+    other, gram_other = hidden_part(place, (1,), devices, *groups[0], pairs[1:], [])
+    hidden.append(((own, 0), (other, 0)))
+    grams = [gram_own, gram_other]
     for hop in range(3, reach + 1):
         while len(hidden) < (1 if hop == 3 else hop - 1):
             work(len(hidden))

time: 106 us -> 106 us (level)
  waiting for transfers between devices: 32.3 us -> 29.1 us
  local copies, waits for them, and re-layouts: 1.93 us -> 4.75 us
    ppermute x30, waiting for transfers between devices: 28.7 us -> 25.5 us  [shift(): return lax.ppermute(value, AXES, pairs)]
    unnamed x12 -> x16, local copies, waits for them, and re-layouts: 1.93 us -> 4.75 us
    pallas_call x6 -> x7, Pallas kernels: 19.4 us -> 19.8 us  [hidden_part(): pl.pallas_call(functools.partial(hidden_kernel, len(pieces), sources, exp...]
  transfers between devices with their start and end apart: 35 -> 35, of which waited for: 21 -> 22; matrix products, arithmetic and copies ran while one was open for 1% -> 1% of each run, Pallas kernels for 26% -> 26%
where the time goes in v5:
time: 106 us
  Pallas kernels  35.4 us (33%)
  starting transfers between devices  34 us (32%)
  waiting for transfers between devices  29.1 us (27%)
  local copies, waits for them, and re-layouts  4.75 us (4%)
  other arithmetic  1.34 us (1%)
    ppermute x30, starting transfers between devices, shift(): return lax.ppermute(value, AXES, pairs)  32.8 us
    ppermute x30, waiting for transfers between devices, shift(): return lax.ppermute(value, AXES, pairs)  25.5 us
    pallas_call x7, Pallas kernels, hidden_part(): pl.pallas_call(functools.partial(hidden_kernel, len(pieces), sources, exp...  19.8 us
    pallas_call x8, Pallas kernels, outputs(): pl.pallas_call(functools.partial(outputs_kernel, rows // 2, len(arrived))...  5.13 us
    unnamed x16, local copies, waits for them, and re-layouts  4.75 us
    ppermute x5, waiting for transfers between devices, swap(): return lax.ppermute(value, AXES, [(i, i ^ 1) for i in range(devices)])  3.62 us
    pallas_call x1, Pallas kernels, prune_first(): pl.pallas_call(prune_kernel, out_shape=[jax.ShapeDtypeStruct((size, cut),...  2.57 us
    pallas_call x2, Pallas kernels, masks(): pl.pallas_call(mask_kernel, out_shape=[jax.ShapeDtypeStruct((rows, cut),...  2.42 us
  transfers between devices with their start and end apart: 35, of which 22 were waited for; matrix products, arithmetic and copies ran while one was open for 1% of the time, Pallas kernels for 26%

profile of v5, /device:TPU:0, one launch (start us, length us, event | category | flops | bytes accessed | tf_op | source)
XLA Modules:
  0.0 105.5 jit_solution(8970903738090758666)
XLA Ops:
  0.6 2.1 %split.1 = (bf16[72,2048]{1,0:T(8,128)(2,1)}, bf16[72,2048]{1,0:T(8,128)(2,1)}, bf16[64,2048]{1,0:T(8,128)(2,1)}, bf16[64,2048]{1,0:T(8,128)(2,1)}) custom-call(bf16[128,2048]{1,0:T(8,128)(2,1)} %x_ref.1, s32[8,128]{1,0:T(8,128)} %bitcast.28, f32[8,128]{1,0:T(8,128)} %bitcast.29), custom_call_target="tpu_custom_call" | custom-call | tf_op jit(solution)/shard_map/split/pallas_call | solution.py:145
  2.7 0.5 collective-permute-start
  3.3 3.0 %collective-permute-start.2 = (bf16[72,2048]{1,0:T(8,128)(2,1)}, bf16[72,2048]{1,0:T(8,128)(2,1)S(1)}, u32[]{:S(2)}, u32[]{:S(2)}) collective-permute-start(bf16[72,2048]{1,0:T(8,128)(2,1)} %get-tuple-element.75.refs_0_), channel_id=1, source_target_pairs={{0,4},{1,5},{4,8},{5,9},{8,12},{9,13},{12,14},{13,15},{14,10},{15,... | collective-permute-start | bytes 884744 | tf_op jit(solution)/shard_map/ppermute | solution.py:464
  6.4 2.2 %collective-permute-done.1.refs_1_ = bf16[384,2048]{1,0:T(8,128)(2,1)S(1)} collective-permute-done((bf16[384,2048]{1,0:T(8,128)(2,1)}, bf16[384,2048]{1,0:T(8,128)(2,1)S(1)}, u32[]{:S(2)}, u32[]{:S(2)}) %collective-permute-start.1) | collective-permute-done | bytes 1572896 | tf_op jit(solution)/shard_map/ppermute | solution.py:467
  8.7 2.9 %collective-permute-start.6 = (bf16[64,2048]{1,0:T(8,128)(2,1)}, bf16[64,2048]{1,0:T(8,128)(2,1)}, u32[]{:S(2)}, u32[]{:S(2)}) collective-permute-start(bf16[64,2048]{1,0:T(8,128)(2,1)} %get-tuple-element.87.refs_1_), channel_id=1, source_target_pairs={{0,4},{1,5},{4,8},{5,9},{8,12},{9,13},{12,14},{13,15},{14,10},{15,... | collective-permute-start | bytes 786440 | tf_op jit(solution)/shard_map/ppermute | solution.py:464
  11.6 2.6 %collective-permute-done.2.refs_0_ = bf16[72,2048]{1,0:T(8,128)(2,1)S(1)} collective-permute-done((bf16[72,2048]{1,0:T(8,128)(2,1)}, bf16[72,2048]{1,0:T(8,128)(2,1)S(1)}, u32[]{:S(2)}, u32[]{:S(2)}) %collective-permute-start.2) | collective-permute-done | bytes 294944 | tf_op jit(solution)/shard_map/ppermute | solution.py:464
  14.2 1.9 %collective-permute-start.3 = (bf16[72,2048]{1,0:T(8,128)(2,1)S(1)}, bf16[72,2048]{1,0:T(8,128)(2,1)}, u32[]{:S(2)}, u32[]{:S(2)}) collective-permute-start(bf16[72,2048]{1,0:T(8,128)(2,1)S(1)} %collective-permute-done.2.refs_0_), channel_id=1, source_target_pairs={{0,4},{1,5},{4,8},{5,9},{8,12},{9,13},{12,14},{13,15},{14,10},{15,... | collective-permute-start | bytes 884744 | tf_op jit(solution)/shard_map/ppermute | solution.py:464
  16.4 1.4 %copy-done = bf16[1,384,2048]{2,1,0:T(8,128)(2,1)S(1)} copy-done((bf16[1,384,2048]{2,1,0:T(8,128)(2,1)S(1)}, bf16[1,384,2048]{2,1,0:T(8,128)(2,1)}, u32[]{:S(2)}) %copy-start) | copy-done | bytes 1572888
  17.8 1.4 %copy-done.2 = bf16[1,384,2048]{2,1,0:T(8,128)(2,1)S(1)} copy-done((bf16[1,384,2048]{2,1,0:T(8,128)(2,1)S(1)}, bf16[1,384,2048]{2,1,0:T(8,128)(2,1)}, u32[]{:S(2)}) %copy-start.2) | copy-done | bytes 1572888
  19.2 1.0 copy-done.6
  20.1 0.9 copy-done.7
  21.1 2.0 %hidden.7 = (bf16[128,384]{1,0:T(8,128)(2,1)S(1)}, f32[384,384]{1,0:T(8,128)S(1)}) custom-call(s32[2]{0:T(128)S(1)} %pad_add_fusion.place_ref, bf16[72,2048]{1,0:T(8,128)(2,1)S(1)} %copy-done.6, bf16[64,2048]{1,0:T(8,128)(2,1)S(1)} %copy-done.7, bf16[384,2048]{1,0:T(8,128)(2,1)S(1)} %bitcast.11, bf16[384,2048]{1,0:T(8,128)(2,1)S(1)} %bitcast.17), custom_call_target="tpu_custom_call" | custom-call | flops 402653184 | bytes 3670016 | tf_op jit(solution)/shard_map/hidden/pallas_call | solution.py:245
  23.4 2.0 %collective-permute-start.10 = (bf16[64,2048]{1,0:T(8,128)(2,1)}, bf16[64,2048]{1,0:T(8,128)(2,1)S(1)}, u32[]{:S(2)}, u32[]{:S(2)}) collective-permute-start(bf16[64,2048]{1,0:T(8,128)(2,1)} %collective-permute-done.6.refs_1_), channel_id=1, source_target_pairs={{0,4},{1,5},{4,8},{5,9},{8,12},{9,13},{12,14},{13,15},{14,10},{15,... | collective-permute-start | bytes 786440 | tf_op jit(solution)/shard_map/ppermute | solution.py:464
  25.5 2.0 %hidden.8 = (bf16[128,384]{1,0:T(8,128)(2,1)S(1)}, f32[384,384]{1,0:T(8,128)S(1)}) custom-call(s32[2]{0:T(128)S(1)} %pad_add_fusion.place_ref, bf16[72,2048]{1,0:T(8,128)(2,1)S(1)} %copy-done.6, bf16[64,2048]{1,0:T(8,128)(2,1)S(1)} %copy-done.7, bf16[384,2048]{1,0:T(8,128)(2,1)S(1)} %get-tuple-element.83.refs_2_.refs_6_, ...), custom_call_target="tpu_custom_call" | custom-call | flops 402653184 | bytes 3670016 | tf_op jit(solution)/shard_map/hidden/pallas_call | solution.py:245
  27.9 1.6 %collective-permute-start.8 = (bf16[72,2048]{1,0:T(8,128)(2,1)}, bf16[72,2048]{1,0:T(8,128)(2,1)S(1)}, u32[]{:S(2)}, u32[]{:S(2)}) collective-permute-start(bf16[72,2048]{1,0:T(8,128)(2,1)} %collective-permute-done.3.refs_0_), channel_id=1, source_target_pairs={{0,4},{1,5},{4,8},{5,9},{8,12},{9,13},{12,14},{13,15},{14,10},{15,... | collective-permute-start | bytes 884744 | tf_op jit(solution)/shard_map/ppermute | solution.py:464
  29.5 0.4 collective-permute-start.9
  30.0 4.2 %hidden.9 = (bf16[256,768]{1,0:T(8,128)(2,1)S(1)}, f32[384,384]{1,0:T(8,128)S(1)}, f32[384,384]{1,0:T(8,128)S(1)}) custom-call(s32[2]{0:T(128)S(1)} %pad_add_fusion.place_ref, bf16[72,2048]{1,0:T(8,128)(2,1)S(1)} %collective-permute-done.2.refs_0_, bf16[64,2048]{1,0:T(8,128)(2,1)} %collective-permute-done.6.refs_1_, ...), custom_call_target="tpu_custom_call" | custom-call | flops 1610612736 | bytes 7340032 | tf_op jit(solution)/shard_map/hidden/pallas_call | solution.py:245
  34.1 0.5 collective-permute-done.11.refs_2_
  34.7 1.6 %collective-permute-start.14 = (bf16[64,2048]{1,0:T(8,128)(2,1)S(1)}, bf16[64,2048]{1,0:T(8,128)(2,1)S(1)}, u32[]{:S(2)}, u32[]{:S(2)}) collective-permute-start(bf16[64,2048]{1,0:T(8,128)(2,1)S(1)} %collective-permute-done.10.refs_1_), channel_id=1, source_target_pairs={{0,4},{1,5},{4,8},{5,9},{8,12},{9,13},{12,14},{13,15},{14,10},{15,... | collective-permute-start | bytes 786440 | tf_op jit(solution)/shard_map/ppermute | solution.py:464
  36.3 0.4 collective-permute-start.15
  36.7 4.1 %hidden.10 = (bf16[256,768]{1,0:T(8,128)(2,1)S(1)}, f32[384,384]{1,0:T(8,128)S(1)}, f32[384,384]{1,0:T(8,128)S(1)}) custom-call(s32[2]{0:T(128)S(1)} %pad_add_fusion.place_ref, bf16[72,2048]{1,0:T(8,128)(2,1)} %collective-permute-done.3.refs_0_, bf16[64,2048]{1,0:T(8,128)(2,1)S(1)} %collective-permute-done.10.refs_1_, ...), custom_call_target="tpu_custom_call" | custom-call | flops 1610612736 | bytes 7340032 | tf_op jit(solution)/shard_map/hidden/pallas_call | solution.py:245
  41.0 1.6 %collective-permute-start.12 = (bf16[72,2048]{1,0:T(8,128)(2,1)S(1)}, bf16[72,2048]{1,0:T(8,128)(2,1)S(1)}, u32[]{:S(2)}, u32[]{:S(2)}) collective-permute-start(bf16[72,2048]{1,0:T(8,128)(2,1)S(1)} %collective-permute-done.8.refs_0_), channel_id=1, source_target_pairs={{0,4},{1,5},{4,8},{5,9},{8,12},{9,13},{12,14},{13,15},{14,10},{15,... | collective-permute-start | bytes 884744 | tf_op jit(solution)/shard_map/ppermute | solution.py:464
  42.6 0.5 collective-permute-start.13
  43.0 1.2 %masks.2 = (bf16[384,1024]{1,0:T(8,128)(2,1)S(1)}, bf16[384,1024]{1,0:T(8,128)(2,1)S(1)}) custom-call(s32[96,2048]{1,0:T(8,128)S(1)} %bitcast.26, bf16[384,2048]{1,0:T(8,128)(2,1)S(1)} %bitcast.22), custom_call_target="tpu_custom_call" | custom-call | flops 301989888 | bytes 3145728 | tf_op jit(solution)/shard_map/masks/pallas_call | solution.py:189
  44.2 1.2 %masks.3 = (bf16[384,1024]{1,0:T(8,128)(2,1)S(1)}, bf16[384,1024]{1,0:T(8,128)(2,1)S(1)}) custom-call(s32[96,2048]{1,0:T(8,128)S(1)} %bitcast.27, bf16[384,2048]{1,0:T(8,128)(2,1)S(1)} %bitcast.23), custom_call_target="tpu_custom_call" | custom-call | flops 301989888 | bytes 3145728 | tf_op jit(solution)/shard_map/masks/pallas_call | solution.py:189
  45.5 1.1 %collective-permute-done.15.refs_2_ = bf16[64,2048]{1,0:T(8,128)(2,1)S(1)} collective-permute-done((bf16[64,2048]{1,0:T(8,128)(2,1)S(1)}, bf16[64,2048]{1,0:T(8,128)(2,1)S(1)}, u32[]{:S(2)}, u32[]{:S(2)}) %collective-permute-start.15) | collective-permute-done | bytes 262176 | tf_op jit(solution)/shard_map/ppermute | solution.py:464
  46.6 3.6 %hidden.11 = (bf16[256,768]{1,0:T(8,128)(2,1)S(1)}, f32[384,384]{1,0:T(8,128)S(1)}, f32[384,384]{1,0:T(8,128)S(1)}) custom-call(s32[2]{0:T(128)S(1)} %pad_add_fusion.place_ref, bf16[72,2048]{1,0:T(8,128)(2,1)S(1)} %collective-permute-done.8.refs_0_, bf16[64,2048]{1,0:T(8,128)(2,1)S(1)} %collective-permute-done.14.refs_1_, ...), custom_call_target="tpu_custom_call" | custom-call | flops 1610612736 | bytes 7340032 | tf_op jit(solution)/shard_map/hidden/pallas_call | solution.py:245
  50.2 0.8 collective-permute-done.13.refs_1_
  50.9 2.0 %hidden.13 = (bf16[128,384]{1,0:T(8,128)(2,1)S(1)}, f32[384,384]{1,0:T(8,128)S(1)}) custom-call(s32[2]{0:T(128)S(1)} %pad_add_fusion.place_ref, bf16[72,2048]{1,0:T(8,128)(2,1)S(1)} %collective-permute-done.12.refs_0_, bf16[72,2048]{1,0:T(8,128)(2,1)S(1)} %collective-permute-done.13.refs_1_, bf16[384,2048]{1,0:T(8,128)(2,1)S(1)} %get-tuple-element.83.refs_2_.refs_6_, ...), custom_call_target="tpu_custom_call" | custom-call | flops 402653184 | bytes 3670016 | tf_op jit(solution)/shard_map/hidden/pallas_call | solution.py:245
  53.0 2.0 %hidden.12 = (bf16[128,384]{1,0:T(8,128)(2,1)S(1)}, f32[384,384]{1,0:T(8,128)S(1)}) custom-call(s32[2]{0:T(128)S(1)} %pad_add_fusion.place_ref, bf16[72,2048]{1,0:T(8,128)(2,1)S(1)} %collective-permute-done.12.refs_0_, bf16[72,2048]{1,0:T(8,128)(2,1)S(1)} %collective-permute-done.13.refs_1_, bf16[384,2048]{1,0:T(8,128)(2,1)S(1)} %bitcast.15, ...), custom_call_target="tpu_custom_call" | custom-call | flops 402653184 | bytes 3670016 | tf_op jit(solution)/shard_map/hidden/pallas_call | solution.py:245
  55.1 2.6 %prune.1 = (bf16[384,1024]{1,0:T(8,128)(2,1)S(1)}, bf16[384,384]{1,0:T(8,128)(2,1)S(1)}) custom-call(f32[384,384]{1,0:T(8,128)S(1)} %get-tuple-element.118.own_ref, f32[384,384]{1,0:T(8,128)S(1)} %collective-permute-done.16.other_ref, bf16[384,1024]{1,0:T(8,128)(2,1)S(1)} %get-tuple-element.110.error_ref, bf16[384,2048]{1,0:T(8,128)(2,1)S(1)} %bitcast.24, ...), custom_call_target="tpu_custom_call" | custom-call | flops 981467136 | bytes 4325376 | tf_op jit(solution)/shard_map/prune/pallas_call | solution.py:310
  57.6 0.6 collective-permute-start.26
  58.2 0.6 prune_next.1.own_ref
  58.9 1.2 %collective-permute-done.26.other_ref = bf16[384,1024]{1,0:T(8,128)(2,1)S(1)} collective-permute-done((bf16[384,1024]{1,0:T(8,128)(2,1)S(1)}, bf16[384,1024]{1,0:T(8,128)(2,1)S(1)}, u32[]{:S(2)}, u32[]{:S(2)}) %collective-permute-start.26) | collective-permute-done | bytes 786464 | tf_op jit(solution)/shard_map/ppermute | solution.py:467
  60.1 0.5 outputs.12
  60.9 1.7 %collective-permute-start.28 = (bf16[64,1024]{1,0:T(8,128)(2,1)S(1)}, bf16[64,1024]{1,0:T(8,128)(2,1)S(1)}, u32[]{:S(2)}, u32[]{:S(2)}) collective-permute-start(bf16[64,1024]{1,0:T(8,128)(2,1)S(1)} %get-tuple-element.137), channel_id=1, source_target_pairs={{0,4},{1,5},{4,8},{5,9},{8,12},{9,13},{12,14},{13,15},{14,10},{15,... | collective-permute-start | bytes 393224 | tf_op jit(solution)/shard_map/ppermute | solution.py:464
  63.4 1.7 %collective-permute-start.19 = (bf16[64,1024]{1,0:T(8,128)(2,1)S(1)}, bf16[64,1024]{1,0:T(8,128)(2,1)S(1)}, u32[]{:S(2)}, u32[]{:S(2)}) collective-permute-start(bf16[64,1024]{1,0:T(8,128)(2,1)S(1)} %get-tuple-element.128), channel_id=1, source_target_pairs={{0,4},{1,5},{4,8},{5,9},{8,12},{9,13},{12,14},{13,15},{14,10},{15,... | collective-permute-start | bytes 393224 | tf_op jit(solution)/shard_map/ppermute | solution.py:464
  65.2 1.8 %collective-permute-done.27.refs_0_ = bf16[64,1024]{1,0:T(8,128)(2,1)S(1)} collective-permute-done((bf16[64,1024]{1,0:T(8,128)(2,1)S(1)}, bf16[64,1024]{1,0:T(8,128)(2,1)S(1)}, u32[]{:S(2)}, u32[]{:S(2)}) %collective-permute-start.27) | collective-permute-done | bytes 131104 | tf_op jit(solution)/shard_map/ppermute | solution.py:464
  67.3 0.7 outputs.13
  68.0 1.7 %collective-permute-start.29 = (bf16[128,1024]{1,0:T(8,128)(2,1)S(1)}, bf16[128,1024]{1,0:T(8,128)(2,1)S(1)}, u32[]{:S(2)}, u32[]{:S(2)}) collective-permute-start(bf16[128,1024]{1,0:T(8,128)(2,1)S(1)} %get-tuple-element.138), channel_id=1, source_target_pairs={{0,2},{1,3},{4,0},{5,1},{8,4},{9,5},{12,8},{13,9},{14,12},{15,13},... | collective-permute-start | bytes 786440 | tf_op jit(solution)/shard_map/ppermute | solution.py:464
  70.0 0.7 outputs.9
  70.8 1.7 %collective-permute-start.20 = (bf16[128,1024]{1,0:T(8,128)(2,1)S(1)}, bf16[128,1024]{1,0:T(8,128)(2,1)S(1)}, u32[]{:S(2)}, u32[]{:S(2)}) collective-permute-start(bf16[128,1024]{1,0:T(8,128)(2,1)S(1)} %get-tuple-element.129), channel_id=1, source_target_pairs={{0,2},{1,3},{4,0},{5,1},{8,4},{9,5},{12,8},{13,9},{14,12},{15,13},... | collective-permute-start | bytes 786440 | tf_op jit(solution)/shard_map/ppermute | solution.py:464
  72.8 4.4 %collective-permute-done.29.refs_0_ = bf16[128,1024]{1,0:T(8,128)(2,1)S(1)} collective-permute-done((bf16[128,1024]{1,0:T(8,128)(2,1)S(1)}, bf16[128,1024]{1,0:T(8,128)(2,1)S(1)}, u32[]{:S(2)}, u32[]{:S(2)}) %collective-permute-start.29) | collective-permute-done | bytes 262176 | tf_op jit(solution)/shard_map/ppermute | solution.py:464
  77.3 1.6 %collective-permute-done.30.refs_1_ = bf16[128,1024]{1,0:T(8,128)(2,1)S(1)} collective-permute-done((bf16[128,1024]{1,0:T(8,128)(2,1)S(1)}, bf16[128,1024]{1,0:T(8,128)(2,1)S(1)}, u32[]{:S(2)}, u32[]{:S(2)}) %collective-permute-start.30) | collective-permute-done | bytes 262176 | tf_op jit(solution)/shard_map/ppermute | solution.py:464
  78.8 0.7 outputs.14
  79.5 1.6 %collective-permute-start.31 = (bf16[128,1024]{1,0:T(8,128)(2,1)S(1)}, bf16[128,1024]{1,0:T(8,128)(2,1)S(1)}, u32[]{:S(2)}, u32[]{:S(2)}) collective-permute-start(bf16[128,1024]{1,0:T(8,128)(2,1)S(1)} %get-tuple-element.140), channel_id=1, source_target_pairs={{0,2},{1,3},{4,0},{5,1},{8,4},{9,5},{12,8},{13,9},{14,12},{15,13},... | collective-permute-start | bytes 786440 | tf_op jit(solution)/shard_map/ppermute | solution.py:464
  81.2 0.4 collective-permute-start.32
  81.6 1.3 %collective-permute-done.20.refs_0_ = bf16[128,1024]{1,0:T(8,128)(2,1)S(1)} collective-permute-done((bf16[128,1024]{1,0:T(8,128)(2,1)S(1)}, bf16[128,1024]{1,0:T(8,128)(2,1)S(1)}, u32[]{:S(2)}, u32[]{:S(2)}) %collective-permute-start.20) | collective-permute-done | bytes 262176 | tf_op jit(solution)/shard_map/ppermute | solution.py:464
  82.9 1.6 %collective-permute-done.21.refs_1_ = bf16[128,1024]{1,0:T(8,128)(2,1)S(1)} collective-permute-done((bf16[128,1024]{1,0:T(8,128)(2,1)S(1)}, bf16[128,1024]{1,0:T(8,128)(2,1)S(1)}, u32[]{:S(2)}, u32[]{:S(2)}) %collective-permute-start.21) | collective-permute-done | bytes 262176 | tf_op jit(solution)/shard_map/ppermute | solution.py:464
  84.4 0.7 outputs.10
  85.1 1.6 %collective-permute-start.22 = (bf16[128,1024]{1,0:T(8,128)(2,1)S(1)}, bf16[128,1024]{1,0:T(8,128)(2,1)S(1)}, u32[]{:S(2)}, u32[]{:S(2)}) collective-permute-start(bf16[128,1024]{1,0:T(8,128)(2,1)S(1)} %get-tuple-element.131), channel_id=1, source_target_pairs={{0,2},{1,3},{4,0},{5,1},{8,4},{9,5},{12,8},{13,9},{14,12},{15,13},... | collective-permute-start | bytes 786440 | tf_op jit(solution)/shard_map/ppermute | solution.py:464
  87.2 1.6 %collective-permute-done.31.refs_0_ = bf16[128,1024]{1,0:T(8,128)(2,1)S(1)} collective-permute-done((bf16[128,1024]{1,0:T(8,128)(2,1)S(1)}, bf16[128,1024]{1,0:T(8,128)(2,1)S(1)}, u32[]{:S(2)}, u32[]{:S(2)}) %collective-permute-start.31) | collective-permute-done | bytes 262176 | tf_op jit(solution)/shard_map/ppermute | solution.py:464
  88.8 1.6 %collective-permute-done.32.refs_1_ = bf16[128,1024]{1,0:T(8,128)(2,1)S(1)} collective-permute-done((bf16[128,1024]{1,0:T(8,128)(2,1)S(1)}, bf16[128,1024]{1,0:T(8,128)(2,1)S(1)}, u32[]{:S(2)}, u32[]{:S(2)}) %collective-permute-start.32) | collective-permute-done | bytes 262176 | tf_op jit(solution)/shard_map/ppermute | solution.py:464
  90.4 0.7 outputs.15
  91.1 1.6 %collective-permute-start.33 = (bf16[128,1024]{1,0:T(8,128)(2,1)S(1)}, bf16[128,1024]{1,0:T(8,128)(2,1)S(1)}, u32[]{:S(2)}, u32[]{:S(2)}) collective-permute-start(bf16[128,1024]{1,0:T(8,128)(2,1)S(1)} %get-tuple-element.142), channel_id=1, source_target_pairs={{0,2},{1,3},{4,0},{5,1},{8,4},{9,5},{12,8},{13,9},{14,12},{15,13},... | collective-permute-start | bytes 786440 | tf_op jit(solution)/shard_map/ppermute | solution.py:464
  93.2 1.3 %collective-permute-done.22.refs_0_ = bf16[128,1024]{1,0:T(8,128)(2,1)S(1)} collective-permute-done((bf16[128,1024]{1,0:T(8,128)(2,1)S(1)}, bf16[128,1024]{1,0:T(8,128)(2,1)S(1)}, u32[]{:S(2)}, u32[]{:S(2)}) %collective-permute-start.22) | collective-permute-done | bytes 262176 | tf_op jit(solution)/shard_map/ppermute | solution.py:464
  94.4 1.6 %collective-permute-done.23.refs_1_ = bf16[128,1024]{1,0:T(8,128)(2,1)S(1)} collective-permute-done((bf16[128,1024]{1,0:T(8,128)(2,1)S(1)}, bf16[128,1024]{1,0:T(8,128)(2,1)S(1)}, u32[]{:S(2)}, u32[]{:S(2)}) %collective-permute-start.23) | collective-permute-done | bytes 262176 | tf_op jit(solution)/shard_map/ppermute | solution.py:464
  96.0 0.7 outputs.11
  96.7 1.6 %collective-permute-start.24 = (bf16[128,1024]{1,0:T(8,128)(2,1)S(1)}, bf16[128,1024]{1,0:T(8,128)(2,1)S(1)}, u32[]{:S(2)}, u32[]{:S(2)}) collective-permute-start(bf16[128,1024]{1,0:T(8,128)(2,1)S(1)} %get-tuple-element.133), channel_id=1, source_target_pairs={{0,2},{1,3},{4,0},{5,1},{8,4},{9,5},{12,8},{13,9},{14,12},{15,13},... | collective-permute-start | bytes 786440 | tf_op jit(solution)/shard_map/ppermute | solution.py:464
  98.8 1.3 %maximum_bitcast_fusion = bf16[1,384,2048]{2,1,0:T(8,128)(2,1)} fusion(bf16[384,1024]{1,0:T(8,128)(2,1)S(1)} %prune_next.1.own_ref, bf16[384,1024]{1,0:T(8,128)(2,1)S(1)} %get-tuple-element.135.own_ref), kind=kLoop, calls=%fused_computation | loop fusion | flops 3145728 | bytes 3145728 | tf_op jit(solution)/shard_map/broadcast_in_dim | solution.py:544
  101.3 0.8 finish.2.refs_0_
  102.1 1.1 collective-permute-done.24.right_ref
  103.2 1.6 %collective-permute-done.25.left_ref = bf16[128,1024]{1,0:T(8,128)(2,1)S(1)} collective-permute-done((bf16[128,1024]{1,0:T(8,128)(2,1)S(1)}, bf16[128,1024]{1,0:T(8,128)(2,1)S(1)}, u32[]{:S(2)}, u32[]{:S(2)}) %collective-permute-start.25) | collective-permute-done | bytes 262176 | tf_op jit(solution)/shard_map/ppermute | solution.py:464
  104.7 0.8 finish.3
  (49 shorter events, 6.3 us)
Async XLA Ops:
  2.7 3.7 %collective-permute-start = (bf16[384,2048]{1,0:T(8,128)(2,1)}, bf16[384,2048]{1,0:T(8,128)(2,1)S(1)}, u32[]{:S(2)}, u32[]{:S(2)}) collective-permute-start(bf16[384,2048]{1,0:T(8,128)(2,1)} %bitcast.10), channel_id=1, source_target_pairs={{0,1},{1,0},{2,3},{3,2},{4,5},{5,4},{6,7},{7,6},{8,9},{9,8},{10,11... | collective-permute-start | bytes 4718600 | tf_op jit(solution)/shard_map/ppermute | solution.py:467
  3.2 5.5 %collective-permute-start.1 = (bf16[384,2048]{1,0:T(8,128)(2,1)}, bf16[384,2048]{1,0:T(8,128)(2,1)S(1)}, u32[]{:S(2)}, u32[]{:S(2)}) collective-permute-start(bf16[384,2048]{1,0:T(8,128)(2,1)} %bitcast.16), channel_id=1, source_target_pairs={{0,1},{1,0},{2,3},{3,2},{4,5},{5,4},{6,7},{7,6},{8,9},{9,8},{10,11... | collective-permute-start | bytes 4718600 | tf_op jit(solution)/shard_map/ppermute | solution.py:467
  3.3 11.0 %collective-permute-start.2 = (bf16[72,2048]{1,0:T(8,128)(2,1)}, bf16[72,2048]{1,0:T(8,128)(2,1)S(1)}, u32[]{:S(2)}, u32[]{:S(2)}) collective-permute-start(bf16[72,2048]{1,0:T(8,128)(2,1)} %get-tuple-element.75.refs_0_), channel_id=1, source_target_pairs={{0,4},{1,5},{4,8},{5,9},{8,12},{9,13},{12,14},{13,15},{14,10},{15,... | collective-permute-start | bytes 884744 | tf_op jit(solution)/shard_map/ppermute | solution.py:464
  6.3 9.9 %collective-permute-start.4 = (bf16[72,2048]{1,0:T(8,128)(2,1)}, bf16[72,2048]{1,0:T(8,128)(2,1)}, u32[]{:S(2)}, u32[]{:S(2)}) collective-permute-start(bf16[72,2048]{1,0:T(8,128)(2,1)} %get-tuple-element.86), channel_id=1, source_target_pairs={{0,2},{1,3},{4,0},{5,1},{8,4},{9,5},{12,8},{13,9},{14,12},{15,13},... | collective-permute-start | bytes 884744 | tf_op jit(solution)/shard_map/ppermute | solution.py:464
  8.7 14.7 %collective-permute-start.6 = (bf16[64,2048]{1,0:T(8,128)(2,1)}, bf16[64,2048]{1,0:T(8,128)(2,1)}, u32[]{:S(2)}, u32[]{:S(2)}) collective-permute-start(bf16[64,2048]{1,0:T(8,128)(2,1)} %get-tuple-element.87.refs_1_), channel_id=1, source_target_pairs={{0,4},{1,5},{4,8},{5,9},{8,12},{9,13},{12,14},{13,15},{14,10},{15,... | collective-permute-start | bytes 786440 | tf_op jit(solution)/shard_map/ppermute | solution.py:464
  11.6 11.7 %collective-permute-start.7 = (bf16[64,2048]{1,0:T(8,128)(2,1)}, bf16[64,2048]{1,0:T(8,128)(2,1)}, u32[]{:S(2)}, u32[]{:S(2)}) collective-permute-start(bf16[64,2048]{1,0:T(8,128)(2,1)} %get-tuple-element.88), channel_id=1, source_target_pairs={{0,2},{1,3},{4,0},{5,1},{8,4},{9,5},{12,8},{13,9},{14,12},{15,13},... | collective-permute-start | bytes 786440 | tf_op jit(solution)/shard_map/ppermute | solution.py:464
  14.2 13.3 %collective-permute-start.3 = (bf16[72,2048]{1,0:T(8,128)(2,1)S(1)}, bf16[72,2048]{1,0:T(8,128)(2,1)}, u32[]{:S(2)}, u32[]{:S(2)}) collective-permute-start(bf16[72,2048]{1,0:T(8,128)(2,1)S(1)} %collective-permute-done.2.refs_0_), channel_id=1, source_target_pairs={{0,4},{1,5},{4,8},{5,9},{8,12},{9,13},{12,14},{13,15},{14,10},{15,... | collective-permute-start | bytes 884744 | tf_op jit(solution)/shard_map/ppermute | solution.py:464
  16.2 11.8 %collective-permute-start.5 = (bf16[72,2048]{1,0:T(8,128)(2,1)}, bf16[72,2048]{1,0:T(8,128)(2,1)}, u32[]{:S(2)}, u32[]{:S(2)}) collective-permute-start(bf16[72,2048]{1,0:T(8,128)(2,1)} %collective-permute-done.4.refs_3_), channel_id=1, source_target_pairs={{0,2},{1,3},{4,0},{5,1},{8,4},{9,5},{12,8},{13,9},{14,12},{15,13},... | collective-permute-start | bytes 884744 | tf_op jit(solution)/shard_map/ppermute | solution.py:464
  16.4 1.4 %copy-start = (bf16[1,384,2048]{2,1,0:T(8,128)(2,1)S(1)}, bf16[1,384,2048]{2,1,0:T(8,128)(2,1)}, u32[]{:S(2)}) copy-start(bf16[1,384,2048]{2,1,0:T(8,128)(2,1)} %param.10) | copy-start | bytes 4718596
  17.8 1.4 %copy-start.2 = (bf16[1,384,2048]{2,1,0:T(8,128)(2,1)S(1)}, bf16[1,384,2048]{2,1,0:T(8,128)(2,1)}, u32[]{:S(2)}) copy-start(bf16[1,384,2048]{2,1,0:T(8,128)(2,1)} %param.11) | copy-start | bytes 4718596
  19.2 1.0 copy-start.6
  20.1 0.9 copy-start.7
  23.4 6.6 %copy-start.1 = (bf16[1,384,2048]{2,1,0:T(8,128)(2,1)S(1)}, bf16[1,384,2048]{2,1,0:T(8,128)(2,1)}, u32[]{:S(2)}) copy-start(bf16[1,384,2048]{2,1,0:T(8,128)(2,1)} %param.10) | copy-start | bytes 4718596
  23.4 6.6 %copy-start.3 = (bf16[1,384,2048]{2,1,0:T(8,128)(2,1)S(1)}, bf16[1,384,2048]{2,1,0:T(8,128)(2,1)}, u32[]{:S(2)}) copy-start(bf16[1,384,2048]{2,1,0:T(8,128)(2,1)} %param.11) | copy-start | bytes 4718596
  23.4 10.7 %collective-permute-start.10 = (bf16[64,2048]{1,0:T(8,128)(2,1)}, bf16[64,2048]{1,0:T(8,128)(2,1)S(1)}, u32[]{:S(2)}, u32[]{:S(2)}) collective-permute-start(bf16[64,2048]{1,0:T(8,128)(2,1)} %collective-permute-done.6.refs_1_), channel_id=1, source_target_pairs={{0,4},{1,5},{4,8},{5,9},{8,12},{9,13},{12,14},{13,15},{14,10},{15,... | collective-permute-start | bytes 786440 | tf_op jit(solution)/shard_map/ppermute | solution.py:464
  25.4 9.3 %collective-permute-start.11 = (bf16[64,2048]{1,0:T(8,128)(2,1)}, bf16[64,2048]{1,0:T(8,128)(2,1)S(1)}, u32[]{:S(2)}, u32[]{:S(2)}) collective-permute-start(bf16[64,2048]{1,0:T(8,128)(2,1)} %collective-permute-done.7.refs_2_), channel_id=1, source_target_pairs={{0,2},{1,3},{4,0},{5,1},{8,4},{9,5},{12,8},{13,9},{14,12},{15,13},... | collective-permute-start | bytes 786440 | tf_op jit(solution)/shard_map/ppermute | solution.py:464
  27.9 12.9 %collective-permute-start.8 = (bf16[72,2048]{1,0:T(8,128)(2,1)}, bf16[72,2048]{1,0:T(8,128)(2,1)S(1)}, u32[]{:S(2)}, u32[]{:S(2)}) collective-permute-start(bf16[72,2048]{1,0:T(8,128)(2,1)} %collective-permute-done.3.refs_0_), channel_id=1, source_target_pairs={{0,4},{1,5},{4,8},{5,9},{8,12},{9,13},{12,14},{13,15},{14,10},{15,... | collective-permute-start | bytes 884744 | tf_op jit(solution)/shard_map/ppermute | solution.py:464
  29.5 11.5 %collective-permute-start.9 = (bf16[72,2048]{1,0:T(8,128)(2,1)}, bf16[72,2048]{1,0:T(8,128)(2,1)S(1)}, u32[]{:S(2)}, u32[]{:S(2)}) collective-permute-start(bf16[72,2048]{1,0:T(8,128)(2,1)} %collective-permute-done.5.refs_3_), channel_id=1, source_target_pairs={{0,2},{1,3},{4,0},{5,1},{8,4},{9,5},{12,8},{13,9},{14,12},{15,13},... | collective-permute-start | bytes 884744 | tf_op jit(solution)/shard_map/ppermute | solution.py:464
  34.7 8.3 %copy-start.4 = (bf16[1,384,2048]{2,1,0:T(8,128)(2,1)S(1)}, bf16[1,384,2048]{2,1,0:T(8,128)(2,1)}, u32[]{:S(2)}) copy-start(bf16[1,384,2048]{2,1,0:T(8,128)(2,1)} %param.12) | copy-start | bytes 4718596
  34.7 8.3 %copy-start.5 = (s32[1,96,2048]{2,1,0:T(8,128)S(1)}, s32[1,96,2048]{2,1,0:T(8,128)}, u32[]{:S(2)}) copy-start(s32[1,96,2048]{2,1,0:T(8,128)} %param.13) | copy-start | bytes 2359300
  34.7 10.8 %collective-permute-start.14 = (bf16[64,2048]{1,0:T(8,128)(2,1)S(1)}, bf16[64,2048]{1,0:T(8,128)(2,1)S(1)}, u32[]{:S(2)}, u32[]{:S(2)}) collective-permute-start(bf16[64,2048]{1,0:T(8,128)(2,1)S(1)} %collective-permute-done.10.refs_1_), channel_id=1, source_target_pairs={{0,4},{1,5},{4,8},{5,9},{8,12},{9,13},{12,14},{13,15},{14,10},{15,... | collective-permute-start | bytes 786440 | tf_op jit(solution)/shard_map/ppermute | solution.py:464
  36.3 10.4 %collective-permute-start.15 = (bf16[64,2048]{1,0:T(8,128)(2,1)S(1)}, bf16[64,2048]{1,0:T(8,128)(2,1)S(1)}, u32[]{:S(2)}, u32[]{:S(2)}) collective-permute-start(bf16[64,2048]{1,0:T(8,128)(2,1)S(1)} %collective-permute-done.11.refs_2_), channel_id=1, source_target_pairs={{0,2},{1,3},{4,0},{5,1},{8,4},{9,5},{12,8},{13,9},{14,12},{15,13},... | collective-permute-start | bytes 786440 | tf_op jit(solution)/shard_map/ppermute | solution.py:464
  41.0 9.2 %collective-permute-start.12 = (bf16[72,2048]{1,0:T(8,128)(2,1)S(1)}, bf16[72,2048]{1,0:T(8,128)(2,1)S(1)}, u32[]{:S(2)}, u32[]{:S(2)}) collective-permute-start(bf16[72,2048]{1,0:T(8,128)(2,1)S(1)} %collective-permute-done.8.refs_0_), channel_id=1, source_target_pairs={{0,4},{1,5},{4,8},{5,9},{8,12},{9,13},{12,14},{13,15},{14,10},{15,... | collective-permute-start | bytes 884744 | tf_op jit(solution)/shard_map/ppermute | solution.py:464
  42.6 8.4 %collective-permute-start.13 = (bf16[72,2048]{1,0:T(8,128)(2,1)S(1)}, bf16[72,2048]{1,0:T(8,128)(2,1)S(1)}, u32[]{:S(2)}, u32[]{:S(2)}) collective-permute-start(bf16[72,2048]{1,0:T(8,128)(2,1)S(1)} %collective-permute-done.9.refs_3_), channel_id=1, source_target_pairs={{0,2},{1,3},{4,0},{5,1},{8,4},{9,5},{12,8},{13,9},{14,12},{15,13},... | collective-permute-start | bytes 884744 | tf_op jit(solution)/shard_map/ppermute | solution.py:464
  53.0 2.1 %collective-permute-start.16 = (f32[384,384]{1,0:T(8,128)S(1)}, f32[384,384]{1,0:T(8,128)S(1)}, u32[]{:S(2)}, u32[]{:S(2)}) collective-permute-start(f32[384,384]{1,0:T(8,128)S(1)} %get-tuple-element.120), channel_id=1, source_target_pairs={{0,1},{1,0},{2,3},{3,2},{4,5},{5,4},{6,7},{7,6},{8,9},{9,8},{10,11... | collective-permute-start | bytes 1769480 | tf_op jit(solution)/shard_map/ppermute | solution.py:467
  57.6 2.5 %collective-permute-start.26 = (bf16[384,1024]{1,0:T(8,128)(2,1)S(1)}, bf16[384,1024]{1,0:T(8,128)(2,1)S(1)}, u32[]{:S(2)}, u32[]{:S(2)}) collective-permute-start(bf16[384,1024]{1,0:T(8,128)(2,1)S(1)} %get-tuple-element.135.own_ref), channel_id=1, source_target_pairs={{0,1},{1,0},{2,3},{3,2},{4,5},{5,4},{6,7},{7,6},{8,9},{9,8},{10,11... | collective-permute-start | bytes 2359304 | tf_op jit(solution)/shard_map/ppermute | solution.py:467
  58.8 3.8 %collective-permute-start.17 = (bf16[384,1024]{1,0:T(8,128)(2,1)S(1)}, bf16[384,1024]{1,0:T(8,128)(2,1)S(1)}, u32[]{:S(2)}, u32[]{:S(2)}) collective-permute-start(bf16[384,1024]{1,0:T(8,128)(2,1)S(1)} %prune_next.1.own_ref), channel_id=1, source_target_pairs={{0,1},{1,0},{2,3},{3,2},{4,5},{5,4},{6,7},{7,6},{8,9},{9,8},{10,11... | collective-permute-start | bytes 2359304 | tf_op jit(solution)/shard_map/ppermute | solution.py:467
  60.6 6.4 %collective-permute-start.27 = (bf16[64,1024]{1,0:T(8,128)(2,1)S(1)}, bf16[64,1024]{1,0:T(8,128)(2,1)S(1)}, u32[]{:S(2)}, u32[]{:S(2)}) collective-permute-start(bf16[64,1024]{1,0:T(8,128)(2,1)S(1)} %get-tuple-element.136), channel_id=1, source_target_pairs={{0,2},{1,3},{4,0},{5,1},{8,4},{9,5},{12,8},{13,9},{14,12},{15,13},... | collective-permute-start | bytes 393224 | tf_op jit(solution)/shard_map/ppermute | solution.py:464
  60.9 6.3 %collective-permute-start.28 = (bf16[64,1024]{1,0:T(8,128)(2,1)S(1)}, bf16[64,1024]{1,0:T(8,128)(2,1)S(1)}, u32[]{:S(2)}, u32[]{:S(2)}) collective-permute-start(bf16[64,1024]{1,0:T(8,128)(2,1)S(1)} %get-tuple-element.137), channel_id=1, source_target_pairs={{0,4},{1,5},{4,8},{5,9},{8,12},{9,13},{12,14},{13,15},{14,10},{15,... | collective-permute-start | bytes 393224 | tf_op jit(solution)/shard_map/ppermute | solution.py:464
  63.1 6.9 %collective-permute-start.18 = (bf16[64,1024]{1,0:T(8,128)(2,1)S(1)}, bf16[64,1024]{1,0:T(8,128)(2,1)S(1)}, u32[]{:S(2)}, u32[]{:S(2)}) collective-permute-start(bf16[64,1024]{1,0:T(8,128)(2,1)S(1)} %get-tuple-element.127), channel_id=1, source_target_pairs={{0,2},{1,3},{4,0},{5,1},{8,4},{9,5},{12,8},{13,9},{14,12},{15,13},... | collective-permute-start | bytes 393224 | tf_op jit(solution)/shard_map/ppermute | solution.py:464
  63.4 6.6 %collective-permute-start.19 = (bf16[64,1024]{1,0:T(8,128)(2,1)S(1)}, bf16[64,1024]{1,0:T(8,128)(2,1)S(1)}, u32[]{:S(2)}, u32[]{:S(2)}) collective-permute-start(bf16[64,1024]{1,0:T(8,128)(2,1)S(1)} %get-tuple-element.128), channel_id=1, source_target_pairs={{0,4},{1,5},{4,8},{5,9},{8,12},{9,13},{12,14},{13,15},{14,10},{15,... | collective-permute-start | bytes 393224 | tf_op jit(solution)/shard_map/ppermute | solution.py:464
  68.0 9.3 %collective-permute-start.29 = (bf16[128,1024]{1,0:T(8,128)(2,1)S(1)}, bf16[128,1024]{1,0:T(8,128)(2,1)S(1)}, u32[]{:S(2)}, u32[]{:S(2)}) collective-permute-start(bf16[128,1024]{1,0:T(8,128)(2,1)S(1)} %get-tuple-element.138), channel_id=1, source_target_pairs={{0,2},{1,3},{4,0},{5,1},{8,4},{9,5},{12,8},{13,9},{14,12},{15,13},... | collective-permute-start | bytes 786440 | tf_op jit(solution)/shard_map/ppermute | solution.py:464
  69.6 9.2 %collective-permute-start.30 = (bf16[128,1024]{1,0:T(8,128)(2,1)S(1)}, bf16[128,1024]{1,0:T(8,128)(2,1)S(1)}, u32[]{:S(2)}, u32[]{:S(2)}) collective-permute-start(bf16[128,1024]{1,0:T(8,128)(2,1)S(1)} %get-tuple-element.139), channel_id=1, source_target_pairs={{0,4},{1,5},{4,8},{5,9},{8,12},{9,13},{12,14},{13,15},{14,10},{15,... | collective-permute-start | bytes 786440 | tf_op jit(solution)/shard_map/ppermute | solution.py:464
  70.8 12.1 %collective-permute-start.20 = (bf16[128,1024]{1,0:T(8,128)(2,1)S(1)}, bf16[128,1024]{1,0:T(8,128)(2,1)S(1)}, u32[]{:S(2)}, u32[]{:S(2)}) collective-permute-start(bf16[128,1024]{1,0:T(8,128)(2,1)S(1)} %get-tuple-element.129), channel_id=1, source_target_pairs={{0,2},{1,3},{4,0},{5,1},{8,4},{9,5},{12,8},{13,9},{14,12},{15,13},... | collective-permute-start | bytes 786440 | tf_op jit(solution)/shard_map/ppermute | solution.py:464
  72.4 12.0 %collective-permute-start.21 = (bf16[128,1024]{1,0:T(8,128)(2,1)S(1)}, bf16[128,1024]{1,0:T(8,128)(2,1)S(1)}, u32[]{:S(2)}, u32[]{:S(2)}) collective-permute-start(bf16[128,1024]{1,0:T(8,128)(2,1)S(1)} %get-tuple-element.130), channel_id=1, source_target_pairs={{0,4},{1,5},{4,8},{5,9},{8,12},{9,13},{12,14},{13,15},{14,10},{15,... | collective-permute-start | bytes 786440 | tf_op jit(solution)/shard_map/ppermute | solution.py:464
  79.5 9.3 %collective-permute-start.31 = (bf16[128,1024]{1,0:T(8,128)(2,1)S(1)}, bf16[128,1024]{1,0:T(8,128)(2,1)S(1)}, u32[]{:S(2)}, u32[]{:S(2)}) collective-permute-start(bf16[128,1024]{1,0:T(8,128)(2,1)S(1)} %get-tuple-element.140), channel_id=1, source_target_pairs={{0,2},{1,3},{4,0},{5,1},{8,4},{9,5},{12,8},{13,9},{14,12},{15,13},... | collective-permute-start | bytes 786440 | tf_op jit(solution)/shard_map/ppermute | solution.py:464
  81.2 9.2 %collective-permute-start.32 = (bf16[128,1024]{1,0:T(8,128)(2,1)S(1)}, bf16[128,1024]{1,0:T(8,128)(2,1)S(1)}, u32[]{:S(2)}, u32[]{:S(2)}) collective-permute-start(bf16[128,1024]{1,0:T(8,128)(2,1)S(1)} %get-tuple-element.141), channel_id=1, source_target_pairs={{0,4},{1,5},{4,8},{5,9},{8,12},{9,13},{12,14},{13,15},{14,10},{15,... | collective-permute-start | bytes 786440 | tf_op jit(solution)/shard_map/ppermute | solution.py:464
  85.1 9.3 %collective-permute-start.22 = (bf16[128,1024]{1,0:T(8,128)(2,1)S(1)}, bf16[128,1024]{1,0:T(8,128)(2,1)S(1)}, u32[]{:S(2)}, u32[]{:S(2)}) collective-permute-start(bf16[128,1024]{1,0:T(8,128)(2,1)S(1)} %get-tuple-element.131), channel_id=1, source_target_pairs={{0,2},{1,3},{4,0},{5,1},{8,4},{9,5},{12,8},{13,9},{14,12},{15,13},... | collective-permute-start | bytes 786440 | tf_op jit(solution)/shard_map/ppermute | solution.py:464
  86.8 9.2 %collective-permute-start.23 = (bf16[128,1024]{1,0:T(8,128)(2,1)S(1)}, bf16[128,1024]{1,0:T(8,128)(2,1)S(1)}, u32[]{:S(2)}, u32[]{:S(2)}) collective-permute-start(bf16[128,1024]{1,0:T(8,128)(2,1)S(1)} %get-tuple-element.132), channel_id=1, source_target_pairs={{0,4},{1,5},{4,8},{5,9},{8,12},{9,13},{12,14},{13,15},{14,10},{15,... | collective-permute-start | bytes 786440 | tf_op jit(solution)/shard_map/ppermute | solution.py:464
  91.1 9.9 %collective-permute-start.33 = (bf16[128,1024]{1,0:T(8,128)(2,1)S(1)}, bf16[128,1024]{1,0:T(8,128)(2,1)S(1)}, u32[]{:S(2)}, u32[]{:S(2)}) collective-permute-start(bf16[128,1024]{1,0:T(8,128)(2,1)S(1)} %get-tuple-element.142), channel_id=1, source_target_pairs={{0,2},{1,3},{4,0},{5,1},{8,4},{9,5},{12,8},{13,9},{14,12},{15,13},... | collective-permute-start | bytes 786440 | tf_op jit(solution)/shard_map/ppermute | solution.py:464
  92.7 8.6 %collective-permute-start.34 = (bf16[128,1024]{1,0:T(8,128)(2,1)S(1)}, bf16[128,1024]{1,0:T(8,128)(2,1)S(1)}, u32[]{:S(2)}, u32[]{:S(2)}) collective-permute-start(bf16[128,1024]{1,0:T(8,128)(2,1)S(1)} %get-tuple-element.143), channel_id=1, source_target_pairs={{0,4},{1,5},{4,8},{5,9},{8,12},{9,13},{12,14},{13,15},{14,10},{15,... | collective-permute-start | bytes 786440 | tf_op jit(solution)/shard_map/ppermute | solution.py:464
  96.7 6.4 %collective-permute-start.24 = (bf16[128,1024]{1,0:T(8,128)(2,1)S(1)}, bf16[128,1024]{1,0:T(8,128)(2,1)S(1)}, u32[]{:S(2)}, u32[]{:S(2)}) collective-permute-start(bf16[128,1024]{1,0:T(8,128)(2,1)S(1)} %get-tuple-element.133), channel_id=1, source_target_pairs={{0,2},{1,3},{4,0},{5,1},{8,4},{9,5},{12,8},{13,9},{14,12},{15,13},... | collective-permute-start | bytes 786440 | tf_op jit(solution)/shard_map/ppermute | solution.py:464
  98.4 6.4 %collective-permute-start.25 = (bf16[128,1024]{1,0:T(8,128)(2,1)S(1)}, bf16[128,1024]{1,0:T(8,128)(2,1)S(1)}, u32[]{:S(2)}, u32[]{:S(2)}) collective-permute-start(bf16[128,1024]{1,0:T(8,128)(2,1)S(1)} %get-tuple-element.134), channel_id=1, source_target_pairs={{0,4},{1,5},{4,8},{5,9},{8,12},{9,13},{12,14},{13,15},{14,10},{15,... | collective-permute-start | bytes 786440 | tf_op jit(solution)/shard_map/ppermute | solution.py:464
